TPU v7x, 256 devices: a whole 4x4x8 slice. The times are simulated.
256 devices in a mesh: chain: 32 (over y, z_hi, x), head: 8 (over z_lo, core).
Axes of the slice: x: 4, y: 4, z: 8 (z_hi: 2, z_lo: 4; z = z_hi * 4 + z_lo), core: 2. Of those that a mesh axis runs over, the one named last changes fastest.
Arguments:
- latent: bfloat16 [8192, 5120], P(('chain', 'head')), may hold values from -3 to 3
- query_in: bfloat16 [8192, 5120], P(('chain', 'head')), may hold values from -64 to 64
- key_in: bfloat16 [8192, 5120], P(('chain', 'head')), may hold values from -64 to 64
- value_in: bfloat16 [8192, 5120], P(('chain', 'head')), may hold values from -6 to 6
- cache_keys: bfloat16 [1024, 5120], P('chain', 'head'), may hold values from -6 to 6
- cache_values: bfloat16 [1024, 5120], P('chain', 'head'), may hold values from -6 to 6
- levels: int32 [4], replicated, may hold values from 0 to 49
- timesteps: int32 [50], replicated, may hold values from 1 to 999
- cache_mask: int32 [4, 32], replicated, may hold values 0 or 1
- time_weight: bfloat16 [256, 5120], replicated, may hold values from -8 to 8
Outputs:
- advanced: bfloat16 [8192, 5120], P(('chain', 'head'))
All inputs are finite; a program needn't handle non-finite values.
Results may differ from a plain program's by a relative error of at most 0.012.
Values may be sent and summed in bfloat16 or wider, within the bound.
A program may use at most 128 MiB of HBM per device.

v0:
```python
import math

import jax
import jax.numpy as jnp
from jax import lax
from jax.sharding import PartitionSpec as P

HEAD_DIM = 128
SPANS = 4


def from_partner(block, axis, bit):
    count = lax.axis_size(axis)
    route = []
    for low in range(count):
        high = low | 1 << bit
        if high != low and high < count:
            route += [(low, high), (high, low)]
    return lax.ppermute(block, axis, route)


def shifted(x, axis, by):
    devices = lax.axis_size(axis)
    return lax.ppermute(x, axis, [(i, (i + by) % devices) for i in range(devices)])


def timestep_gate(level_index, timesteps, time_weight):
    half = time_weight.shape[0] // 2
    freqs = jnp.exp(-math.log(10000.0) * jnp.arange(half, dtype=jnp.float32) / half)
    chosen = jnp.arange(timesteps.shape[0], dtype=jnp.int32) == level_index
    stamp = jnp.sum(jnp.where(chosen, timesteps, 0)).astype(jnp.float32)
    phase = stamp * freqs
    embed = jnp.concatenate([jnp.cos(phase), jnp.sin(phase)])[None, :].astype(jnp.bfloat16)
    return jnp.dot(embed, time_weight, preferred_element_type=jnp.float32)[0]


def update_state(state, query, key_rows, value_rows, visible):
    peak, total, summed = state
    count = key_rows.shape[0]
    heads_here = query.shape[1]
    key_heads = key_rows.reshape(count, heads_here, HEAD_DIM)
    value_heads = value_rows.reshape(count, heads_here, HEAD_DIM)
    scores = jnp.einsum("qhd,khd->hqk", query, key_heads, preferred_element_type=jnp.float32)
    scores = scores * (1.0 / math.sqrt(HEAD_DIM))
    scores = jnp.where(visible[None, None, :], scores, -1e30)
    new_peak = jnp.maximum(peak, jnp.max(scores, axis=2))
    weights = jnp.where(visible[None, None, :], jnp.exp(scores - new_peak[:, :, None]), 0.0)
    factor = jnp.exp(peak - new_peak)
    total = factor * total + jnp.sum(weights, axis=2)
    added = jnp.einsum(
        "hqk,khd->qhd",
        weights.astype(jnp.bfloat16),
        value_heads,
        preferred_element_type=jnp.float32,
    )
    summed = factor.T[:, :, None] * summed + added
    return (new_peak, total, summed)


def attend(state, query, key_rows, value_rows, visible):
    state = lax.cond(
        jnp.any(visible),
        lambda current: update_state(current, query, key_rows, value_rows, visible),
        lambda current: current,
        state,
    )
    return state


def shards(
    latent,
    query_in,
    key_in,
    value_in,
    cache_keys,
    cache_values,
    levels,
    timesteps,
    cache_mask,
    time_weight,
):
    chain_count = lax.axis_size("chain")
    section = chain_count // SPANS
    position = lax.axis_index("chain")
    mine = position // section
    query, keys, values = (
        lax.all_to_all(query_in, "head", split_axis=1, concat_axis=0, tiled=True),
        lax.all_to_all(key_in, "head", split_axis=1, concat_axis=0, tiled=True),
        lax.all_to_all(value_in, "head", split_axis=1, concat_axis=0, tiled=True),
    )
    local_rows = query.shape[0]
    width = query.shape[1]
    heads_here = width // HEAD_DIM
    query = query.reshape(local_rows, heads_here, HEAD_DIM)
    state = (
        jnp.full((heads_here, local_rows), -1e30, jnp.float32),
        jnp.zeros((heads_here, local_rows), jnp.float32),
        jnp.zeros((local_rows, heads_here, HEAD_DIM), jnp.float32),
    )
    state = attend(state, query, keys, values, jnp.ones((local_rows,), dtype=bool))
    held = jnp.stack((keys, values))
    steps_count = section.bit_length() - 1
    for bit in range(steps_count):
        partner = from_partner(held, "chain", bit)
        state = attend(
            state, query, partner[0], partner[1], jnp.ones((partner.shape[1],), dtype=bool)
        )
        if bit + 1 < steps_count:
            held = jnp.concatenate([held, partner], axis=1)
    span_ids = jnp.arange(SPANS, dtype=jnp.int32)
    mask_row = jnp.sum(jnp.where(span_ids[:, None] == mine, cache_mask, 0), axis=0)
    cache_rows = cache_keys.shape[0]
    owners = jnp.arange(chain_count, dtype=jnp.int32)
    piece_keys = lax.all_gather(cache_keys, "chain", axis=0, tiled=True)
    piece_values = lax.all_gather(cache_values, "chain", axis=0, tiled=True)
    block_index = jnp.arange(piece_keys.shape[0], dtype=jnp.int32) // cache_rows
    visible = jnp.any((block_index[:, None] == owners[None, :]) & (mask_row[None, :] == 1), axis=1)
    state = attend(state, query, piece_keys, piece_values, visible)
    peak, total, summed = state
    attended = (summed / total.T[:, :, None]).reshape(local_rows, width).astype(jnp.bfloat16)
    returned = lax.all_to_all(attended, "head", split_axis=0, concat_axis=1, tiled=True)
    level_index = jnp.sum(jnp.where(span_ids == mine, levels, 0))
    gate = timestep_gate(level_index, timesteps, time_weight)
    updated = (latent.astype(jnp.float32) + gate[None, :] * returned.astype(jnp.float32)).astype(
        jnp.bfloat16
    )
    return shifted(updated, "chain", -section)


def solution(mesh):
    return jax.shard_map(
        shards,
        mesh=mesh,
        in_specs=(
            P(("chain", "head"), None),
            P(("chain", "head"), None),
            P(("chain", "head"), None),
            P(("chain", "head"), None),
            P("chain", "head"),
            P("chain", "head"),
            P(),
            P(),
            P(),
            P(),
        ),
        out_specs=P(("chain", "head"), None),
        check_vma=False,
    )
```

profile of v0, /device:TPU:1, one launch (start us, length us, event | category | flops | bytes accessed | tf_op | source)
XLA Modules:
  0.0 338.6 jit_solution(6251163875623207673)
XLA Ops:
  6.5 1.9 copy.162
  8.4 7.4 %all-to-all-start.2 = ((bf16[32,8,640]{2,0,1:T(8,128)(2,1)}), bf16[32,8,640]{2,0,1:T(8,128)(2,1)S(1)}, u32[]{:S(2)}, u32[]{:S(2)}) async-start(bf16[32,8,640]{2,0,1:T(8,128)(2,1)} %bitcast.126), calls=%async_computation.2 | async-start | bytes 655360 | tf_op jit(solution)/shard_map/all_to_all | solution.py:89
  17.5 8.3 %all-to-all-done.2 = bf16[32,8,640]{2,0,1:T(8,128)(2,1)S(1)} async-done(((bf16[32,8,640]{2,0,1:T(8,128)(2,1)}), bf16[32,8,640]{2,0,1:T(8,128)(2,1)S(1)}, u32[]{:S(2)}, u32[]{:S(2)}) %all-to-all-start.2) | async-done | bytes 327712 | tf_op jit(solution)/shard_map/all_to_all | solution.py:89
  25.8 14.9 %all_to_all.58 = bf16[32,8,640]{2,0,1:T(8,128)(2,1)S(1)} all-to-all(bf16[32,8,640]{2,0,1:T(8,128)(2,1)} %bitcast.147), channel_id=1, replica_groups=mesh['chain'=32,'head'=8] {'head'}, dimensions={1} | all-to-all | bytes 655360 | tf_op jit(solution)/shard_map/all_to_all | solution.py:88
  42.9 14.6 %collective-permute-done = bf16[2,256,640]{2,1,0:T(8,128)(2,1)} collective-permute-done((bf16[2,256,640]{2,1,0:T(8,128)(2,1)}, bf16[2,256,640]{2,1,0:T(8,128)(2,1)}, u32[]{:S(2)}, u32[]{:S(2)}) %collective-permute-start) | collective-permute-done | bytes 655392 | tf_op jit(solution)/shard_map/ppermute | solution.py:19
  58.7 2.8 collective-permute-start.1
  61.6 28.0 %collective-permute-done.1 = bf16[2,512,640]{2,1,0:T(8,128)(2,1)S(1)} collective-permute-done((bf16[2,512,640]{2,1,0:T(8,128)(2,1)S(1)}, bf16[2,512,640]{2,1,0:T(8,128)(2,1)S(1)}, u32[]{:S(2)}, u32[]{:S(2)}) %collective-permute-start.1) | collective-permute-done | bytes 1310752 | tf_op jit(solution)/shard_map/ppermute | solution.py:19
  89.6 3.3 pad_maximum_fusion
  92.8 4.7 %collective-permute-start.2 = (bf16[2,1024,640]{2,1,0:T(8,128)(2,1)}, bf16[2,1024,640]{2,1,0:T(8,128)(2,1)}, u32[]{:S(2)}, u32[]{:S(2)}) collective-permute-start(bf16[2,1024,640]{2,1,0:T(8,128)(2,1)} %pad_maximum_fusion), channel_id=1, source_target_pairs={{0,32},{32,0},{8,40},{40,8},{16,48},{48,16},{24,56},{56,24},{64,96... | collective-permute-start | bytes 7864328 | tf_op jit(solution)/shard_map/ppermute | solution.py:19
  98.3 6.3 %all-to-all-start = ((bf16[32,8,640]{2,0,1:T(8,128)(2,1)}), bf16[32,8,640]{2,0,1:T(8,128)(2,1)S(1)}, u32[]{:S(2)}, u32[]{:S(2)}) async-start(bf16[32,8,640]{2,0,1:T(8,128)(2,1)} %bitcast.146), calls=%async_computation | async-start | bytes 655360 | tf_op jit(solution)/shard_map/all_to_all | solution.py:87
  108.3 133.7 %all-to-all-done = bf16[32,8,640]{2,0,1:T(8,128)(2,1)S(1)} async-done(((bf16[32,8,640]{2,0,1:T(8,128)(2,1)}), bf16[32,8,640]{2,0,1:T(8,128)(2,1)S(1)}, u32[]{:S(2)}, u32[]{:S(2)}) %all-to-all-start) | async-done | bytes 327712 | tf_op jit(solution)/shard_map/all_to_all | solution.py:87
  244.1 2.1 reshape.102
  247.4 2.5 fusion.81
  253.8 2.5 fusion.80
  257.5 2.2 copy.96
  259.7 2.2 copy.106
  261.9 3.1 bitcast_reduce_fusion.1
  265.0 3.4 %fusion.77 = (bf16[1,1024,640]{2,1,0:T(8,128)(2,1)}, bf16[1,1024,640]{2,1,0:T(8,128)(2,1)}) fusion(bf16[2,1024,640]{2,1,0:T(8,128)(2,1)} %collective-permute-done.2), kind=kLoop, calls=%fused_computation.108 | loop fusion | bytes 5242880 | tf_op jit(solution)/shard_map/slice | solution.py:106
  268.4 2.5 copy.99
  270.9 4.5 %bitcast_reduce_fusion = (f32[5,256]{1,0:T(8,128)S(1)}, f32[5,1024,256]{2,1,0:T(8,128)}) fusion(bf16[1024,5,128]{0,2,1:T(8,128)(2,1)} %bitcast.138, bf16[256,5,128]{2,1,0:T(8,128)(2,1)S(1)} %reshape.101), kind=kOutput, calls=%fused_computation.18 | convolution fusion | flops 338164480 | bytes 6886400 | tf_op jit(solution)/shard_map/cond/branch_1_fun/qhd,khd->hqk/dot_general | solution.py:43
  275.4 2.5 copy.109
  277.9 1.9 fusion.49
  281.4 2.2 fusion.27
  289.5 15.6 %conditional.1 = ((f32[5,256]{1,0:T(8,128)S(1)}, f32[256,5,128]{2,0,1:T(8,128)})) conditional(s32[]{:T(128)} %convert_element_type.49, (f32[5,256]{1,0:T(8,128)S(1)}, f32[256,5,128]{2,0,1:T(8,128)}) %tuple.12, (pred[1024,32]{1,0:T(8,128)(4,1)}, bf16[1024,640]{1,0:T(8,128)(2,1)}, bf16[256,5,128]{2,1,0:T(8,128)(2,1)S(1)}, f32[5,256]{1,0:T(8,128)S(1)}, ...), branch_computations={%region_12.13_spmd, %region_13.17_spmd} | conditional | flops 688491264 | bytes 51554412 | solution.py:61
  290.7 2.5 copy.112
  293.2 2.4 fusion
  297.9 2.6 copy.114
  300.5 3.8 %fusion.9 = f32[256,5,128]{2,0,1:T(8,128)S(1)} fusion(bf16[1024,5,128]{0,2,1:T(8,128)(2,1)} %bitcast.144, f32[5,256,1024]{2,1,0:T(8,128)} %copy-done.3, f32[5,256]{1,0:T(8,128)S(1)} %get-tuple-element.58, pred[1024]{0:T(1024)(128)(4,1)S(1)} %reduce_or.17, f32[256,5,128]{2,0,1:T(8,128)S(1)} %copy-done.11, f32[256,5]{0,1:T(8,128)S(1)} %get-tuple-element.57), kind=kOutput, calls=%fused_computation.8 | convolution fusion | flops 342425600 | bytes 7875584 | tf_op jit(solution)/shard_map/cond/branch_1_fun/hqk,khd->qhd/dot_general | solution.py:50
  307.9 4.3 %all-to-all-start.3 = ((bf16[8,32,640]{2,1,0:T(8,128)(2,1)}), bf16[8,32,640]{2,1,0:T(8,128)(2,1)S(1)}, u32[]{:S(2)}, u32[]{:S(2)}) async-start(bf16[8,32,640]{2,1,0:T(8,128)(2,1)} %convert_element_type.55), calls=%async_computation.3 | async-start | bytes 655360 | tf_op jit(solution)/shard_map/all_to_all | solution.py:121
  314.6 7.6 %all-to-all-done.3 = bf16[8,32,640]{2,1,0:T(8,128)(2,1)S(1)} async-done(((bf16[8,32,640]{2,1,0:T(8,128)(2,1)}), bf16[8,32,640]{2,1,0:T(8,128)(2,1)S(1)}, u32[]{:S(2)}, u32[]{:S(2)}) %all-to-all-start.3) | async-done | bytes 327712 | tf_op jit(solution)/shard_map/all_to_all | solution.py:121
  322.4 2.7 collective-permute-start.3
  325.1 5.9 %collective-permute-done.3 = bf16[32,5120]{1,0:T(8,128)(2,1)S(1)} collective-permute-done((bf16[32,5120]{1,0:T(8,128)(2,1)S(1)}, bf16[32,5120]{1,0:T(8,128)(2,1)S(1)}, u32[]{:S(2)}, u32[]{:S(2)}) %collective-permute-start.3) | collective-permute-done | bytes 327712 | tf_op jit(solution)/shard_map/ppermute | solution.py:24
  (89 shorter events, 34.4 us)
Async XLA Ops:
  6.5 307.6 %copy-start = (bf16[256,5120]{1,0:T(8,128)(2,1)S(1)}, bf16[256,5120]{1,0:T(8,128)(2,1)}, u32[]{:S(2)}) copy-start(bf16[256,5120]{1,0:T(8,128)(2,1)} %param.21) | copy-start | bytes 7864324
  8.4 17.4 %all-to-all-start.2 = ((bf16[32,8,640]{2,0,1:T(8,128)(2,1)}), bf16[32,8,640]{2,0,1:T(8,128)(2,1)S(1)}, u32[]{:S(2)}, u32[]{:S(2)}) async-start(bf16[32,8,640]{2,0,1:T(8,128)(2,1)} %bitcast.126), calls=%async_computation.2 | async-start | bytes 655360 | tf_op jit(solution)/shard_map/all_to_all | solution.py:89
  15.8 273.7 %all-gather.3.cloned.1.call-start = ((), (), s32[]{:S(2)}) async-start(), calls=%async_computation.4 | async-start | bytes 1351680 | tf_op jit(solution)/shard_map/all_gather | solution.py:114
  40.7 52.1 %copy-start.6 = (bf16[32,8,640]{2,0,1:T(8,128)(2,1)}, bf16[32,8,640]{2,0,1:T(8,128)(2,1)S(1)}, u32[]{:S(2)}) copy-start(bf16[32,8,640]{2,0,1:T(8,128)(2,1)S(1)} %all_to_all.58) | copy-start | bytes 983044
  41.7 15.8 %collective-permute-start = (bf16[2,256,640]{2,1,0:T(8,128)(2,1)}, bf16[2,256,640]{2,1,0:T(8,128)(2,1)}, u32[]{:S(2)}, u32[]{:S(2)}) collective-permute-start(bf16[2,256,640]{2,1,0:T(8,128)(2,1)} %pad_maximum_fusion.2), channel_id=1, source_target_pairs={{0,8},{8,0},{16,24},{24,16},{32,40},{40,32},{48,56},{56,48},{64,72... | collective-permute-start | bytes 1966088 | tf_op jit(solution)/shard_map/ppermute | solution.py:19
  58.7 38.9 %copy-start.15 = (bf16[32,5120]{1,0:T(8,128)(2,1)S(1)}, bf16[32,5120]{1,0:T(8,128)(2,1)}, u32[]{:S(2)}) copy-start(bf16[32,5120]{1,0:T(8,128)(2,1)} %param.13) | copy-start | bytes 983044
  58.7 46.7 %copy-start.17 = (s32[4,32]{1,0:T(4,128)S(1)}, s32[4,32]{1,0:T(4,128)}, u32[]{:S(2)}) copy-start(s32[4,32]{1,0:T(4,128)} %param.20) | copy-start | bytes 1540
  58.7 48.9 %copy-start.18 = (s32[4]{0:T(128)S(1)}, s32[4]{0:T(128)}, u32[]{:S(2)}) copy-start(s32[4]{0:T(128)} %param.18) | copy-start | bytes 52
  58.7 30.8 %collective-permute-start.1 = (bf16[2,512,640]{2,1,0:T(8,128)(2,1)S(1)}, bf16[2,512,640]{2,1,0:T(8,128)(2,1)S(1)}, u32[]{:S(2)}, u32[]{:S(2)}) collective-permute-start(bf16[2,512,640]{2,1,0:T(8,128)(2,1)S(1)} %pad_maximum_fusion.1), channel_id=1, source_target_pairs={{0,16},{16,0},{8,24},{24,8},{32,48},{48,32},{40,56},{56,40},{64,80... | collective-permute-start | bytes 3932168 | tf_op jit(solution)/shard_map/ppermute | solution.py:19
  89.6 3.3 copy-start.7
  92.8 172.2 %collective-permute-start.2 = (bf16[2,1024,640]{2,1,0:T(8,128)(2,1)}, bf16[2,1024,640]{2,1,0:T(8,128)(2,1)}, u32[]{:S(2)}, u32[]{:S(2)}) collective-permute-start(bf16[2,1024,640]{2,1,0:T(8,128)(2,1)} %pad_maximum_fusion), channel_id=1, source_target_pairs={{0,32},{32,0},{8,40},{40,8},{16,48},{48,16},{24,56},{56,24},{64,96... | collective-permute-start | bytes 7864328 | tf_op jit(solution)/shard_map/ppermute | solution.py:19
  98.3 143.7 %all-to-all-start = ((bf16[32,8,640]{2,0,1:T(8,128)(2,1)}), bf16[32,8,640]{2,0,1:T(8,128)(2,1)S(1)}, u32[]{:S(2)}, u32[]{:S(2)}) async-start(bf16[32,8,640]{2,0,1:T(8,128)(2,1)} %bitcast.146), calls=%async_computation | async-start | bytes 655360 | tf_op jit(solution)/shard_map/all_to_all | solution.py:87
  104.6 184.9 %all-gather.5.cloned.1.call-start = ((), (), s32[]{:S(2)}) async-start(), calls=%async_computation.5 | async-start | bytes 1351680 | tf_op jit(solution)/shard_map/all_gather | solution.py:115
  242.0 0.7 copy-start.14
  253.8 2.5 copy-start.8
  277.9 5.7 %copy-start.1 = (f32[5,1024,256]{2,1,0:T(8,128)S(1)}, f32[5,1024,256]{2,1,0:T(8,128)}, u32[]{:S(2)}) copy-start(f32[5,1024,256]{2,1,0:T(8,128)} %get-tuple-element.78) | copy-start | bytes 15728644
  283.6 1.3 copy-start.5
  283.6 1.4 copy-start.13
  283.6 2.3 copy-start.2
  283.6 2.4 copy-start.10
  285.0 1.7 copy-start.9
  286.8 1.3 copy-start.4
  295.5 2.3 copy-start.3
  297.8 2.6 copy-start.11
  304.3 0.9 copy-start.12
  305.2 7.0 %copy-start.19 = (s32[50]{0:T(128)S(1)}, s32[50]{0:T(128)}, u32[]{:S(2)}) copy-start(s32[50]{0:T(128)} %param.19) | copy-start | bytes 604
  307.9 14.3 %all-to-all-start.3 = ((bf16[8,32,640]{2,1,0:T(8,128)(2,1)}), bf16[8,32,640]{2,1,0:T(8,128)(2,1)S(1)}, u32[]{:S(2)}, u32[]{:S(2)}) async-start(bf16[8,32,640]{2,1,0:T(8,128)(2,1)} %convert_element_type.55), calls=%async_computation.3 | async-start | bytes 655360 | tf_op jit(solution)/shard_map/all_to_all | solution.py:121
  312.2 10.1 %copy-start.16 = (bf16[32,5120]{1,0:T(8,128)(2,1)S(1)}, bf16[32,5120]{1,0:T(8,128)(2,1)}, u32[]{:S(2)}) copy-start(bf16[32,5120]{1,0:T(8,128)(2,1)} %param.12) | copy-start | bytes 983044
  322.4 8.6 %collective-permute-start.3 = (bf16[32,5120]{1,0:T(8,128)(2,1)S(1)}, bf16[32,5120]{1,0:T(8,128)(2,1)S(1)}, u32[]{:S(2)}, u32[]{:S(2)}) collective-permute-start(bf16[32,5120]{1,0:T(8,128)(2,1)S(1)} %add_convert_fusion), channel_id=1, source_target_pairs={{0,192},{8,200},{16,208},{24,216},{32,224},{40,232},{48,240},{56,2... | collective-permute-start | bytes 983048 | tf_op jit(solution)/shard_map/ppermute | solution.py:24
Sparse Core Ops, SparseCore 0:
  43.0 93.8 all-gather.2
  140.3 97.5 all-gather.4
where the time goes:
time: 341 us; the launch traced here: 339 us
  waiting for transfers between devices  199 us (58%)
  local copies, waits for them, and re-layouts  37.4 us (11%)
  starting transfers between devices  29.5 us (9%)
  matrix products  23.4 us (7%)
  other arithmetic  19.6 us (6%)
  blocking collectives  14.9 us (4%)
  between operations  14.9 us (4%)
    all_to_all x1, waiting for transfers between devices, shards(): lax.all_to_all(query_in, 'head', split_axis=1, concat_axis=0, tiled=True)  134 us
    ppermute x3, waiting for transfers between devices, from_partner(): return lax.ppermute(block, axis, route)  42.6 us
    dot_general x5, matrix products, update_state(): jnp.einsum('qhd,khd->hqk', query, key_heads, preferred_element_type=jnp.f...  15 us
    all_to_all x1, blocking collectives, shards(): lax.all_to_all(key_in, 'head', split_axis=1, concat_axis=0, tiled=True)  14.9 us
    slice x6, local copies, waits for them, and re-layouts, shards(): partner[1]  12.3 us
    ppermute x3, starting transfers between devices, from_partner(): return lax.ppermute(block, axis, route)  8.75 us
    all_to_all x1, waiting for transfers between devices, shards(): lax.all_to_all(value_in, 'head', split_axis=1, concat_axis=0, tiled=True)  8.3 us
    dot_general x5, matrix products, update_state(): jnp.einsum('hqk,khd->qhd', weights.astype(jnp.bfloat16), value_heads, pre...  7.95 us
  transfers between devices with their start and end apart: 9, of which 6 were waited for; matrix products, arithmetic and copies ran while one was open for 17% of the time, Pallas kernels for 0%

commit v1 on v0

v1 whole, which is shorter than its diff:
```python
import functools
import math

import jax
import jax.numpy as jnp
from jax import lax
from jax.experimental import pallas as pl
from jax.experimental.pallas import tpu as pltpu
from jax.sharding import PartitionSpec as P

MESH = pl.DeviceIdType.MESH
HEAD_DIM = 128
SPANS = 4
NY, NX, NZ = 4, 4, 8
GROUP = 5
WIDTH = GROUP * HEAD_DIM
ROWS = 32
HOPS = (0, 1, 7, 2, 6, 3, 5, 4)
CHUNKS = 12
FIRST_Z = 2
X_CHUNKS = 9
KEYS = 8 * ROWS
LOG2E = 1.4426950408889634
HIDDEN = -1e30


def device(y, z, x, core):
    return {"chain": (y * 2 + z // 4) * NX + x, "head": (z % 4) * 2 + core}


def group_columns(z):
    group = (z % 4) * 2 + z // 4
    return pl.ds(pl.multiple_of(group * WIDTH, 128), WIDTH)


def kernel(
    levels, timesteps, cache_mask, latent, query_in, key_in, value_in, cache_keys, cache_values, time_weight,
    out,
    query, kv, attended, returned, shifted, weight, gate, peak, total, summed, bias,
    send_z, send_x, send_y, send_o, recv_q, recv_k, recv_v, recv_x, recv_y, recv_o, local,
):
    chain, head = lax.axis_index("chain"), lax.axis_index("head")
    y, x = chain // 8, chain % 4
    zh, zl, core = (chain // 4) % 2, head // 2, head % 2
    z = zh * 4 + zl
    up, down = (y + 1) % 4, (y + 3) % 4
    right, left = (x + 1) % 4, (x + 3) % 4
    sibling = device(y, z, x, 1 - core)
    across = device(y, (z + 4) % 8, x, 1 - core)

    def remote(src, dst, send, recv, to):
        return pltpu.make_async_remote_copy(
            src_ref=src, dst_ref=dst, send_sem=send, recv_sem=recv, device_id=to, device_id_type=MESH
        )

    mine = group_columns(z)
    own = [
        pltpu.make_async_copy(key_in.at[:, mine], kv.at[0, 0, 0], recv_k.at[0]),
        pltpu.make_async_copy(value_in.at[:, mine], kv.at[0, 1, 0], recv_v.at[0]),
        pltpu.make_async_copy(query_in.at[:, mine], query.at[0], recv_q.at[0]),
    ]
    for copy in own:
        copy.start()
    weight_copy = pltpu.make_async_copy(time_weight, weight, local.at[0])
    weight_copy.start()

    @pl.when(core == zh)
    def _():
        pltpu.make_async_copy(cache_keys, kv.at[1, 0, 0], recv_k.at[1]).start()
        pltpu.make_async_copy(cache_values, kv.at[1, 1, 0], recv_v.at[1]).start()

    barrier = pltpu.get_barrier_semaphore()
    partners = [sibling, across, device(y, z, right, core), device(y, z, left, core)]
    partners += [device(up, z, x, core), device(down, z, x, core)]
    for hop in HOPS[1:]:
        partners += [device(row, (z + hop) % 8, x, core) for row in (y, up, down)]
    for partner in partners:
        pl.semaphore_signal(barrier, inc=1, device_id=partner, device_id_type=MESH)
    pl.semaphore_wait(barrier, len(partners))

    def cache_across(which, source, recv):
        return remote(source, kv.at[1, which, 0], send_z.at[0, which], recv.at[1], across)

    def query_over_z(j):
        to = (z + HOPS[j]) % 8
        return remote(
            query_in.at[:, group_columns(to)], query.at[j], send_z.at[j, 2], recv_q.at[j], device(y, to, x, core)
        )

    def kv_over_z(j, which, source, recv):
        to = (z + HOPS[j]) % 8
        return remote(
            source.at[:, group_columns(to)],
            kv.at[j + 1, which, 0],
            send_z.at[j, which],
            recv.at[j + 1],
            device(y, to, x, core),
        )

    def over_x(i):
        own_kv = kv.at[i, :, 0]
        return (
            remote(own_kv, kv.at[i, :, 1], send_x.at[i, 0], recv_x.at[i, 0], device(y, z, right, core)),
            remote(own_kv, kv.at[i, :, 3], send_x.at[i, 1], recv_x.at[i, 1], device(y, z, left, core)),
            remote(kv.at[i, 0, 1], kv.at[i, 0, 2], send_x.at[i, 2], recv_x.at[i, 2], device(y, z, right, core)),
            remote(kv.at[i, 1, 3], kv.at[i, 1, 2], send_x.at[i, 3], recv_x.at[i, 3], device(y, z, left, core)),
        )

    def to_sibling(i, send, recv):
        return remote(kv.at[i, :, 0:4], kv.at[i, :, 4:8], send, recv, sibling)

    def sibling_x(i):
        return to_sibling(i, send_x.at[i, 4], recv_x.at[i, 4])

    half = slice(0, 4)
    to_up, to_down = device(up, z, x, core), device(down, z, x, core)
    y_up = remote(kv.at[1, :, half], kv.at[9, :, half], send_y.at[0], recv_y.at[0], to_up)
    y_down = remote(kv.at[1, :, half], kv.at[10, :, half], send_y.at[1], recv_y.at[1], to_down)
    y_on_up = remote(kv.at[9, 0, half], kv.at[11, 0, half], send_y.at[2], recv_y.at[2], to_up)
    y_on_down = remote(kv.at[10, 1, half], kv.at[11, 1, half], send_y.at[3], recv_y.at[3], to_down)
    latent_down = remote(latent, shifted, send_y.at[7], recv_y.at[7], to_down)

    def sibling_y(i):
        return to_sibling(i, send_y.at[i - 5], recv_y.at[i - 5])

    def back(j):
        to = (z - HOPS[j] + 8) % 8
        return remote(attended.at[j], returned.at[:, mine], send_o.at[j], recv_o.at[j], device(down, to, x, core))

    @pl.when(core != zh)
    def _():
        cache_across(0, cache_keys, recv_k).start()
        cache_across(1, cache_values, recv_v).start()

    for j in range(1, 8):
        if j == 3:
            for early in range(1, 8):
                query_over_z(early).start()
        kv_over_z(j, 0, key_in, recv_k).start()
        kv_over_z(j, 1, value_in, recv_v).start()
    latent_down.start()

    for i in range(CHUNKS):
        for slot in range(8):
            if i == 1 or i >= 9:
                plane = {1: y, 9: down, 10: up, 11: (y + 2) % 4}[i]
                side = core if slot < 4 else 1 - core
                block = plane * 8 + side * 4 + (x + (0, 3, 2, 1)[slot % 4]) % 4
                bias[i * 8 + slot] = jnp.where(cache_mask[y, block] == 1, 0.0, HIDDEN).astype(jnp.float32)
            else:
                bias[i * 8 + slot] = jnp.float32(0.0)

    stamp = timesteps[levels[up]].astype(jnp.float32)
    count = 128
    index = lax.broadcasted_iota(jnp.int32, (8, count), 1).astype(jnp.float32)
    phase = stamp * jnp.exp(-math.log(10000.0) * index / count)
    embed = jnp.concatenate([jnp.cos(phase), jnp.sin(phase)], axis=1).astype(jnp.bfloat16)
    weight_copy.wait()

    def gate_columns(c, carry):
        columns = pl.ds(pl.multiple_of(c * WIDTH, 128), WIDTH)
        gate[:, columns] = jnp.dot(embed, weight[:, columns], preferred_element_type=jnp.float32)
        return carry

    lax.fori_loop(0, 8, gate_columns, 0)

    peak[...] = jnp.full_like(peak, HIDDEN)
    total[...] = jnp.zeros_like(total)
    summed[...] = jnp.zeros_like(summed)
    own[2].wait()
    for j in range(1, 8):
        query_over_z(j).wait_recv()

    def attend(i):
        for h in range(GROUP):
            columns = slice(h * HEAD_DIM, (h + 1) * HEAD_DIM)
            keys = kv[i, 0, :, :, columns].reshape(KEYS, HEAD_DIM)
            values = kv[i, 1, :, :, columns].reshape(KEYS, HEAD_DIM)
            queries = query[:, :, columns].reshape(KEYS, HEAD_DIM)
            scores = lax.dot_general(keys, queries, (((1,), (1,)), ((), ())), preferred_element_type=jnp.float32)
            scores = scores * (LOG2E / math.sqrt(HEAD_DIM))
            scores = jnp.concatenate(
                [scores[slot * ROWS : (slot + 1) * ROWS] + bias[i * 8 + slot] for slot in range(8)], axis=0
            )
            old = peak[h]
            new = jnp.maximum(old, jnp.max(scores, axis=0, keepdims=True))
            weights = jnp.exp2(scores - new)
            factor = jnp.exp2(old - new)
            peak[h] = new
            total[h] = factor * total[h] + jnp.sum(weights, axis=0, keepdims=True)
            added = lax.dot_general(
                values, weights.astype(jnp.bfloat16), (((0,), (0,)), ((), ())), preferred_element_type=jnp.float32
            )
            summed[h] = factor * summed[h] + added

    def turn(t, carry):
        @pl.when(t < X_CHUNKS)
        def _():
            pltpu.make_async_copy(kv.at[t, 0, 0], kv.at[t, 0, 0], recv_k.at[t]).wait()
            pltpu.make_async_copy(kv.at[t, 1, 0], kv.at[t, 1, 0], recv_v.at[t]).wait()
            over_x(t)[0].start()
            over_x(t)[1].start()

        @pl.when((t >= 1) & (t < X_CHUNKS + 1))
        def _():
            copies = over_x(t - 1)
            copies[0].wait_recv()
            copies[2].start()
            copies[1].wait_recv()
            copies[3].start()

        @pl.when((t >= 2) & (t < X_CHUNKS + 2))
        def _():
            copies = over_x(t - 2)
            copies[2].wait_recv()
            copies[3].wait_recv()
            sibling_x(t - 2).start()

        @pl.when(t == 3)
        def _():
            y_up.start()
            y_down.start()

        @pl.when(t == 6)
        def _():
            y_up.wait_recv()
            y_on_up.start()
            y_down.wait_recv()
            y_on_down.start()
            sibling_y(9).start()
            sibling_y(10).start()

        @pl.when(t == 8)
        def _():
            y_on_up.wait_recv()
            y_on_down.wait_recv()
            sibling_y(11).start()

        @pl.when(t >= 3)
        def _():
            sibling_x(t - 3).wait_recv()

        @pl.when(t == 8)
        def _():
            sibling_y(9).wait_recv()

        @pl.when(t == 9)
        def _():
            sibling_y(10).wait_recv()

        @pl.when(t == 10)
        def _():
            sibling_y(11).wait_recv()

        def ready(e, carry):
            attend(jnp.where(e == 0, t - 3, t + 1))
            return carry

        ready_count = jnp.where(t < 3, 0, jnp.where((t >= 8) & (t <= 10), 2, 1))
        lax.fori_loop(0, ready_count, ready, 0)
        return carry

    lax.fori_loop(0, X_CHUNKS + 3, turn, 0)

    for h in range(GROUP):
        result = summed[h] * (1.0 / total[h])
        attended[:, :, h * HEAD_DIM : (h + 1) * HEAD_DIM] = result.T.astype(jnp.bfloat16).reshape(8, ROWS, HEAD_DIM)
    for j in range(8):
        back(j).start()

    latent_down.wait_recv()
    for j in range(8):
        back(j).wait_recv()
        columns = group_columns((z + HOPS[j]) % 8)
        out[:, columns] = (
            shifted[:, columns].astype(jnp.float32) + gate[0:1, columns] * returned[:, columns].astype(jnp.float32)
        ).astype(jnp.bfloat16)

    @pl.when(core != zh)
    def _():
        cache_across(0, cache_keys, recv_k).wait_send()
        cache_across(1, cache_values, recv_v).wait_send()

    for j in range(1, 8):
        query_over_z(j).wait_send()
        kv_over_z(j, 0, key_in, recv_k).wait_send()
        kv_over_z(j, 1, value_in, recv_v).wait_send()

    def sent(i, carry):
        for copy in over_x(i):
            copy.wait_send()
        sibling_x(i).wait_send()
        return carry

    lax.fori_loop(0, X_CHUNKS, sent, 0)
    for copy in (y_up, y_down, y_on_up, y_on_down, sibling_y(9), sibling_y(10), sibling_y(11), latent_down):
        copy.wait_send()
    for j in range(8):
        back(j).wait_send()


def shards(
    latent, query_in, key_in, value_in, cache_keys, cache_values, levels, timesteps, cache_mask, time_weight
):
    anywhere = pl.BlockSpec(memory_space=pl.ANY)
    scalars = pl.BlockSpec(memory_space=pltpu.SMEM)
    bf16, f32 = jnp.bfloat16, jnp.float32
    dma = pltpu.SemaphoreType.DMA
    return pl.pallas_call(
        kernel,
        out_shape=jax.ShapeDtypeStruct(latent.shape, latent.dtype),
        in_specs=[scalars] * 3 + [anywhere] * 7,
        out_specs=pl.BlockSpec(memory_space=pltpu.VMEM),
        scratch_shapes=[
            pltpu.VMEM((8, ROWS, WIDTH), bf16),
            pltpu.VMEM((CHUNKS, 2, 8, ROWS, WIDTH), bf16),
            pltpu.VMEM((8, ROWS, WIDTH), bf16),
            pltpu.VMEM(latent.shape, bf16),
            pltpu.VMEM(latent.shape, bf16),
            pltpu.VMEM(time_weight.shape, bf16),
            pltpu.VMEM((8, latent.shape[1]), f32),
            pltpu.VMEM((GROUP, 1, KEYS), f32),
            pltpu.VMEM((GROUP, 1, KEYS), f32),
            pltpu.VMEM((GROUP, HEAD_DIM, KEYS), f32),
            pltpu.SMEM((CHUNKS * 8,), f32),
            dma((8, 3)),
            dma((X_CHUNKS, 5)),
            dma((8,)),
            dma((8,)),
            dma((8,)),
            dma((X_CHUNKS,)),
            dma((X_CHUNKS,)),
            dma((X_CHUNKS, 5)),
            dma((8,)),
            dma((8,)),
            dma((1,)),
        ],
        compiler_params=pltpu.CompilerParams(
            collective_id=0, has_side_effects=True, vmem_limit_bytes=40 * 1024 * 1024
        ),
        cost_estimate=pl.CostEstimate(flops=2 * 10**9, bytes_accessed=5 * 10**6, transcendentals=4 * 10**6),
    )(
        levels, timesteps, cache_mask, latent, query_in, key_in, value_in, cache_keys, cache_values, time_weight
    )


def solution(mesh):
    return jax.shard_map(
        shards,
        mesh=mesh,
        in_specs=(
            P(("chain", "head"), None),
            P(("chain", "head"), None),
            P(("chain", "head"), None),
            P(("chain", "head"), None),
            P("chain", "head"),
            P("chain", "head"),
            P(),
            P(),
            P(),
            P(),
        ),
        out_specs=P(("chain", "head"), None),
        check_vma=False,
    )
```

time: 341 us -> 85.6 us (0.25)
  the two profiles are of different devices: /device:TPU:1 before, /device:TPU:56 now
where the time goes in v1:
time: 85.6 us; the launch traced here: 85.2 us
  Pallas kernels  75.2 us (88%)
  local copies, waits for them, and re-layouts  9.9 us (12%)
    pallas_call x1, Pallas kernels, shards(): pl.pallas_call(kernel, out_shape=jax.ShapeDtypeStruct(latent.shape, laten...  75.2 us
    unnamed x21, local copies, waits for them, and re-layouts  9.9 us

profile of v1, /device:TPU:56, one launch (start us, length us, event | category | flops | bytes accessed | tf_op | source)
XLA Modules:
  0.0 85.2 jit_solution(17190244411339057539)
XLA Ops:
  0.0 0.0 copy-start
  0.0 1.7 %copy-done = bf16[256,5120]{1,0:T(8,128)(2,1)S(1)} copy-done((bf16[256,5120]{1,0:T(8,128)(2,1)S(1)}, bf16[256,5120]{1,0:T(8,128)(2,1)}, u32[]{:S(2)}) %copy-start) | copy-done | bytes 2621464
  1.7 0.0 copy-start.1
  1.7 1.0 %copy-done.1 = bf16[32,5120]{1,0:T(8,128)(2,1)S(1)} copy-done((bf16[32,5120]{1,0:T(8,128)(2,1)S(1)}, bf16[32,5120]{1,0:T(8,128)(2,1)}, u32[]{:S(2)}) %copy-start.1) | copy-done | bytes 327704
  2.7 0.0 copy-start.2
  2.7 1.0 %copy-done.2 = bf16[32,5120]{1,0:T(8,128)(2,1)S(1)} copy-done((bf16[32,5120]{1,0:T(8,128)(2,1)S(1)}, bf16[32,5120]{1,0:T(8,128)(2,1)}, u32[]{:S(2)}) %copy-start.2) | copy-done | bytes 327704
  3.7 0.0 copy-start.3
  3.7 1.0 %copy-done.3 = bf16[32,5120]{1,0:T(8,128)(2,1)S(1)} copy-done((bf16[32,5120]{1,0:T(8,128)(2,1)S(1)}, bf16[32,5120]{1,0:T(8,128)(2,1)}, u32[]{:S(2)}) %copy-start.3) | copy-done | bytes 327704
  4.7 0.0 copy-start.4
  4.7 1.0 %copy-done.4 = bf16[32,5120]{1,0:T(8,128)(2,1)S(1)} copy-done((bf16[32,5120]{1,0:T(8,128)(2,1)S(1)}, bf16[32,5120]{1,0:T(8,128)(2,1)}, u32[]{:S(2)}) %copy-start.4) | copy-done | bytes 327704
  5.6 0.0 copy-start.5
  5.6 0.8 copy-done.5
  6.4 0.0 copy-start.6
  6.4 0.8 copy-done.6
  7.2 0.0 copy-start.7
  7.2 0.7 copy-done.7
  7.9 0.0 copy-start.8
  7.9 0.7 copy-done.8
  8.5 0.0 copy-start.9
  8.5 0.7 copy-done.9
  9.2 75.2 %shard_map.100 = bf16[32,5120]{1,0:T(8,128)(2,1)S(1)} custom-call(s32[4]{0:T(128)S(1)} %copy-done.8, s32[50]{0:T(128)S(1)} %copy-done.9, s32[4,32]{1,0:T(4,128)S(1)} %copy-done.7, bf16[32,5120]{1,0:T(8,128)(2,1)S(1)} %copy-done.1, bf16[32,5120]{1,0:T(8,128)(2,1)S(1)} %copy-done.2, bf16[32,5120]{1,0:T(8,128)(2,1)S(1)} %copy-done.3, ...), custom_call_target="tpu_custom_call" | custom-call | flops 2000000000 | bytes 5000000 | tf_op jit(solution)/shard_map/pallas_call | solution.py:309
  84.4 0.7 copy.12
Async XLA Ops:
  0.0 1.7 %copy-start = (bf16[256,5120]{1,0:T(8,128)(2,1)S(1)}, bf16[256,5120]{1,0:T(8,128)(2,1)}, u32[]{:S(2)}) copy-start(bf16[256,5120]{1,0:T(8,128)(2,1)} %time_weight.1) | copy-start | bytes 7864324
  1.7 1.0 %copy-start.1 = (bf16[32,5120]{1,0:T(8,128)(2,1)S(1)}, bf16[32,5120]{1,0:T(8,128)(2,1)}, u32[]{:S(2)}) copy-start(bf16[32,5120]{1,0:T(8,128)(2,1)} %latent.1) | copy-start | bytes 983044
  2.7 1.0 %copy-start.2 = (bf16[32,5120]{1,0:T(8,128)(2,1)S(1)}, bf16[32,5120]{1,0:T(8,128)(2,1)}, u32[]{:S(2)}) copy-start(bf16[32,5120]{1,0:T(8,128)(2,1)} %query_in.1) | copy-start | bytes 983044
  3.7 1.0 %copy-start.3 = (bf16[32,5120]{1,0:T(8,128)(2,1)S(1)}, bf16[32,5120]{1,0:T(8,128)(2,1)}, u32[]{:S(2)}) copy-start(bf16[32,5120]{1,0:T(8,128)(2,1)} %key_in.1) | copy-start | bytes 983044
  4.7 1.0 %copy-start.4 = (bf16[32,5120]{1,0:T(8,128)(2,1)S(1)}, bf16[32,5120]{1,0:T(8,128)(2,1)}, u32[]{:S(2)}) copy-start(bf16[32,5120]{1,0:T(8,128)(2,1)} %value_in.1) | copy-start | bytes 983044
  5.6 0.8 copy-start.5
  6.4 0.8 copy-start.6
  7.2 0.7 copy-start.7
  7.9 0.7 copy-start.8
  8.5 0.7 copy-start.9

commit v2 on v1

--- a/solution.py
+++ b/solution.py
@@ -132,12 +132,14 @@
         cache_across(0, cache_keys, recv_k).start()
         cache_across(1, cache_values, recv_v).start()
 
-    for j in range(1, 8):
-        if j == 3:
-            for early in range(1, 8):
-                query_over_z(early).start()
+    def start_kv(j):
         kv_over_z(j, 0, key_in, recv_k).start()
         kv_over_z(j, 1, value_in, recv_v).start()
+
+    start_kv(1)
+    start_kv(2)
+    for j in range(1, 8):
+        query_over_z(j).start()
     latent_down.start()
 
     for i in range(CHUNKS):
@@ -167,9 +169,6 @@
     peak[...] = jnp.full_like(peak, HIDDEN)
     total[...] = jnp.zeros_like(total)
     summed[...] = jnp.zeros_like(summed)
-    own[2].wait()
-    for j in range(1, 8):
-        query_over_z(j).wait_recv()
 
     def attend(i):
         for h in range(GROUP):
@@ -201,6 +200,13 @@
             over_x(t)[0].start()
             over_x(t)[1].start()
 
+        for turn_of, hops in ((1, (3, 4)), (3, (5, 6)), (5, (7,))):
+
+            @pl.when(t == turn_of)
+            def _(hops=hops):
+                for j in hops:
+                    start_kv(j)
+
         @pl.when((t >= 1) & (t < X_CHUNKS + 1))
         def _():
             copies = over_x(t - 1)
@@ -220,6 +226,9 @@
         def _():
             y_up.start()
             y_down.start()
+            own[2].wait()
+            for j in range(1, 8):
+                query_over_z(j).wait_recv()
 
         @pl.when(t == 6)
         def _():
@@ -336,7 +345,7 @@
             dma((1,)),
         ],
         compiler_params=pltpu.CompilerParams(
-            collective_id=0, has_side_effects=True, vmem_limit_bytes=40 * 1024 * 1024
+            collective_id=0, has_side_effects=True, vmem_limit_bytes=64 * 1024 * 1024
         ),
         cost_estimate=pl.CostEstimate(flops=2 * 10**9, bytes_accessed=5 * 10**6, transcendentals=4 * 10**6),
     )(

time: 85.6 us -> 69.8 us (0.82)
  the two profiles are of different devices: /device:TPU:56 before, /device:TPU:1 now
where the time goes in v2:
time: 69.8 us; the launch traced here: 69.4 us
  Pallas kernels  67.6 us (97%)
  local copies, waits for them, and re-layouts  1.72 us (2%)
    pallas_call x1, Pallas kernels, shards(): pl.pallas_call(kernel, out_shape=jax.ShapeDtypeStruct(latent.shape, laten...  67.6 us
    unnamed x1, local copies, waits for them, and re-layouts  1.72 us

profile of v2, /device:TPU:1, one launch (start us, length us, event | category | flops | bytes accessed | tf_op | source)
XLA Modules:
  0.0 69.4 jit_solution(7993305069915089559)
XLA Ops:
  0.0 67.6 %shard_map.100 = bf16[32,5120]{1,0:T(8,128)(2,1)} custom-call(s32[4]{0:T(128)} %levels.1, s32[50]{0:T(128)} %timesteps.1, s32[4,32]{1,0:T(4,128)} %cache_mask.1, bf16[32,5120]{1,0:T(8,128)(2,1)} %latent.1, bf16[32,5120]{1,0:T(8,128)(2,1)} %query_in.1, bf16[32,5120]{1,0:T(8,128)(2,1)} %key_in.1, bf16[32,5120]{1,0:T(8,128)(2,1)} %value_in.1, ...), custom_call_target="tpu_custom_call" | custom-call | flops 2000000000 | bytes 5000000 | tf_op jit(solution)/shard_map/pallas_call | solution.py:318
  67.7 1.7 %copy.12 = bf16[32,5120]{1,0:T(8,128)(2,1)} copy(bf16[32,5120]{1,0:T(8,128)(2,1)} %shard_map.100) | data formatting | bytes 655360

commit v3 on v1

v3 whole, which is shorter than its diff:
```python
import functools
import math

import jax
import jax.numpy as jnp
from jax import lax
from jax.experimental import pallas as pl
from jax.experimental.pallas import tpu as pltpu
from jax.sharding import PartitionSpec as P

MESH = pl.DeviceIdType.MESH
HEAD_DIM = 128
SPANS = 4
NY, NX, NZ = 4, 4, 8
GROUP = 5
WIDTH = GROUP * HEAD_DIM
ROWS = 32
HOPS = (0, 1, 7, 2, 6, 3, 5, 4)
CHUNKS = 12
ATTEND = (0, 1, 2, 3, 9, 10, 8, 4, 5, 11, 6, 7)
PLACE = tuple(ATTEND.index(i) for i in range(CHUNKS))
X_CHUNKS = 9
PARTS = ((0, 3), (3, 5))
KEYS = 8 * ROWS
LOG2E = 1.4426950408889634
HIDDEN = -1e30


def device(y, z, x, core):
    return {"chain": (y * 2 + z // 4) * NX + x, "head": (z % 4) * 2 + core}


def group_columns(z):
    group = (z % 4) * 2 + z // 4
    return pl.ds(pl.multiple_of(group * WIDTH, 128), WIDTH)


def part_columns(z, part):
    group = (z % 4) * 2 + z // 4
    lower, upper = PARTS[part]
    return pl.ds(pl.multiple_of(group * WIDTH + lower * HEAD_DIM, 128), (upper - lower) * HEAD_DIM)


def kernel(
    levels, timesteps, cache_mask, latent, query_in, key_in, value_in, cache_keys, cache_values, time_weight,
    out,
    query, kv, relay, attended, returned, shifted, weight, gate, peak, total, summed, bias,
    send_z, send_x, send_y, send_o, recv_q, recv_kv, recv_relay, recv_x, recv_y, recv_o, local,
):
    chain, head = lax.axis_index("chain"), lax.axis_index("head")
    y, x = chain // 8, chain % 4
    zh, zl, core = (chain // 4) % 2, head // 2, head % 2
    z = zh * 4 + zl
    up, down = (y + 1) % 4, (y + 3) % 4
    right, left = device(y, z, (x + 1) % 4, core), device(y, z, (x + 3) % 4, core)
    sibling = device(y, z, x, 1 - core)
    across = device(y, (z + 4) % 8, x, 1 - core)
    back_two = device(y, (z + 6) % 8, x, core)
    to_up, to_down = device(up, z, x, core), device(down, z, x, core)
    mine = group_columns(z)

    def remote(src, dst, send, recv, to):
        return pltpu.make_async_remote_copy(
            src_ref=src, dst_ref=dst, send_sem=send, recv_sem=recv, device_id=to, device_id_type=MESH
        )

    def chunk(i):
        return kv.at[PLACE[i]]

    own_query = pltpu.make_async_copy(query_in.at[:, mine], query.at[0], recv_q.at[0])
    own_query.start()
    for which, source in enumerate((key_in, value_in)):
        pltpu.make_async_copy(source.at[:, mine], chunk(0).at[which, 0], recv_kv.at[0, which]).start()
    weight_copy = pltpu.make_async_copy(time_weight, weight, local.at[0])
    weight_copy.start()

    @pl.when(core == zh)
    def _():
        for which, source in enumerate((cache_keys, cache_values)):
            pltpu.make_async_copy(source, chunk(1).at[which, 0], recv_kv.at[1, which]).start()

    barrier = pltpu.get_barrier_semaphore()
    partners = [sibling, across, right, left, to_up, to_down]
    for hop in HOPS[1:]:
        partners += [device(row, (z + hop) % 8, x, core) for row in (y, up, down)]
    for partner in partners:
        pl.semaphore_signal(barrier, inc=1, device_id=partner, device_id_type=MESH)
    pl.semaphore_wait(barrier, len(partners))

    def cache_across(which):
        source = (cache_keys, cache_values)[which]
        return remote(source, chunk(1).at[which, 0], send_z.at[0, which], recv_kv.at[1, which], across)

    def query_over_z(j):
        to = (z + HOPS[j]) % 8
        return remote(
            query_in.at[:, group_columns(to)], query.at[j], send_z.at[j, 2], recv_q.at[j], device(y, to, x, core)
        )

    def kv_over_z(j, which):
        to = (z + HOPS[j]) % 8
        source = (key_in, value_in)[which].at[:, group_columns(to)]
        if HOPS[j] == 4:
            return remote(source, relay.at[which], send_z.at[j, which], recv_relay.at[which], back_two)
        return remote(
            source, chunk(j + 1).at[which, 0], send_z.at[j, which], recv_kv.at[j + 1, which], device(y, to, x, core)
        )

    def relay_on(which):
        return remote(relay.at[which], chunk(8).at[which, 0], send_z.at[8, which], recv_kv.at[8, which], back_two)

    def x_copy(i, n):
        c = chunk(i)
        src, dst, to = (
            (c.at[:, 0], c.at[:, 1], right),
            (c.at[:, 0], c.at[:, 3], left),
            (c.at[0, 1], c.at[0, 2], right),
            (c.at[1, 3], c.at[1, 2], left),
            (c.at[:, 0], c.at[:, 4], sibling),
            (c.at[:, 1], c.at[:, 5], sibling),
            (c.at[:, 2], c.at[:, 6], sibling),
            (c.at[:, 3], c.at[:, 7], sibling),
        )[n]
        return remote(src, dst, send_x.at[i, n], recv_x.at[i, n], to)

    def y_copy(n):
        src, dst, to = (
            (chunk(1).at[:, 0:4], chunk(9).at[:, 0:4], to_up),
            (chunk(1).at[:, 0:4], chunk(10).at[:, 0:4], to_down),
            (chunk(9).at[0, 0:4], chunk(11).at[0, 0:4], to_up),
            (chunk(10).at[1, 0:4], chunk(11).at[1, 0:4], to_down),
            (chunk(9).at[:, 0:4], chunk(9).at[:, 4:8], sibling),
            (chunk(10).at[:, 0:4], chunk(10).at[:, 4:8], sibling),
            (chunk(11).at[:, 0:4], chunk(11).at[:, 4:8], sibling),
            (latent, shifted, to_down),
        )[n]
        return remote(src, dst, send_y.at[n], recv_y.at[n], to)

    def back(j, part):
        to = device(down, (z - HOPS[j] + 8) % 8, x, core)
        lower, upper = (PARTS[part][end] * HEAD_DIM for end in (0, 1))
        columns = part_columns(z, part)
        return remote(
            attended.at[j, :, lower:upper], returned.at[:, columns], send_o.at[j, part], recv_o.at[j, part], to
        )

    def start_z(*js):
        for j in js:
            for which in (0, 1):
                kv_over_z(j, which).start()

    def arrived(i):
        for which in (0, 1):
            place = chunk(i).at[which, 0]
            pltpu.make_async_copy(place, place, recv_kv.at[i, which]).wait()
        for n in (0, 1, 4):
            x_copy(i, n).start()

    def forward(i):
        x_copy(i, 0).wait_recv()
        x_copy(i, 2).start()
        x_copy(i, 1).wait_recv()
        x_copy(i, 3).start()
        x_copy(i, 5).start()
        x_copy(i, 7).start()

    def last_piece(i):
        x_copy(i, 2).wait_recv()
        x_copy(i, 3).wait_recv()
        x_copy(i, 6).start()

    def complete(i):
        if i >= X_CHUNKS:
            y_copy(i - 5).wait_recv()
        else:
            for n in (4, 5, 6, 7):
                x_copy(i, n).wait_recv()

    def start_y():
        y_copy(0).start()
        y_copy(1).start()

    def forward_y():
        for n in (0, 1):
            y_copy(n).wait_recv()
            y_copy(n + 2).start()
            y_copy(n + 4).start()

    def last_y():
        y_copy(2).wait_recv()
        y_copy(3).wait_recv()
        y_copy(6).start()

    def relay_all():
        for which in (0, 1):
            kv_over_z(7, which).wait_recv()
            relay_on(which).start()

    def queries(*js):
        for j in js:
            query_over_z(j).wait_recv()

    @pl.when(core != zh)
    def _():
        cache_across(0).start()
        cache_across(1).start()

    start_z(1, 2, 7)
    for j in range(1, 8):
        query_over_z(j).start()
    y_copy(7).start()

    for i in range(CHUNKS):
        for slot in range(8):
            shown = jnp.float32(0.0)
            if i == 1 or i >= 9:
                plane = {1: y, 9: down, 10: up, 11: (y + 2) % 4}[i]
                side = core if slot < 4 else 1 - core
                block = plane * 8 + side * 4 + (x + (0, 3, 2, 1)[slot % 4]) % 4
                shown = jnp.where(cache_mask[y, block] == 1, 0.0, HIDDEN).astype(jnp.float32)
            bias[PLACE[i] * 8 + slot] = shown

    peak[...] = jnp.full_like(peak, HIDDEN)
    total[...] = jnp.zeros_like(total)
    summed[...] = jnp.zeros_like(summed)

    arrived(0)

    stamp = timesteps[levels[up]].astype(jnp.float32)
    count = 128
    index = lax.broadcasted_iota(jnp.int32, (8, count), 1).astype(jnp.float32)
    phase = stamp * jnp.exp(-math.log(10000.0) * index / count)
    embed = jnp.concatenate([jnp.cos(phase), jnp.sin(phase)], axis=1).astype(jnp.bfloat16)
    weight_copy.wait()

    def gate_columns(c, carry):
        columns = pl.ds(pl.multiple_of(c * WIDTH, 128), WIDTH)
        gate[:, columns] = jnp.dot(embed, weight[:, columns], preferred_element_type=jnp.float32)
        return carry

    lax.fori_loop(0, 8, gate_columns, 0)

    def attend(c, finish=None):
        for h in range(GROUP):
            columns = slice(h * HEAD_DIM, (h + 1) * HEAD_DIM)
            keys = kv[c, 0, :, :, columns].reshape(KEYS, HEAD_DIM)
            values = kv[c, 1, :, :, columns].reshape(KEYS, HEAD_DIM)
            queries = query[:, :, columns].reshape(KEYS, HEAD_DIM)
            scores = lax.dot_general(keys, queries, (((1,), (1,)), ((), ())), preferred_element_type=jnp.float32)
            scores = scores * (LOG2E / math.sqrt(HEAD_DIM))
            scores = jnp.concatenate(
                [scores[slot * ROWS : (slot + 1) * ROWS] + bias[c * 8 + slot] for slot in range(8)], axis=0
            )
            old = peak[h]
            new = jnp.maximum(old, jnp.max(scores, axis=0, keepdims=True))
            weights = jnp.exp2(scores - new)
            factor = jnp.exp2(old - new)
            weight_sum = factor * total[h] + jnp.sum(weights, axis=0, keepdims=True)
            added = lax.dot_general(
                values, weights.astype(jnp.bfloat16), (((0,), (0,)), ((), ())), preferred_element_type=jnp.float32
            )
            value_sum = factor * summed[h] + added
            if finish is None:
                peak[h], total[h], summed[h] = new, weight_sum, value_sum
            else:
                finish(h, value_sum * (1.0 / weight_sum))

    def finish(h, result):
        columns = slice(h * HEAD_DIM, (h + 1) * HEAD_DIM)
        attended[:, :, columns] = result.T.astype(jnp.bfloat16).reshape(8, ROWS, HEAD_DIM)
        for part, (lower, upper) in enumerate(PARTS):
            if h == upper - 1:
                for j in range(8):
                    back(j, part).start()

    def before(c):
        if c == 0:
            arrived(1)
            forward(0)
            arrived(2)
            arrived(3)
            last_piece(0)
            forward(1)
            forward(2)
            last_piece(1)
            start_y()
            forward(3)
            last_piece(2)
            last_piece(3)
            relay_all()
            own_query.wait()
            queries(1, 2, 3, 4)
            start_z(3, 4)
            queries(5, 6, 7)
        if c == 3:
            arrived(8)
        if c == 4:
            arrived(4)
            start_z(5, 6)
            arrived(5)
            forward(8)
            forward_y()
        if c == 5:
            last_piece(8)
            forward(4)
            forward(5)
        if c == 6:
            last_piece(4)
            last_piece(5)
        if c == 8:
            arrived(6)
            arrived(7)
        if c == 9:
            forward(6)
            forward(7)
            last_y()
        if c == 10:
            last_piece(6)
            last_piece(7)
        complete(ATTEND[c])

    def turn(c, carry):
        for now in range(CHUNKS - 1):
            pl.when(c == now)(functools.partial(before, now))
        attend(c)
        return carry

    lax.fori_loop(0, CHUNKS - 1, turn, 0)
    before(CHUNKS - 1)
    attend(CHUNKS - 1, finish)

    y_copy(7).wait_recv()
    for part in range(len(PARTS)):
        for j in range(8):
            back(j, part).wait_recv()
            columns = part_columns((z + HOPS[j]) % 8, part)
            out[:, columns] = (
                shifted[:, columns].astype(jnp.float32) + gate[0:1, columns] * returned[:, columns].astype(jnp.float32)
            ).astype(jnp.bfloat16)

    @pl.when(core != zh)
    def _():
        cache_across(0).wait_send()
        cache_across(1).wait_send()

    for which in (0, 1):
        relay_on(which).wait_send()
    for j in range(1, 8):
        query_over_z(j).wait_send()
        for which in (0, 1):
            kv_over_z(j, which).wait_send()
    for i in range(X_CHUNKS):
        for n in range(8):
            x_copy(i, n).wait_send()
    for n in range(8):
        y_copy(n).wait_send()
    for part in range(len(PARTS)):
        for j in range(8):
            back(j, part).wait_send()


def shards(
    latent, query_in, key_in, value_in, cache_keys, cache_values, levels, timesteps, cache_mask, time_weight
):
    anywhere = pl.BlockSpec(memory_space=pl.ANY)
    scalars = pl.BlockSpec(memory_space=pltpu.SMEM)
    bf16, f32 = jnp.bfloat16, jnp.float32
    dma = pltpu.SemaphoreType.DMA
    return pl.pallas_call(
        kernel,
        out_shape=jax.ShapeDtypeStruct(latent.shape, latent.dtype),
        in_specs=[scalars] * 3 + [anywhere] * 7,
        out_specs=pl.BlockSpec(memory_space=pltpu.VMEM),
        scratch_shapes=[
            pltpu.VMEM((8, ROWS, WIDTH), bf16),
            pltpu.VMEM((CHUNKS, 2, 8, ROWS, WIDTH), bf16),
            pltpu.VMEM((2, ROWS, WIDTH), bf16),
            pltpu.VMEM((8, ROWS, WIDTH), bf16),
            pltpu.VMEM(latent.shape, bf16),
            pltpu.VMEM(latent.shape, bf16),
            pltpu.VMEM(time_weight.shape, bf16),
            pltpu.VMEM((8, latent.shape[1]), f32),
            pltpu.VMEM((GROUP, 1, KEYS), f32),
            pltpu.VMEM((GROUP, 1, KEYS), f32),
            pltpu.VMEM((GROUP, HEAD_DIM, KEYS), f32),
            pltpu.SMEM((CHUNKS * 8,), f32),
            dma((9, 3)),
            dma((X_CHUNKS, 8)),
            dma((8,)),
            dma((8, len(PARTS))),
            dma((8,)),
            dma((X_CHUNKS, 2)),
            dma((2,)),
            dma((X_CHUNKS, 8)),
            dma((8,)),
            dma((8, len(PARTS))),
            dma((1,)),
        ],
        compiler_params=pltpu.CompilerParams(
            collective_id=0, has_side_effects=True, vmem_limit_bytes=64 * 1024 * 1024
        ),
        cost_estimate=pl.CostEstimate(flops=2 * 10**9, bytes_accessed=5 * 10**6, transcendentals=4 * 10**6),
    )(
        levels, timesteps, cache_mask, latent, query_in, key_in, value_in, cache_keys, cache_values, time_weight
    )


def solution(mesh):
    return jax.shard_map(
        shards,
        mesh=mesh,
        in_specs=(
            P(("chain", "head"), None),
            P(("chain", "head"), None),
            P(("chain", "head"), None),
            P(("chain", "head"), None),
            P("chain", "head"),
            P("chain", "head"),
            P(),
            P(),
            P(),
            P(),
        ),
        out_specs=P(("chain", "head"), None),
        check_vma=False,
    )
```

time: 85.6 us -> 78.3 us (0.915)
  the two profiles are of different devices: /device:TPU:56 before, /device:TPU:1 now
where the time goes in v3:
time: 78.3 us; the launch traced here: 77.7 us
  Pallas kernels  76 us (97%)
  local copies, waits for them, and re-layouts  1.72 us (2%)
    pallas_call x1, Pallas kernels, shards(): pl.pallas_call(kernel, out_shape=jax.ShapeDtypeStruct(latent.shape, laten...  76 us
    unnamed x1, local copies, waits for them, and re-layouts  1.72 us

profile of v3, /device:TPU:1, one launch (start us, length us, event | category | flops | bytes accessed | tf_op | source)
XLA Modules:
  0.0 77.7 jit_solution(12751956220869561540)
XLA Ops:
  0.0 76.0 %shard_map.100 = bf16[32,5120]{1,0:T(8,128)(2,1)} custom-call(s32[4]{0:T(128)} %levels.1, s32[50]{0:T(128)} %timesteps.1, s32[4,32]{1,0:T(4,128)} %cache_mask.1, bf16[32,5120]{1,0:T(8,128)(2,1)} %latent.1, bf16[32,5120]{1,0:T(8,128)(2,1)} %query_in.1, bf16[32,5120]{1,0:T(8,128)(2,1)} %key_in.1, bf16[32,5120]{1,0:T(8,128)(2,1)} %value_in.1, ...), custom_call_target="tpu_custom_call" | custom-call | flops 2000000000 | bytes 5000000 | tf_op jit(solution)/shard_map/pallas_call | solution.py:369
  76.0 1.7 %copy.12 = bf16[32,5120]{1,0:T(8,128)(2,1)} copy(bf16[32,5120]{1,0:T(8,128)(2,1)} %shard_map.100) | data formatting | bytes 655360

commit v4 on v2

--- a/solution.py
+++ b/solution.py
@@ -36,7 +36,7 @@
 def kernel(
     levels, timesteps, cache_mask, latent, query_in, key_in, value_in, cache_keys, cache_values, time_weight,
     out,
-    query, kv, attended, returned, shifted, weight, gate, peak, total, summed, bias,
+    query, turned, kv, attended, returned, shifted, weight, gate, peak, total, summed, bias,
     send_z, send_x, send_y, send_o, recv_q, recv_k, recv_v, recv_x, recv_y, recv_o, local,
 ):
     chain, head = lax.axis_index("chain"), lax.axis_index("head")
@@ -136,10 +136,10 @@
         kv_over_z(j, 0, key_in, recv_k).start()
         kv_over_z(j, 1, value_in, recv_v).start()
 
+    for j in range(1, 8):
+        query_over_z(j).start()
     start_kv(1)
     start_kv(2)
-    for j in range(1, 8):
-        query_over_z(j).start()
     latent_down.start()
 
     for i in range(CHUNKS):
@@ -170,26 +170,31 @@
     total[...] = jnp.zeros_like(total)
     summed[...] = jnp.zeros_like(summed)
 
-    def attend(i):
+    def attend(i, cached):
+        def scores_of(h):
+            keys = kv[i, 0, :, :, h * HEAD_DIM : (h + 1) * HEAD_DIM].reshape(KEYS, HEAD_DIM)
+            return jnp.dot(keys, turned[h], preferred_element_type=jnp.float32)
+
+        scale = LOG2E / math.sqrt(HEAD_DIM)
+        following = scores_of(0)
         for h in range(GROUP):
-            columns = slice(h * HEAD_DIM, (h + 1) * HEAD_DIM)
-            keys = kv[i, 0, :, :, columns].reshape(KEYS, HEAD_DIM)
-            values = kv[i, 1, :, :, columns].reshape(KEYS, HEAD_DIM)
-            queries = query[:, :, columns].reshape(KEYS, HEAD_DIM)
-            scores = lax.dot_general(keys, queries, (((1,), (1,)), ((), ())), preferred_element_type=jnp.float32)
-            scores = scores * (LOG2E / math.sqrt(HEAD_DIM))
-            scores = jnp.concatenate(
-                [scores[slot * ROWS : (slot + 1) * ROWS] + bias[i * 8 + slot] for slot in range(8)], axis=0
-            )
+            scores = following
+            if h + 1 < GROUP:
+                following = scores_of(h + 1)
+            if cached:
+                scores = jnp.concatenate(
+                    [scores[slot * ROWS : (slot + 1) * ROWS] + bias[i * 8 + slot] for slot in range(8)], axis=0
+                )
             old = peak[h]
-            new = jnp.maximum(old, jnp.max(scores, axis=0, keepdims=True))
-            weights = jnp.exp2(scores - new)
+            new = jnp.maximum(old, jnp.max(scores, axis=0, keepdims=True) * scale)
+            weights = jnp.exp2(scores * scale - new)
             factor = jnp.exp2(old - new)
-            peak[h] = new
-            total[h] = factor * total[h] + jnp.sum(weights, axis=0, keepdims=True)
+            values = kv[i, 1, :, :, h * HEAD_DIM : (h + 1) * HEAD_DIM].reshape(KEYS, HEAD_DIM)
             added = lax.dot_general(
                 values, weights.astype(jnp.bfloat16), (((0,), (0,)), ((), ())), preferred_element_type=jnp.float32
             )
+            peak[h] = new
+            total[h] = factor * total[h] + jnp.sum(weights, axis=0, keepdims=True)
             summed[h] = factor * summed[h] + added
 
     def turn(t, carry):
@@ -229,6 +234,9 @@
             own[2].wait()
             for j in range(1, 8):
                 query_over_z(j).wait_recv()
+            for h in range(GROUP):
+                columns = slice(h * HEAD_DIM, (h + 1) * HEAD_DIM)
+                turned[h] = query[:, :, columns].reshape(KEYS, HEAD_DIM).astype(jnp.float32).T.astype(jnp.bfloat16)
 
         @pl.when(t == 6)
         def _():
@@ -261,12 +269,14 @@
         def _():
             sibling_y(11).wait_recv()
 
-        def ready(e, carry):
-            attend(jnp.where(e == 0, t - 3, t + 1))
-            return carry
-
-        ready_count = jnp.where(t < 3, 0, jnp.where((t >= 8) & (t <= 10), 2, 1))
-        lax.fori_loop(0, ready_count, ready, 0)
+        @pl.when((t >= 3) & (t != 4))
+        def _():
+            attend(t - 3, False)
+
+        @pl.when((t == 4) | ((t >= 8) & (t <= 10)))
+        def _():
+            attend(jnp.where(t == 4, 1, t + 1), True)
+
         return carry
 
     lax.fori_loop(0, X_CHUNKS + 3, turn, 0)
@@ -276,6 +286,26 @@
         attended[:, :, h * HEAD_DIM : (h + 1) * HEAD_DIM] = result.T.astype(jnp.bfloat16).reshape(8, ROWS, HEAD_DIM)
     for j in range(8):
         back(j).start()
+
+    @pl.when(core != zh)
+    def _():
+        cache_across(0, cache_keys, recv_k).wait_send()
+        cache_across(1, cache_values, recv_v).wait_send()
+
+    for j in range(1, 8):
+        query_over_z(j).wait_send()
+        kv_over_z(j, 0, key_in, recv_k).wait_send()
+        kv_over_z(j, 1, value_in, recv_v).wait_send()
+
+    def sent(i, carry):
+        for copy in over_x(i):
+            copy.wait_send()
+        sibling_x(i).wait_send()
+        return carry
+
+    lax.fori_loop(0, X_CHUNKS, sent, 0)
+    for copy in (y_up, y_down, y_on_up, y_on_down, sibling_y(9), sibling_y(10), sibling_y(11), latent_down):
+        copy.wait_send()
 
     latent_down.wait_recv()
     for j in range(8):
@@ -284,26 +314,6 @@
         out[:, columns] = (
             shifted[:, columns].astype(jnp.float32) + gate[0:1, columns] * returned[:, columns].astype(jnp.float32)
         ).astype(jnp.bfloat16)
-
-    @pl.when(core != zh)
-    def _():
-        cache_across(0, cache_keys, recv_k).wait_send()
-        cache_across(1, cache_values, recv_v).wait_send()
-
-    for j in range(1, 8):
-        query_over_z(j).wait_send()
-        kv_over_z(j, 0, key_in, recv_k).wait_send()
-        kv_over_z(j, 1, value_in, recv_v).wait_send()
-
-    def sent(i, carry):
-        for copy in over_x(i):
-            copy.wait_send()
-        sibling_x(i).wait_send()
-        return carry
-
-    lax.fori_loop(0, X_CHUNKS, sent, 0)
-    for copy in (y_up, y_down, y_on_up, y_on_down, sibling_y(9), sibling_y(10), sibling_y(11), latent_down):
-        copy.wait_send()
     for j in range(8):
         back(j).wait_send()
 
@@ -322,6 +332,7 @@
         out_specs=pl.BlockSpec(memory_space=pltpu.VMEM),
         scratch_shapes=[
             pltpu.VMEM((8, ROWS, WIDTH), bf16),
+            pltpu.VMEM((GROUP, HEAD_DIM, KEYS), bf16),
             pltpu.VMEM((CHUNKS, 2, 8, ROWS, WIDTH), bf16),
             pltpu.VMEM((8, ROWS, WIDTH), bf16),
             pltpu.VMEM(latent.shape, bf16),

time: 69.8 us -> 67 us (0.960); the launches traced: 69.4 us -> 65.8 us
  Pallas kernels: 67.6 us -> 64.1 us
    pallas_call x1, Pallas kernels: 67.6 us -> 64.1 us  [shards(): pl.pallas_call(kernel, out_shape=jax.ShapeDtypeStruct(latent.shape, laten...]
where the time goes in v4:
time: 67 us; the launch traced here: 65.8 us
  Pallas kernels  64.1 us (96%)
  local copies, waits for them, and re-layouts  1.72 us (3%)
    pallas_call x1, Pallas kernels, shards(): pl.pallas_call(kernel, out_shape=jax.ShapeDtypeStruct(latent.shape, laten...  64.1 us
    unnamed x1, local copies, waits for them, and re-layouts  1.72 us

profile of v4, /device:TPU:1, one launch (start us, length us, event | category | flops | bytes accessed | tf_op | source)
XLA Modules:
  0.0 65.8 jit_solution(1089984967925978883)
XLA Ops:
  0.0 64.1 %shard_map.100 = bf16[32,5120]{1,0:T(8,128)(2,1)} custom-call(s32[4]{0:T(128)} %levels.1, s32[50]{0:T(128)} %timesteps.1, s32[4,32]{1,0:T(4,128)} %cache_mask.1, bf16[32,5120]{1,0:T(8,128)(2,1)} %latent.1, bf16[32,5120]{1,0:T(8,128)(2,1)} %query_in.1, bf16[32,5120]{1,0:T(8,128)(2,1)} %key_in.1, bf16[32,5120]{1,0:T(8,128)(2,1)} %value_in.1, ...), custom_call_target="tpu_custom_call" | custom-call | flops 2000000000 | bytes 5000000 | tf_op jit(solution)/shard_map/pallas_call | solution.py:328
  64.1 1.7 %copy.12 = bf16[32,5120]{1,0:T(8,128)(2,1)} copy(bf16[32,5120]{1,0:T(8,128)(2,1)} %shard_map.100) | data formatting | bytes 655360

commit v5 on v4

v5 whole, which is shorter than its diff:
```python
import functools
import math

import jax
import jax.numpy as jnp
from jax import lax
from jax.experimental import pallas as pl
from jax.experimental.pallas import tpu as pltpu
from jax.sharding import PartitionSpec as P

MESH = pl.DeviceIdType.MESH
HEAD_DIM = 128
SPANS = 4
NY, NX, NZ = 4, 4, 8
GROUP = 5
WIDTH = GROUP * HEAD_DIM
ROWS = 32
CHUNKS = 12
FIRST_Z = 2
X_CHUNKS = 9
KEYS = 8 * ROWS
LOG2E = 1.4426950408889634
HIDDEN = -1e30


def device(y, z, x, core):
    return {"chain": (y * 2 + z // 4) * NX + x, "head": (z % 4) * 2 + core}


def group_columns(z):
    group = (z % 4) * 2 + z // 4
    return pl.ds(pl.multiple_of(group * WIDTH, 128), WIDTH)


def hop_of(j):
    return jnp.where(j % 2 == 1, (j + 1) // 2, (8 - j // 2) % 8)


def kernel(
    levels, timesteps, cache_mask, latent, query_in, key_in, value_in, cache_keys, cache_values, time_weight,
    out,
    query, turned, kv, attended, returned, shifted, weight, gate, peak, total, summed, bias,
    send_z, send_x, send_y, send_o, recv_q, recv_kv, recv_x, recv_y, recv_o, local,
):
    chain, head = lax.axis_index("chain"), lax.axis_index("head")
    y, x = chain // 8, chain % 4
    zh, zl, core = (chain // 4) % 2, head // 2, head % 2
    z = zh * 4 + zl
    up, down = (y + 1) % 4, (y + 3) % 4
    right, left = device(y, z, (x + 1) % 4, core), device(y, z, (x + 3) % 4, core)
    sibling = device(y, z, x, 1 - core)
    across = device(y, (z + 4) % 8, x, 1 - core)
    to_up, to_down = device(up, z, x, core), device(down, z, x, core)
    mine = group_columns(z)

    def loop(lower, upper, body):
        def step(n, carry):
            body(n)
            return carry

        lax.fori_loop(lower, upper, step, 0)

    def remote(src, dst, send, recv, to):
        return pltpu.make_async_remote_copy(
            src_ref=src, dst_ref=dst, send_sem=send, recv_sem=recv, device_id=to, device_id_type=MESH
        )

    pltpu.make_async_copy(key_in.at[:, mine], kv.at[0, 0, 0], recv_kv.at[0, 0]).start()
    pltpu.make_async_copy(value_in.at[:, mine], kv.at[0, 1, 0], recv_kv.at[0, 1]).start()
    own_query = pltpu.make_async_copy(query_in.at[:, mine], query.at[0], recv_q.at[0])
    own_query.start()
    weight_copy = pltpu.make_async_copy(time_weight, weight, local.at[0])
    weight_copy.start()

    @pl.when(core == zh)
    def _():
        pltpu.make_async_copy(cache_keys, kv.at[1, 0, 0], recv_kv.at[1, 0]).start()
        pltpu.make_async_copy(cache_values, kv.at[1, 1, 0], recv_kv.at[1, 1]).start()

    barrier = pltpu.get_barrier_semaphore()

    def greet(partner):
        pl.semaphore_signal(barrier, inc=1, device_id=partner, device_id_type=MESH)

    for partner in (sibling, across, right, left, to_up, to_down):
        greet(partner)

    @functools.partial(loop, 1, 8)
    def _(hop):
        for row in (y, up, down):
            greet(device(row, (z + hop) % 8, x, core))

    pl.semaphore_wait(barrier, 6 + 21)

    def cache_across(which, source):
        return remote(source, kv.at[1, which, 0], send_z.at[0, which], recv_kv.at[1, which], across)

    def query_over_z(j):
        to = (z + hop_of(j)) % 8
        return remote(
            query_in.at[:, group_columns(to)], query.at[j], send_z.at[j, 2], recv_q.at[j], device(y, to, x, core)
        )

    def kv_over_z(j, which):
        to = (z + hop_of(j)) % 8
        return remote(
            (key_in, value_in)[which].at[:, group_columns(to)],
            kv.at[j + 1, which, 0],
            send_z.at[j, which],
            recv_kv.at[j + 1, which],
            device(y, to, x, core),
        )

    def x_copy(i, n):
        src, dst, to = (
            lambda: (kv.at[i, :, 0], kv.at[i, :, 1], right),
            lambda: (kv.at[i, :, 0], kv.at[i, :, 3], left),
            lambda: (kv.at[i, 0, 1], kv.at[i, 0, 2], right),
            lambda: (kv.at[i, 1, 3], kv.at[i, 1, 2], left),
            lambda: (kv.at[i, :, 0:4], kv.at[i, :, 4:8], sibling),
        )[n]()
        return remote(src, dst, send_x.at[i, n], recv_x.at[i, n], to)

    def y_copy(n):
        src, dst, to = (
            lambda: (kv.at[1, :, 0:4], kv.at[9, :, 0:4], to_up),
            lambda: (kv.at[1, :, 0:4], kv.at[10, :, 0:4], to_down),
            lambda: (kv.at[9, 0, 0:4], kv.at[11, 0, 0:4], to_up),
            lambda: (kv.at[10, 1, 0:4], kv.at[11, 1, 0:4], to_down),
            lambda: (kv.at[9, :, 0:4], kv.at[9, :, 4:8], sibling),
            lambda: (kv.at[10, :, 0:4], kv.at[10, :, 4:8], sibling),
            lambda: (kv.at[11, :, 0:4], kv.at[11, :, 4:8], sibling),
            lambda: (latent, shifted, to_down),
        )[n]()
        return remote(src, dst, send_y.at[n], recv_y.at[n], to)

    def back(j):
        to = device(down, (z - hop_of(j) + 8) % 8, x, core)
        return remote(attended.at[j], returned.at[:, mine], send_o.at[j], recv_o.at[j], to)

    def start_kv(j):
        kv_over_z(j, 0).start()
        kv_over_z(j, 1).start()

    @pl.when(core != zh)
    def _():
        cache_across(0, cache_keys).start()
        cache_across(1, cache_values).start()

    loop(1, 8, lambda j: query_over_z(j).start())
    loop(1, 3, start_kv)
    y_copy(7).start()

    def prepare():
        def show(n):
            i, slot = n // 8, n % 8
            plane = jnp.where(i == 1, y, jnp.where(i == 9, down, jnp.where(i == 10, up, (y + 2) % 4)))
            side = jnp.where(slot < 4, core, 1 - core)
            block = plane * 8 + side * 4 + (x + 4 - slot % 4) % 4
            hidden = ((i == 1) | (i >= 9)) & (cache_mask[y, block] == 0)
            bias[n] = jnp.where(hidden, HIDDEN, 0.0).astype(jnp.float32)

        loop(0, CHUNKS * 8, show)

        stamp = timesteps[levels[up]].astype(jnp.float32)
        count = 128
        index = lax.broadcasted_iota(jnp.int32, (8, count), 1).astype(jnp.float32)
        phase = stamp * jnp.exp(-math.log(10000.0) * index / count)
        embed = jnp.concatenate([jnp.cos(phase), jnp.sin(phase)], axis=1).astype(jnp.bfloat16)
        weight_copy.wait()

        def gate_columns(c):
            columns = pl.ds(pl.multiple_of(c * WIDTH, 128), WIDTH)
            gate[:, columns] = jnp.dot(embed, weight[:, columns], preferred_element_type=jnp.float32)

        loop(0, 8, gate_columns)

        def clear(h):
            peak[h] = jnp.full_like(peak[h], HIDDEN)
            total[h] = jnp.zeros_like(total[h])
            summed[h] = jnp.zeros_like(summed[h])

        loop(0, GROUP, clear)

    def of_head(h):
        return pl.ds(pl.multiple_of(h * HEAD_DIM, 128), HEAD_DIM)

    def turn_query(h):
        rows = query[:, :, of_head(h)].reshape(KEYS, HEAD_DIM)
        turned[h] = rows.astype(jnp.float32).T.astype(jnp.bfloat16)

    def attend(i):
        def scores_of(h):
            keys = kv[i, 0, :, :, of_head(h)].reshape(KEYS, HEAD_DIM)
            return jnp.dot(keys, turned[h], preferred_element_type=jnp.float32)

        scale = LOG2E / math.sqrt(HEAD_DIM)

        def one_head(h, scores):
            following = scores_of(jnp.minimum(h + 1, GROUP - 1))
            scores = jnp.concatenate(
                [scores[slot * ROWS : (slot + 1) * ROWS] + bias[i * 8 + slot] for slot in range(8)], axis=0
            )
            old = peak[h]
            new = jnp.maximum(old, jnp.max(scores, axis=0, keepdims=True) * scale)
            weights = jnp.exp2(scores * scale - new)
            factor = jnp.exp2(old - new)
            values = kv[i, 1, :, :, of_head(h)].reshape(KEYS, HEAD_DIM)
            added = lax.dot_general(
                values, weights.astype(jnp.bfloat16), (((0,), (0,)), ((), ())), preferred_element_type=jnp.float32
            )
            peak[h] = new
            total[h] = factor * total[h] + jnp.sum(weights, axis=0, keepdims=True)
            summed[h] = factor * summed[h] + added
            return following

        lax.fori_loop(0, GROUP, one_head, scores_of(0))

    def turn(t, carry):
        @pl.when(t < X_CHUNKS)
        def _():
            for which in (0, 1):
                place = kv.at[t, which, 0]
                pltpu.make_async_copy(place, place, recv_kv.at[t, which]).wait()
            x_copy(t, 0).start()
            x_copy(t, 1).start()

        @pl.when((t == 1) | (t == 3))
        def _():
            start_kv(t + 2)
            start_kv(t + 3)

        @pl.when(t == 5)
        def _():
            start_kv(7)

        @pl.when((t >= 1) & (t < X_CHUNKS + 1))
        def _():
            x_copy(t - 1, 0).wait_recv()
            x_copy(t - 1, 2).start()
            x_copy(t - 1, 1).wait_recv()
            x_copy(t - 1, 3).start()

        pl.when(t == 1)(prepare)

        @pl.when((t >= 2) & (t < X_CHUNKS + 2))
        def _():
            x_copy(t - 2, 2).wait_recv()
            x_copy(t - 2, 3).wait_recv()
            x_copy(t - 2, 4).start()

        @pl.when(t == 3)
        def _():
            y_copy(0).start()
            y_copy(1).start()
            own_query.wait()
            loop(1, 8, lambda j: query_over_z(j).wait_recv())
            loop(0, GROUP, turn_query)

        @pl.when(t == 6)
        def _():
            for n in (0, 1):
                y_copy(n).wait_recv()
                y_copy(n + 2).start()
                y_copy(n + 4).start()

        @pl.when(t == 8)
        def _():
            y_copy(2).wait_recv()
            y_copy(3).wait_recv()
            y_copy(6).start()

        @pl.when(t >= 3)
        def _():
            x_copy(t - 3, 4).wait_recv()

        for n in (4, 5, 6):

            @pl.when(t == n + 4)
            def _(n=n):
                y_copy(n).wait_recv()

        def ready(e):
            attend(jnp.where(e == 0, t - 3, t + 1))

        loop(0, jnp.where(t < 3, 0, jnp.where((t >= 8) & (t <= 10), 2, 1)), ready)
        return carry

    lax.fori_loop(0, X_CHUNKS + 3, turn, 0)

    def finish(h):
        result = summed[h] * (1.0 / total[h])
        attended[:, :, of_head(h)] = result.T.astype(jnp.bfloat16).reshape(8, ROWS, HEAD_DIM)

    loop(0, GROUP, finish)
    loop(0, 8, lambda j: back(j).start())

    @pl.when(core != zh)
    def _():
        cache_across(0, cache_keys).wait_send()
        cache_across(1, cache_values).wait_send()

    @functools.partial(loop, 1, 8)
    def _(j):
        query_over_z(j).wait_send()
        kv_over_z(j, 0).wait_send()
        kv_over_z(j, 1).wait_send()

    @functools.partial(loop, 0, X_CHUNKS)
    def _(i):
        for n in range(5):
            x_copy(i, n).wait_send()

    for n in range(8):
        y_copy(n).wait_send()

    y_copy(7).wait_recv()

    @functools.partial(loop, 0, 8)
    def _(j):
        back(j).wait_recv()
        columns = group_columns((z + hop_of(j)) % 8)
        out[:, columns] = (
            shifted[:, columns].astype(jnp.float32) + gate[0:1, columns] * returned[:, columns].astype(jnp.float32)
        ).astype(jnp.bfloat16)

    loop(0, 8, lambda j: back(j).wait_send())


def shards(
    latent, query_in, key_in, value_in, cache_keys, cache_values, levels, timesteps, cache_mask, time_weight
):
    anywhere = pl.BlockSpec(memory_space=pl.ANY)
    scalars = pl.BlockSpec(memory_space=pltpu.SMEM)
    bf16, f32 = jnp.bfloat16, jnp.float32
    dma = pltpu.SemaphoreType.DMA
    return pl.pallas_call(
        kernel,
        out_shape=jax.ShapeDtypeStruct(latent.shape, latent.dtype),
        in_specs=[scalars] * 3 + [anywhere] * 7,
        out_specs=pl.BlockSpec(memory_space=pltpu.VMEM),
        scratch_shapes=[
            pltpu.VMEM((8, ROWS, WIDTH), bf16),
            pltpu.VMEM((GROUP, HEAD_DIM, KEYS), bf16),
            pltpu.VMEM((CHUNKS, 2, 8, ROWS, WIDTH), bf16),
            pltpu.VMEM((8, ROWS, WIDTH), bf16),
            pltpu.VMEM(latent.shape, bf16),
            pltpu.VMEM(latent.shape, bf16),
            pltpu.VMEM(time_weight.shape, bf16),
            pltpu.VMEM((8, latent.shape[1]), f32),
            pltpu.VMEM((GROUP, 1, KEYS), f32),
            pltpu.VMEM((GROUP, 1, KEYS), f32),
            pltpu.VMEM((GROUP, HEAD_DIM, KEYS), f32),
            pltpu.SMEM((CHUNKS * 8,), f32),
            dma((8, 3)),
            dma((X_CHUNKS, 5)),
            dma((8,)),
            dma((8,)),
            dma((8,)),
            dma((X_CHUNKS, 2)),
            dma((X_CHUNKS, 5)),
            dma((8,)),
            dma((8,)),
            dma((1,)),
        ],
        compiler_params=pltpu.CompilerParams(
            collective_id=0, has_side_effects=True, vmem_limit_bytes=64 * 1024 * 1024
        ),
        cost_estimate=pl.CostEstimate(flops=2 * 10**9, bytes_accessed=5 * 10**6, transcendentals=4 * 10**6),
    )(
        levels, timesteps, cache_mask, latent, query_in, key_in, value_in, cache_keys, cache_values, time_weight
    )


def solution(mesh):
    return jax.shard_map(
        shards,
        mesh=mesh,
        in_specs=(
            P(("chain", "head"), None),
            P(("chain", "head"), None),
            P(("chain", "head"), None),
            P(("chain", "head"), None),
            P("chain", "head"),
            P("chain", "head"),
            P(),
            P(),
            P(),
            P(),
        ),
        out_specs=P(("chain", "head"), None),
        check_vma=False,
    )
```

time: 67 us -> 71.5 us (1.067)
  the two profiles are of different devices: /device:TPU:1 before, /device:TPU:24 now
where the time goes in v5:
time: 71.5 us; the launch traced here: 71.4 us
  Pallas kernels  69.7 us (97%)
  local copies, waits for them, and re-layouts  1.72 us (2%)
    pallas_call x1, Pallas kernels, shards(): pl.pallas_call(kernel, out_shape=jax.ShapeDtypeStruct(latent.shape, laten...  69.7 us
    unnamed x1, local copies, waits for them, and re-layouts  1.72 us

profile of v5, /device:TPU:24, one launch (start us, length us, event | category | flops | bytes accessed | tf_op | source)
XLA Modules:
  0.0 71.4 jit_solution(3252082024202860662)
XLA Ops:
  0.0 69.7 %shard_map.100 = bf16[32,5120]{1,0:T(8,128)(2,1)} custom-call(s32[4]{0:T(128)} %levels.1, s32[50]{0:T(128)} %timesteps.1, s32[4,32]{1,0:T(4,128)} %cache_mask.1, bf16[32,5120]{1,0:T(8,128)(2,1)} %latent.1, bf16[32,5120]{1,0:T(8,128)(2,1)} %query_in.1, bf16[32,5120]{1,0:T(8,128)(2,1)} %key_in.1, bf16[32,5120]{1,0:T(8,128)(2,1)} %value_in.1, ...), custom_call_target="tpu_custom_call" | custom-call | flops 2000000000 | bytes 5000000 | tf_op jit(solution)/shard_map/pallas_call | solution.py:337
  69.7 1.7 %copy.12 = bf16[32,5120]{1,0:T(8,128)(2,1)} copy(bf16[32,5120]{1,0:T(8,128)(2,1)} %shard_map.100) | data formatting | bytes 655360

commit v6 on v4

--- a/solution.py
+++ b/solution.py
@@ -16,6 +16,7 @@
 WIDTH = GROUP * HEAD_DIM
 ROWS = 32
 HOPS = (0, 1, 7, 2, 6, 3, 5, 4)
+ITEMS = (0, 2, 3, 5, 6, 7, 8, 4)
 CHUNKS = 12
 FIRST_Z = 2
 X_CHUNKS = 9
@@ -28,16 +29,19 @@
     return {"chain": (y * 2 + z // 4) * NX + x, "head": (z % 4) * 2 + core}
 
 
+def first_column(z):
+    return ((z % 4) * 2 + z // 4) * WIDTH
+
+
 def group_columns(z):
-    group = (z % 4) * 2 + z // 4
-    return pl.ds(pl.multiple_of(group * WIDTH, 128), WIDTH)
+    return pl.ds(pl.multiple_of(first_column(z), 128), WIDTH)
 
 
 def kernel(
     levels, timesteps, cache_mask, latent, query_in, key_in, value_in, cache_keys, cache_values, time_weight,
     out,
-    query, turned, kv, attended, returned, shifted, weight, gate, peak, total, summed, bias,
-    send_z, send_x, send_y, send_o, recv_q, recv_k, recv_v, recv_x, recv_y, recv_o, local,
+    query, turned, kv, relay, relay_o, attended, returned, shifted, weight, gate, peak, total, summed, bias,
+    send_z, send_x, send_y, send_o, recv_q, recv_k, recv_v, recv_relay, recv_x, recv_y, recv_o, local,
 ):
     chain, head = lax.axis_index("chain"), lax.axis_index("head")
     y, x = chain // 8, chain % 4
@@ -47,6 +51,7 @@
     right, left = (x + 1) % 4, (x + 3) % 4
     sibling = device(y, z, x, 1 - core)
     across = device(y, (z + 4) % 8, x, 1 - core)
+    back_two = device(y, (z + 6) % 8, x, core)
 
     def remote(src, dst, send, recv, to):
         return pltpu.make_async_remote_copy(
@@ -89,13 +94,15 @@
 
     def kv_over_z(j, which, source, recv):
         to = (z + HOPS[j]) % 8
+        source = source.at[:, group_columns(to)]
+        if HOPS[j] == 4:
+            return remote(source, relay.at[which], send_z.at[j, which], recv_relay.at[which], back_two)
         return remote(
-            source.at[:, group_columns(to)],
-            kv.at[j + 1, which, 0],
-            send_z.at[j, which],
-            recv.at[j + 1],
-            device(y, to, x, core),
+            source, kv.at[ITEMS[j], which, 0], send_z.at[j, which], recv.at[ITEMS[j]], device(y, to, x, core)
         )
+
+    def relay_on(which, recv):
+        return remote(relay.at[which], kv.at[ITEMS[7], which, 0], send_z.at[8, which], recv.at[ITEMS[7]], back_two)
 
     def over_x(i):
         own_kv = kv.at[i, :, 0]
@@ -123,9 +130,22 @@
     def sibling_y(i):
         return to_sibling(i, send_y.at[i - 5], recv_y.at[i - 5])
 
+    cut = 3 * HEAD_DIM
+    lower = pl.ds(pl.multiple_of(first_column(z), 128), cut)
+
+    def upper(z):
+        return pl.ds(pl.multiple_of(first_column(z) + cut, 128), WIDTH - cut)
+
     def back(j):
-        to = (z - HOPS[j] + 8) % 8
-        return remote(attended.at[j], returned.at[:, mine], send_o.at[j], recv_o.at[j], device(down, to, x, core))
+        to = device(down, (z - HOPS[j] + 8) % 8, x, core)
+        if HOPS[j] == 4:
+            return remote(attended.at[j, :, 0:cut], returned.at[:, lower], send_o.at[j], recv_o.at[j], to)
+        return remote(attended.at[j], returned.at[:, mine], send_o.at[j], recv_o.at[j], to)
+
+    back_relay = remote(
+        attended.at[7, :, cut:WIDTH], relay_o, send_o.at[8], recv_o.at[8], device(down, (z + 6) % 8, x, core)
+    )
+    back_last = remote(relay_o, returned.at[:, upper((z + 2) % 8)], send_o.at[9], recv_o.at[9], back_two)
 
     @pl.when(core != zh)
     def _():
@@ -140,6 +160,7 @@
         query_over_z(j).start()
     start_kv(1)
     start_kv(2)
+    start_kv(7)
     latent_down.start()
 
     for i in range(CHUNKS):
@@ -205,7 +226,7 @@
             over_x(t)[0].start()
             over_x(t)[1].start()
 
-        for turn_of, hops in ((1, (3, 4)), (3, (5, 6)), (5, (7,))):
+        for turn_of, hops in ((1, (3, 4)), (3, (5, 6))):
 
             @pl.when(t == turn_of)
             def _(hops=hops):
@@ -229,6 +250,9 @@
 
         @pl.when(t == 3)
         def _():
+            for which, source, recv in ((0, key_in, recv_k), (1, value_in, recv_v)):
+                kv_over_z(7, which, source, recv).wait_recv()
+                relay_on(which, recv).start()
             y_up.start()
             y_down.start()
             own[2].wait()
@@ -284,6 +308,7 @@
     for h in range(GROUP):
         result = summed[h] * (1.0 / total[h])
         attended[:, :, h * HEAD_DIM : (h + 1) * HEAD_DIM] = result.T.astype(jnp.bfloat16).reshape(8, ROWS, HEAD_DIM)
+    back_relay.start()
     for j in range(8):
         back(j).start()
 
@@ -292,6 +317,8 @@
         cache_across(0, cache_keys, recv_k).wait_send()
         cache_across(1, cache_values, recv_v).wait_send()
 
+    relay_on(0, recv_k).wait_send()
+    relay_on(1, recv_v).wait_send()
     for j in range(1, 8):
         query_over_z(j).wait_send()
         kv_over_z(j, 0, key_in, recv_k).wait_send()
@@ -308,14 +335,20 @@
         copy.wait_send()
 
     latent_down.wait_recv()
+    back_relay.wait_recv()
+    back_last.start()
     for j in range(8):
         back(j).wait_recv()
+        if j == 7:
+            back_last.wait_recv()
         columns = group_columns((z + HOPS[j]) % 8)
         out[:, columns] = (
             shifted[:, columns].astype(jnp.float32) + gate[0:1, columns] * returned[:, columns].astype(jnp.float32)
         ).astype(jnp.bfloat16)
     for j in range(8):
         back(j).wait_send()
+    back_relay.wait_send()
+    back_last.wait_send()
 
 
 def shards(
@@ -334,6 +367,8 @@
             pltpu.VMEM((8, ROWS, WIDTH), bf16),
             pltpu.VMEM((GROUP, HEAD_DIM, KEYS), bf16),
             pltpu.VMEM((CHUNKS, 2, 8, ROWS, WIDTH), bf16),
+            pltpu.VMEM((2, ROWS, WIDTH), bf16),
+            pltpu.VMEM((ROWS, 2 * HEAD_DIM), bf16),
             pltpu.VMEM((8, ROWS, WIDTH), bf16),
             pltpu.VMEM(latent.shape, bf16),
             pltpu.VMEM(latent.shape, bf16),
@@ -343,16 +378,17 @@
             pltpu.VMEM((GROUP, 1, KEYS), f32),
             pltpu.VMEM((GROUP, HEAD_DIM, KEYS), f32),
             pltpu.SMEM((CHUNKS * 8,), f32),
-            dma((8, 3)),
+            dma((9, 3)),
             dma((X_CHUNKS, 5)),
             dma((8,)),
-            dma((8,)),
+            dma((10,)),
             dma((8,)),
             dma((X_CHUNKS,)),
             dma((X_CHUNKS,)),
+            dma((2,)),
             dma((X_CHUNKS, 5)),
             dma((8,)),
-            dma((8,)),
+            dma((10,)),
             dma((1,)),
         ],
         compiler_params=pltpu.CompilerParams(

time: 67 us -> 75.5 us (1.13); the launches traced: 65.8 us -> 75.4 us
  Pallas kernels: 64.1 us -> 73.6 us
    pallas_call x1, Pallas kernels: 64.1 us -> 73.6 us  [shards(): pl.pallas_call(kernel, out_shape=jax.ShapeDtypeStruct(latent.shape, laten...]
where the time goes in v6:
time: 75.5 us; the launch traced here: 75.4 us
  Pallas kernels  73.6 us (97%)
  local copies, waits for them, and re-layouts  1.72 us (2%)
    pallas_call x1, Pallas kernels, shards(): pl.pallas_call(kernel, out_shape=jax.ShapeDtypeStruct(latent.shape, laten...  73.6 us
    unnamed x1, local copies, waits for them, and re-layouts  1.72 us

profile of v6, /device:TPU:1, one launch (start us, length us, event | category | flops | bytes accessed | tf_op | source)
XLA Modules:
  0.0 75.4 jit_solution(696212200708976007)
XLA Ops:
  0.0 73.6 %shard_map.100 = bf16[32,5120]{1,0:T(8,128)(2,1)} custom-call(s32[4]{0:T(128)} %levels.1, s32[50]{0:T(128)} %timesteps.1, s32[4,32]{1,0:T(4,128)} %cache_mask.1, bf16[32,5120]{1,0:T(8,128)(2,1)} %latent.1, bf16[32,5120]{1,0:T(8,128)(2,1)} %query_in.1, bf16[32,5120]{1,0:T(8,128)(2,1)} %key_in.1, bf16[32,5120]{1,0:T(8,128)(2,1)} %value_in.1, ...), custom_call_target="tpu_custom_call" | custom-call | flops 2000000000 | bytes 5000000 | tf_op jit(solution)/shard_map/pallas_call | solution.py:361
  73.6 1.7 %copy.12 = bf16[32,5120]{1,0:T(8,128)(2,1)} copy(bf16[32,5120]{1,0:T(8,128)(2,1)} %shard_map.100) | data formatting | bytes 655360

commit v7 on v3

--- a/solution.py
+++ b/solution.py
@@ -17,7 +17,7 @@
 ROWS = 32
 HOPS = (0, 1, 7, 2, 6, 3, 5, 4)
 CHUNKS = 12
-ATTEND = (0, 1, 2, 3, 9, 10, 8, 4, 5, 11, 6, 7)
+ATTEND = (0, 1, 2, 3, 9, 10, 4, 5, 11, 6, 7, 8)
 PLACE = tuple(ATTEND.index(i) for i in range(CHUNKS))
 X_CHUNKS = 9
 PARTS = ((0, 3), (3, 5))
@@ -44,8 +44,8 @@
 def kernel(
     levels, timesteps, cache_mask, latent, query_in, key_in, value_in, cache_keys, cache_values, time_weight,
     out,
-    query, kv, relay, attended, returned, shifted, weight, gate, peak, total, summed, bias,
-    send_z, send_x, send_y, send_o, recv_q, recv_kv, recv_relay, recv_x, recv_y, recv_o, local,
+    query, turned, kv, attended, returned, shifted, weight, gate, peak, total, summed, bias,
+    send_z, send_x, send_y, send_o, recv_q, recv_kv, recv_x, recv_y, recv_o, local,
 ):
     chain, head = lax.axis_index("chain"), lax.axis_index("head")
     y, x = chain // 8, chain % 4
@@ -55,7 +55,6 @@
     right, left = device(y, z, (x + 1) % 4, core), device(y, z, (x + 3) % 4, core)
     sibling = device(y, z, x, 1 - core)
     across = device(y, (z + 4) % 8, x, 1 - core)
-    back_two = device(y, (z + 6) % 8, x, core)
     to_up, to_down = device(up, z, x, core), device(down, z, x, core)
     mine = group_columns(z)
 
@@ -100,14 +99,9 @@
     def kv_over_z(j, which):
         to = (z + HOPS[j]) % 8
         source = (key_in, value_in)[which].at[:, group_columns(to)]
-        if HOPS[j] == 4:
-            return remote(source, relay.at[which], send_z.at[j, which], recv_relay.at[which], back_two)
         return remote(
             source, chunk(j + 1).at[which, 0], send_z.at[j, which], recv_kv.at[j + 1, which], device(y, to, x, core)
         )
-
-    def relay_on(which):
-        return remote(relay.at[which], chunk(8).at[which, 0], send_z.at[8, which], recv_kv.at[8, which], back_two)
 
     def x_copy(i, n):
         c = chunk(i)
@@ -116,10 +110,7 @@
             (c.at[:, 0], c.at[:, 3], left),
             (c.at[0, 1], c.at[0, 2], right),
             (c.at[1, 3], c.at[1, 2], left),
-            (c.at[:, 0], c.at[:, 4], sibling),
-            (c.at[:, 1], c.at[:, 5], sibling),
-            (c.at[:, 2], c.at[:, 6], sibling),
-            (c.at[:, 3], c.at[:, 7], sibling),
+            (c.at[:, 0:4], c.at[:, 4:8], sibling),
         )[n]
         return remote(src, dst, send_x.at[i, n], recv_x.at[i, n], to)
 
@@ -153,7 +144,7 @@
         for which in (0, 1):
             place = chunk(i).at[which, 0]
             pltpu.make_async_copy(place, place, recv_kv.at[i, which]).wait()
-        for n in (0, 1, 4):
+        for n in (0, 1):
             x_copy(i, n).start()
 
     def forward(i):
@@ -161,20 +152,17 @@
         x_copy(i, 2).start()
         x_copy(i, 1).wait_recv()
         x_copy(i, 3).start()
-        x_copy(i, 5).start()
-        x_copy(i, 7).start()
 
     def last_piece(i):
         x_copy(i, 2).wait_recv()
         x_copy(i, 3).wait_recv()
-        x_copy(i, 6).start()
+        x_copy(i, 4).start()
 
     def complete(i):
         if i >= X_CHUNKS:
             y_copy(i - 5).wait_recv()
         else:
-            for n in (4, 5, 6, 7):
-                x_copy(i, n).wait_recv()
+            x_copy(i, 4).wait_recv()
 
     def start_y():
         y_copy(0).start()
@@ -191,11 +179,6 @@
         y_copy(3).wait_recv()
         y_copy(6).start()
 
-    def relay_all():
-        for which in (0, 1):
-            kv_over_z(7, which).wait_recv()
-            relay_on(which).start()
-
     def queries(*js):
         for j in js:
             query_over_z(j).wait_recv()
@@ -205,7 +188,9 @@
         cache_across(0).start()
         cache_across(1).start()
 
-    start_z(1, 2, 7)
+    start_z(1, 2)
+    arrived(0)
+    arrived(2)
     for j in range(1, 8):
         query_over_z(j).start()
     y_copy(7).start()
@@ -224,7 +209,8 @@
     total[...] = jnp.zeros_like(total)
     summed[...] = jnp.zeros_like(summed)
 
-    arrived(0)
+    arrived(1)
+    arrived(3)
 
     stamp = timesteps[levels[up]].astype(jnp.float32)
     count = 128
@@ -240,25 +226,30 @@
 
     lax.fori_loop(0, 8, gate_columns, 0)
 
-    def attend(c, finish=None):
+    def attend(c, cached, finish=None):
+        def scores_of(h):
+            keys = kv[c, 0, :, :, h * HEAD_DIM : (h + 1) * HEAD_DIM].reshape(KEYS, HEAD_DIM)
+            return jnp.dot(keys, turned[h], preferred_element_type=jnp.float32)
+
+        scale = LOG2E / math.sqrt(HEAD_DIM)
+        following = scores_of(0)
         for h in range(GROUP):
-            columns = slice(h * HEAD_DIM, (h + 1) * HEAD_DIM)
-            keys = kv[c, 0, :, :, columns].reshape(KEYS, HEAD_DIM)
-            values = kv[c, 1, :, :, columns].reshape(KEYS, HEAD_DIM)
-            queries = query[:, :, columns].reshape(KEYS, HEAD_DIM)
-            scores = lax.dot_general(keys, queries, (((1,), (1,)), ((), ())), preferred_element_type=jnp.float32)
-            scores = scores * (LOG2E / math.sqrt(HEAD_DIM))
-            scores = jnp.concatenate(
-                [scores[slot * ROWS : (slot + 1) * ROWS] + bias[c * 8 + slot] for slot in range(8)], axis=0
-            )
+            scores = following
+            if h + 1 < GROUP:
+                following = scores_of(h + 1)
+            if cached:
+                scores = jnp.concatenate(
+                    [scores[slot * ROWS : (slot + 1) * ROWS] + bias[c * 8 + slot] for slot in range(8)], axis=0
+                )
             old = peak[h]
-            new = jnp.maximum(old, jnp.max(scores, axis=0, keepdims=True))
-            weights = jnp.exp2(scores - new)
+            new = jnp.maximum(old, jnp.max(scores, axis=0, keepdims=True) * scale)
+            weights = jnp.exp2(scores * scale - new)
             factor = jnp.exp2(old - new)
-            weight_sum = factor * total[h] + jnp.sum(weights, axis=0, keepdims=True)
+            values = kv[c, 1, :, :, h * HEAD_DIM : (h + 1) * HEAD_DIM].reshape(KEYS, HEAD_DIM)
             added = lax.dot_general(
                 values, weights.astype(jnp.bfloat16), (((0,), (0,)), ((), ())), preferred_element_type=jnp.float32
             )
+            weight_sum = factor * total[h] + jnp.sum(weights, axis=0, keepdims=True)
             value_sum = factor * summed[h] + added
             if finish is None:
                 peak[h], total[h], summed[h] = new, weight_sum, value_sum
@@ -275,59 +266,81 @@
 
     def before(c):
         if c == 0:
-            arrived(1)
             forward(0)
-            arrived(2)
-            arrived(3)
             last_piece(0)
             forward(1)
             forward(2)
             last_piece(1)
             start_y()
-            forward(3)
-            last_piece(2)
-            last_piece(3)
-            relay_all()
             own_query.wait()
             queries(1, 2, 3, 4)
             start_z(3, 4)
+            forward(3)
+            last_piece(2)
             queries(5, 6, 7)
+            for h in range(GROUP):
+                columns = slice(h * HEAD_DIM, (h + 1) * HEAD_DIM)
+                turned[h] = query[:, :, columns].reshape(KEYS, HEAD_DIM).astype(jnp.float32).T.astype(jnp.bfloat16)
+        if c == 1:
+            last_piece(3)
         if c == 3:
-            arrived(8)
-        if c == 4:
             arrived(4)
             start_z(5, 6)
             arrived(5)
-            forward(8)
+        if c == 4:
+            forward(4)
             forward_y()
         if c == 5:
-            last_piece(8)
-            forward(4)
             forward(5)
+            last_piece(4)
+            start_z(7)
         if c == 6:
-            last_piece(4)
             last_piece(5)
-        if c == 8:
+        if c == 7:
             arrived(6)
             arrived(7)
+        if c == 8:
+            forward(6)
+            last_y()
         if c == 9:
-            forward(6)
             forward(7)
-            last_y()
+            last_piece(6)
+            arrived(8)
         if c == 10:
-            last_piece(6)
             last_piece(7)
+            forward(8)
+        if c == 11:
+            last_piece(8)
         complete(ATTEND[c])
 
     def turn(c, carry):
+        cached = False
         for now in range(CHUNKS - 1):
             pl.when(c == now)(functools.partial(before, now))
-        attend(c)
+            if ATTEND[now] == 1 or ATTEND[now] >= X_CHUNKS:
+                cached = cached | (c == now)
+        pl.when(cached)(functools.partial(attend, c, True))
+        pl.when(jnp.logical_not(cached))(functools.partial(attend, c, False))
         return carry
 
     lax.fori_loop(0, CHUNKS - 1, turn, 0)
     before(CHUNKS - 1)
-    attend(CHUNKS - 1, finish)
+    attend(CHUNKS - 1, False, finish)
+
+    @pl.when(core != zh)
+    def _():
+        cache_across(0).wait_send()
+        cache_across(1).wait_send()
+
+    for j in range(1, 8):
+        query_over_z(j).wait_send()
+        for which in (0, 1):
+            kv_over_z(j, which).wait_send()
+    for i in range(X_CHUNKS):
+        for n in range(5):
+            x_copy(i, n).wait_send()
+    for n in range(8):
+        y_copy(n).wait_send()
 
     y_copy(7).wait_recv()
     for part in range(len(PARTS)):
@@ -337,23 +350,6 @@
             out[:, columns] = (
                 shifted[:, columns].astype(jnp.float32) + gate[0:1, columns] * returned[:, columns].astype(jnp.float32)
             ).astype(jnp.bfloat16)
-
-    @pl.when(core != zh)
-    def _():
-        cache_across(0).wait_send()
-        cache_across(1).wait_send()
-
-    for which in (0, 1):
-        relay_on(which).wait_send()
-    for j in range(1, 8):
-        query_over_z(j).wait_send()
-        for which in (0, 1):
-            kv_over_z(j, which).wait_send()
-    for i in range(X_CHUNKS):
-        for n in range(8):
-            x_copy(i, n).wait_send()
-    for n in range(8):
-        y_copy(n).wait_send()
     for part in range(len(PARTS)):
         for j in range(8):
             back(j, part).wait_send()
@@ -373,8 +369,8 @@
         out_specs=pl.BlockSpec(memory_space=pltpu.VMEM),
         scratch_shapes=[
             pltpu.VMEM((8, ROWS, WIDTH), bf16),
+            pltpu.VMEM((GROUP, HEAD_DIM, KEYS), bf16),
             pltpu.VMEM((CHUNKS, 2, 8, ROWS, WIDTH), bf16),
-            pltpu.VMEM((2, ROWS, WIDTH), bf16),
             pltpu.VMEM((8, ROWS, WIDTH), bf16),
             pltpu.VMEM(latent.shape, bf16),
             pltpu.VMEM(latent.shape, bf16),
@@ -384,14 +380,13 @@
             pltpu.VMEM((GROUP, 1, KEYS), f32),
             pltpu.VMEM((GROUP, HEAD_DIM, KEYS), f32),
             pltpu.SMEM((CHUNKS * 8,), f32),
-            dma((9, 3)),
-            dma((X_CHUNKS, 8)),
+            dma((8, 3)),
+            dma((X_CHUNKS, 5)),
             dma((8,)),
             dma((8, len(PARTS))),
             dma((8,)),
             dma((X_CHUNKS, 2)),
-            dma((2,)),
-            dma((X_CHUNKS, 8)),
+            dma((X_CHUNKS, 5)),
             dma((8,)),
             dma((8, len(PARTS))),
             dma((1,)),

time: 78.3 us -> 76.4 us (0.976)
  Pallas kernels: 76 us -> 73.8 us
    pallas_call x1, Pallas kernels: 76 us -> 73.8 us  [shards(): pl.pallas_call(kernel, out_shape=jax.ShapeDtypeStruct(latent.shape, laten...]
where the time goes in v7:
time: 76.4 us; the launch traced here: 75.5 us
  Pallas kernels  73.8 us (97%)
  local copies, waits for them, and re-layouts  1.72 us (2%)
    pallas_call x1, Pallas kernels, shards(): pl.pallas_call(kernel, out_shape=jax.ShapeDtypeStruct(latent.shape, laten...  73.8 us
    unnamed x1, local copies, waits for them, and re-layouts  1.72 us

profile of v7, /device:TPU:1, one launch (start us, length us, event | category | flops | bytes accessed | tf_op | source)
XLA Modules:
  0.0 75.5 jit_solution(14149132228718767317)
XLA Ops:
  0.0 73.8 %shard_map.100 = bf16[32,5120]{1,0:T(8,128)(2,1)} custom-call(s32[4]{0:T(128)} %levels.1, s32[50]{0:T(128)} %timesteps.1, s32[4,32]{1,0:T(4,128)} %cache_mask.1, bf16[32,5120]{1,0:T(8,128)(2,1)} %latent.1, bf16[32,5120]{1,0:T(8,128)(2,1)} %query_in.1, bf16[32,5120]{1,0:T(8,128)(2,1)} %key_in.1, bf16[32,5120]{1,0:T(8,128)(2,1)} %value_in.1, ...), custom_call_target="tpu_custom_call" | custom-call | flops 2000000000 | bytes 5000000 | tf_op jit(solution)/shard_map/pallas_call | solution.py:365
  73.8 1.7 %copy.12 = bf16[32,5120]{1,0:T(8,128)(2,1)} copy(bf16[32,5120]{1,0:T(8,128)(2,1)} %shard_map.100) | data formatting | bytes 655360

commit v8 on v4

--- a/solution.py
+++ b/solution.py
@@ -20,7 +20,6 @@
 FIRST_Z = 2
 X_CHUNKS = 9
 KEYS = 8 * ROWS
-LOG2E = 1.4426950408889634
 HIDDEN = -1e30
 
 
@@ -36,7 +35,7 @@
 def kernel(
     levels, timesteps, cache_mask, latent, query_in, key_in, value_in, cache_keys, cache_values, time_weight,
     out,
-    query, turned, kv, attended, returned, shifted, weight, gate, peak, total, summed, bias,
+    query, turned, kv, attended, returned, shifted, weight, gate, scored, weighed, factor, peak, total, summed, bias,
     send_z, send_x, send_y, send_o, recv_q, recv_k, recv_v, recv_x, recv_y, recv_o, local,
 ):
     chain, head = lax.axis_index("chain"), lax.axis_index("head")
@@ -171,31 +170,32 @@
     summed[...] = jnp.zeros_like(summed)
 
     def attend(i, cached):
-        def scores_of(h):
-            keys = kv[i, 0, :, :, h * HEAD_DIM : (h + 1) * HEAD_DIM].reshape(KEYS, HEAD_DIM)
-            return jnp.dot(keys, turned[h], preferred_element_type=jnp.float32)
-
-        scale = LOG2E / math.sqrt(HEAD_DIM)
-        following = scores_of(0)
+        def of_head(which, h):
+            return kv[i, which, :, :, h * HEAD_DIM : (h + 1) * HEAD_DIM].reshape(KEYS, HEAD_DIM)
+
+        scale = 1.0 / math.sqrt(HEAD_DIM)
         for h in range(GROUP):
-            scores = following
-            if h + 1 < GROUP:
-                following = scores_of(h + 1)
-            if cached:
-                scores = jnp.concatenate(
-                    [scores[slot * ROWS : (slot + 1) * ROWS] + bias[i * 8 + slot] for slot in range(8)], axis=0
-                )
-            old = peak[h]
-            new = jnp.maximum(old, jnp.max(scores, axis=0, keepdims=True) * scale)
-            weights = jnp.exp2(scores * scale - new)
-            factor = jnp.exp2(old - new)
-            values = kv[i, 1, :, :, h * HEAD_DIM : (h + 1) * HEAD_DIM].reshape(KEYS, HEAD_DIM)
+            scored[h] = jnp.dot(of_head(0, h), turned[h], preferred_element_type=jnp.float32)
+        for h in range(GROUP):
+            for side in (slice(0, 128), slice(128, 256)):
+                scores = scored[h, :, side]
+                if cached:
+                    scores = jnp.concatenate(
+                        [scores[slot * ROWS : (slot + 1) * ROWS] + bias[i * 8 + slot] for slot in range(8)], axis=0
+                    )
+                old = peak[h, :, side]
+                new = jnp.maximum(old, jnp.max(scores, axis=0, keepdims=True) * scale)
+                weights = jnp.exp(scores * scale - new)
+                shrink = jnp.exp(old - new)
+                peak[h, :, side] = new
+                factor[h, :, side] = shrink
+                total[h, :, side] = shrink * total[h, :, side] + jnp.sum(weights, axis=0, keepdims=True)
+                weighed[h, :, side] = weights.astype(jnp.bfloat16)
+        for h in range(GROUP):
             added = lax.dot_general(
-                values, weights.astype(jnp.bfloat16), (((0,), (0,)), ((), ())), preferred_element_type=jnp.float32
+                of_head(1, h), weighed[h], (((0,), (0,)), ((), ())), preferred_element_type=jnp.float32
             )
-            peak[h] = new
-            total[h] = factor * total[h] + jnp.sum(weights, axis=0, keepdims=True)
-            summed[h] = factor * summed[h] + added
+            summed[h] = factor[h] * summed[h] + added
 
     def turn(t, carry):
         @pl.when(t < X_CHUNKS)
@@ -339,6 +339,9 @@
             pltpu.VMEM(latent.shape, bf16),
             pltpu.VMEM(time_weight.shape, bf16),
             pltpu.VMEM((8, latent.shape[1]), f32),
+            pltpu.VMEM((GROUP, KEYS, KEYS), f32),
+            pltpu.VMEM((GROUP, KEYS, KEYS), bf16),
+            pltpu.VMEM((GROUP, 1, KEYS), f32),
             pltpu.VMEM((GROUP, 1, KEYS), f32),
             pltpu.VMEM((GROUP, 1, KEYS), f32),
             pltpu.VMEM((GROUP, HEAD_DIM, KEYS), f32),

time: 67 us -> 66.7 us (level)
  no operation moved by 1% of the time
where the time goes in v8:
time: 66.7 us; the launch traced here: 65.7 us
  Pallas kernels  64 us (96%)
  local copies, waits for them, and re-layouts  1.72 us (3%)
    pallas_call x1, Pallas kernels, shards(): pl.pallas_call(kernel, out_shape=jax.ShapeDtypeStruct(latent.shape, laten...  64 us
    unnamed x1, local copies, waits for them, and re-layouts  1.72 us

profile of v8, /device:TPU:1, one launch (start us, length us, event | category | flops | bytes accessed | tf_op | source)
XLA Modules:
  0.0 65.7 jit_solution(5848885652543136114)
XLA Ops:
  0.0 64.0 %shard_map.100 = bf16[32,5120]{1,0:T(8,128)(2,1)} custom-call(s32[4]{0:T(128)} %levels.1, s32[50]{0:T(128)} %timesteps.1, s32[4,32]{1,0:T(4,128)} %cache_mask.1, bf16[32,5120]{1,0:T(8,128)(2,1)} %latent.1, bf16[32,5120]{1,0:T(8,128)(2,1)} %query_in.1, bf16[32,5120]{1,0:T(8,128)(2,1)} %key_in.1, bf16[32,5120]{1,0:T(8,128)(2,1)} %value_in.1, ...), custom_call_target="tpu_custom_call" | custom-call | flops 2000000000 | bytes 5000000 | tf_op jit(solution)/shard_map/pallas_call | solution.py:328
  64.0 1.7 %copy.12 = bf16[32,5120]{1,0:T(8,128)(2,1)} copy(bf16[32,5120]{1,0:T(8,128)(2,1)} %shard_map.100) | data formatting | bytes 655360

commit v9 on v8

--- a/solution.py
+++ b/solution.py
@@ -137,37 +137,38 @@
 
     for j in range(1, 8):
         query_over_z(j).start()
-    start_kv(1)
-    start_kv(2)
+    for j in range(1, 5):
+        start_kv(j)
     latent_down.start()
 
-    for i in range(CHUNKS):
-        for slot in range(8):
-            if i == 1 or i >= 9:
-                plane = {1: y, 9: down, 10: up, 11: (y + 2) % 4}[i]
-                side = core if slot < 4 else 1 - core
-                block = plane * 8 + side * 4 + (x + (0, 3, 2, 1)[slot % 4]) % 4
-                bias[i * 8 + slot] = jnp.where(cache_mask[y, block] == 1, 0.0, HIDDEN).astype(jnp.float32)
-            else:
-                bias[i * 8 + slot] = jnp.float32(0.0)
-
-    stamp = timesteps[levels[up]].astype(jnp.float32)
-    count = 128
-    index = lax.broadcasted_iota(jnp.int32, (8, count), 1).astype(jnp.float32)
-    phase = stamp * jnp.exp(-math.log(10000.0) * index / count)
-    embed = jnp.concatenate([jnp.cos(phase), jnp.sin(phase)], axis=1).astype(jnp.bfloat16)
-    weight_copy.wait()
-
-    def gate_columns(c, carry):
-        columns = pl.ds(pl.multiple_of(c * WIDTH, 128), WIDTH)
-        gate[:, columns] = jnp.dot(embed, weight[:, columns], preferred_element_type=jnp.float32)
-        return carry
-
-    lax.fori_loop(0, 8, gate_columns, 0)
-
-    peak[...] = jnp.full_like(peak, HIDDEN)
-    total[...] = jnp.zeros_like(total)
-    summed[...] = jnp.zeros_like(summed)
+    def prepare():
+        for i in range(CHUNKS):
+            for slot in range(8):
+                if i == 1 or i >= 9:
+                    plane = {1: y, 9: down, 10: up, 11: (y + 2) % 4}[i]
+                    side = core if slot < 4 else 1 - core
+                    block = plane * 8 + side * 4 + (x + (0, 3, 2, 1)[slot % 4]) % 4
+                    bias[i * 8 + slot] = jnp.where(cache_mask[y, block] == 1, 0.0, HIDDEN).astype(jnp.float32)
+                else:
+                    bias[i * 8 + slot] = jnp.float32(0.0)
+
+        stamp = timesteps[levels[up]].astype(jnp.float32)
+        count = 128
+        index = lax.broadcasted_iota(jnp.int32, (8, count), 1).astype(jnp.float32)
+        phase = stamp * jnp.exp(-math.log(10000.0) * index / count)
+        embed = jnp.concatenate([jnp.cos(phase), jnp.sin(phase)], axis=1).astype(jnp.bfloat16)
+        weight_copy.wait()
+
+        def gate_columns(c, carry):
+            columns = pl.ds(pl.multiple_of(c * WIDTH, 128), WIDTH)
+            gate[:, columns] = jnp.dot(embed, weight[:, columns], preferred_element_type=jnp.float32)
+            return carry
+
+        lax.fori_loop(0, 8, gate_columns, 0)
+
+        peak[...] = jnp.full_like(peak, HIDDEN)
+        total[...] = jnp.zeros_like(total)
+        summed[...] = jnp.zeros_like(summed)
 
     def attend(i, cached):
         def of_head(which, h):
@@ -198,36 +199,22 @@
             summed[h] = factor[h] * summed[h] + added
 
     def turn(t, carry):
-        @pl.when(t < X_CHUNKS)
-        def _():
-            pltpu.make_async_copy(kv.at[t, 0, 0], kv.at[t, 0, 0], recv_k.at[t]).wait()
-            pltpu.make_async_copy(kv.at[t, 1, 0], kv.at[t, 1, 0], recv_v.at[t]).wait()
-            over_x(t)[0].start()
-            over_x(t)[1].start()
-
-        for turn_of, hops in ((1, (3, 4)), (3, (5, 6)), (5, (7,))):
-
-            @pl.when(t == turn_of)
-            def _(hops=hops):
-                for j in hops:
-                    start_kv(j)
-
-        @pl.when((t >= 1) & (t < X_CHUNKS + 1))
-        def _():
-            copies = over_x(t - 1)
+        @pl.when((t >= 2) & (t < X_CHUNKS + 2))
+        def _():
+            copies = over_x(t - 2)
             copies[0].wait_recv()
             copies[2].start()
             copies[1].wait_recv()
             copies[3].start()
 
-        @pl.when((t >= 2) & (t < X_CHUNKS + 2))
-        def _():
-            copies = over_x(t - 2)
+        @pl.when((t >= 3) & (t < X_CHUNKS + 3))
+        def _():
+            copies = over_x(t - 3)
             copies[2].wait_recv()
             copies[3].wait_recv()
-            sibling_x(t - 2).start()
-
-        @pl.when(t == 3)
+            sibling_x(t - 3).start()
+
+        @pl.when(t == 4)
         def _():
             y_up.start()
             y_down.start()
@@ -238,7 +225,7 @@
                 columns = slice(h * HEAD_DIM, (h + 1) * HEAD_DIM)
                 turned[h] = query[:, :, columns].reshape(KEYS, HEAD_DIM).astype(jnp.float32).T.astype(jnp.bfloat16)
 
-        @pl.when(t == 6)
+        @pl.when(t == 7)
         def _():
             y_up.wait_recv()
             y_on_up.start()
@@ -247,39 +234,48 @@
             sibling_y(9).start()
             sibling_y(10).start()
 
-        @pl.when(t == 8)
+        @pl.when(t == 9)
         def _():
             y_on_up.wait_recv()
             y_on_down.wait_recv()
             sibling_y(11).start()
 
-        @pl.when(t >= 3)
-        def _():
-            sibling_x(t - 3).wait_recv()
-
-        @pl.when(t == 8)
-        def _():
-            sibling_y(9).wait_recv()
-
-        @pl.when(t == 9)
-        def _():
-            sibling_y(10).wait_recv()
-
-        @pl.when(t == 10)
-        def _():
-            sibling_y(11).wait_recv()
-
-        @pl.when((t >= 3) & (t != 4))
-        def _():
-            attend(t - 3, False)
-
-        @pl.when((t == 4) | ((t >= 8) & (t <= 10)))
-        def _():
-            attend(jnp.where(t == 4, 1, t + 1), True)
-
+        @pl.when(t >= 4)
+        def _():
+            sibling_x(t - 4).wait_recv()
+
+        @pl.when((t >= 4) & (t != 5))
+        def _():
+            attend(t - 4, False)
+
+        for i in (9, 10, 11):
+
+            @pl.when(t == i)
+            def _(i=i):
+                sibling_y(i).wait_recv()
+
+        @pl.when((t == 5) | ((t >= 9) & (t <= 11)))
+        def _():
+            attend(jnp.where(t == 5, 1, t), True)
+
+        @pl.when(t < X_CHUNKS)
+        def _():
+            pltpu.make_async_copy(kv.at[t, 0, 0], kv.at[t, 0, 0], recv_k.at[t]).wait()
+            pltpu.make_async_copy(kv.at[t, 1, 0], kv.at[t, 1, 0], recv_v.at[t]).wait()
+            over_x(t)[0].start()
+            over_x(t)[1].start()
+
+        for turn_of, hops in ((1, (5, 6)), (3, (7,))):
+
+            @pl.when(t == turn_of)
+            def _(hops=hops):
+                for j in hops:
+                    start_kv(j)
+
+        pl.when(t == 1)(prepare)
         return carry
 
-    lax.fori_loop(0, X_CHUNKS + 3, turn, 0)
+    lax.fori_loop(0, X_CHUNKS + 4, turn, 0)
 
     for h in range(GROUP):
         result = summed[h] * (1.0 / total[h])

time: 66.7 us -> 67.2 us (level)
  Pallas kernels: 64 us -> 65.1 us
    pallas_call x1, Pallas kernels: 64 us -> 65.1 us  [shards(): pl.pallas_call(kernel, out_shape=jax.ShapeDtypeStruct(latent.shape, laten...]
where the time goes in v9:
time: 67.2 us; the launch traced here: 66.8 us
  Pallas kernels  65.1 us (97%)
  local copies, waits for them, and re-layouts  1.72 us (3%)
    pallas_call x1, Pallas kernels, shards(): pl.pallas_call(kernel, out_shape=jax.ShapeDtypeStruct(latent.shape, laten...  65.1 us
    unnamed x1, local copies, waits for them, and re-layouts  1.72 us

profile of v9, /device:TPU:1, one launch (start us, length us, event | category | flops | bytes accessed | tf_op | source)
XLA Modules:
  0.0 66.8 jit_solution(11012586188327891948)
XLA Ops:
  0.0 65.1 %shard_map.100 = bf16[32,5120]{1,0:T(8,128)(2,1)} custom-call(s32[4]{0:T(128)} %levels.1, s32[50]{0:T(128)} %timesteps.1, s32[4,32]{1,0:T(4,128)} %cache_mask.1, bf16[32,5120]{1,0:T(8,128)(2,1)} %latent.1, bf16[32,5120]{1,0:T(8,128)(2,1)} %query_in.1, bf16[32,5120]{1,0:T(8,128)(2,1)} %key_in.1, bf16[32,5120]{1,0:T(8,128)(2,1)} %value_in.1, ...), custom_call_target="tpu_custom_call" | custom-call | flops 2000000000 | bytes 5000000 | tf_op jit(solution)/shard_map/pallas_call | solution.py:324
  65.1 1.7 %copy.12 = bf16[32,5120]{1,0:T(8,128)(2,1)} copy(bf16[32,5120]{1,0:T(8,128)(2,1)} %shard_map.100) | data formatting | bytes 655360

commit v10 on v9

--- a/solution.py
+++ b/solution.py
@@ -35,8 +35,8 @@
 def kernel(
     levels, timesteps, cache_mask, latent, query_in, key_in, value_in, cache_keys, cache_values, time_weight,
     out,
-    query, turned, kv, attended, returned, shifted, weight, gate, scored, weighed, factor, peak, total, summed, bias,
-    send_z, send_x, send_y, send_o, recv_q, recv_k, recv_v, recv_x, recv_y, recv_o, local,
+    query, turned, kv, relay, attended, returned, shifted, weight, gate, scored, weighed, factor, peak, total, summed, bias,
+    send_z, send_x, send_y, send_o, recv_q, recv_k, recv_v, recv_relay, recv_x, recv_y, recv_o, local,
 ):
     chain, head = lax.axis_index("chain"), lax.axis_index("head")
     y, x = chain // 8, chain % 4
@@ -46,6 +46,7 @@
     right, left = (x + 1) % 4, (x + 3) % 4
     sibling = device(y, z, x, 1 - core)
     across = device(y, (z + 4) % 8, x, 1 - core)
+    back_two = device(y, (z + 6) % 8, x, core)
 
     def remote(src, dst, send, recv, to):
         return pltpu.make_async_remote_copy(
@@ -88,13 +89,13 @@
 
     def kv_over_z(j, which, source, recv):
         to = (z + HOPS[j]) % 8
-        return remote(
-            source.at[:, group_columns(to)],
-            kv.at[j + 1, which, 0],
-            send_z.at[j, which],
-            recv.at[j + 1],
-            device(y, to, x, core),
-        )
+        source = source.at[:, group_columns(to)]
+        if HOPS[j] == 4:
+            return remote(source, relay.at[which], send_z.at[j, which], recv_relay.at[which], back_two)
+        return remote(source, kv.at[j + 1, which, 0], send_z.at[j, which], recv.at[j + 1], device(y, to, x, core))
+
+    def relay_on(which, recv):
+        return remote(relay.at[which], kv.at[8, which, 0], send_z.at[8, which], recv.at[8], back_two)
 
     def over_x(i):
         own_kv = kv.at[i, :, 0]
@@ -137,7 +138,7 @@
 
     for j in range(1, 8):
         query_over_z(j).start()
-    for j in range(1, 5):
+    for j in (1, 2, 7, 3, 4):
         start_kv(j)
     latent_down.start()
 
@@ -216,6 +217,9 @@
 
         @pl.when(t == 4)
         def _():
+            for which, source, recv in ((0, key_in, recv_k), (1, value_in, recv_v)):
+                kv_over_z(7, which, source, recv).wait_recv()
+                relay_on(which, recv).start()
             y_up.start()
             y_down.start()
             own[2].wait()
@@ -265,7 +269,7 @@
             over_x(t)[0].start()
             over_x(t)[1].start()
 
-        for turn_of, hops in ((1, (5, 6)), (3, (7,))):
+        for turn_of, hops in ((1, (5, 6)),):
 
             @pl.when(t == turn_of)
             def _(hops=hops):
@@ -288,6 +292,8 @@
         cache_across(0, cache_keys, recv_k).wait_send()
         cache_across(1, cache_values, recv_v).wait_send()
 
+    relay_on(0, recv_k).wait_send()
+    relay_on(1, recv_v).wait_send()
     for j in range(1, 8):
         query_over_z(j).wait_send()
         kv_over_z(j, 0, key_in, recv_k).wait_send()
@@ -330,6 +336,7 @@
             pltpu.VMEM((8, ROWS, WIDTH), bf16),
             pltpu.VMEM((GROUP, HEAD_DIM, KEYS), bf16),
             pltpu.VMEM((CHUNKS, 2, 8, ROWS, WIDTH), bf16),
+            pltpu.VMEM((2, ROWS, WIDTH), bf16),
             pltpu.VMEM((8, ROWS, WIDTH), bf16),
             pltpu.VMEM(latent.shape, bf16),
             pltpu.VMEM(latent.shape, bf16),
@@ -342,13 +349,14 @@
             pltpu.VMEM((GROUP, 1, KEYS), f32),
             pltpu.VMEM((GROUP, HEAD_DIM, KEYS), f32),
             pltpu.SMEM((CHUNKS * 8,), f32),
-            dma((8, 3)),
+            dma((9, 3)),
             dma((X_CHUNKS, 5)),
             dma((8,)),
             dma((8,)),
             dma((8,)),
             dma((X_CHUNKS,)),
             dma((X_CHUNKS,)),
+            dma((2,)),
             dma((X_CHUNKS, 5)),
             dma((8,)),
             dma((8,)),

time: 67.2 us -> 67 us (level)
  the two profiles are of different devices: /device:TPU:1 before, /device:TPU:88 now
where the time goes in v10:
time: 67 us; the launch traced here: 66.8 us
  Pallas kernels  65.1 us (97%)
  local copies, waits for them, and re-layouts  1.72 us (3%)
    pallas_call x1, Pallas kernels, shards(): pl.pallas_call(kernel, out_shape=jax.ShapeDtypeStruct(latent.shape, laten...  65.1 us
    unnamed x1, local copies, waits for them, and re-layouts  1.72 us

profile of v10, /device:TPU:88, one launch (start us, length us, event | category | flops | bytes accessed | tf_op | source)
XLA Modules:
  0.0 66.8 jit_solution(12722571503730795428)
XLA Ops:
  0.0 65.1 %shard_map.100 = bf16[32,5120]{1,0:T(8,128)(2,1)} custom-call(s32[4]{0:T(128)} %levels.1, s32[50]{0:T(128)} %timesteps.1, s32[4,32]{1,0:T(4,128)} %cache_mask.1, bf16[32,5120]{1,0:T(8,128)(2,1)} %latent.1, bf16[32,5120]{1,0:T(8,128)(2,1)} %query_in.1, bf16[32,5120]{1,0:T(8,128)(2,1)} %key_in.1, bf16[32,5120]{1,0:T(8,128)(2,1)} %value_in.1, ...), custom_call_target="tpu_custom_call" | custom-call | flops 2000000000 | bytes 5000000 | tf_op jit(solution)/shard_map/pallas_call | solution.py:330
  65.1 1.7 %copy.12 = bf16[32,5120]{1,0:T(8,128)(2,1)} copy(bf16[32,5120]{1,0:T(8,128)(2,1)} %shard_map.100) | data formatting | bytes 655360

commit v11 on v9

v11 whole, which is shorter than its diff:
```python
import functools
import math

import jax
import jax.numpy as jnp
from jax import lax
from jax.experimental import pallas as pl
from jax.experimental.pallas import tpu as pltpu
from jax.sharding import PartitionSpec as P

MESH = pl.DeviceIdType.MESH
HEAD_DIM = 128
SPANS = 4
NY, NX, NZ = 4, 4, 8
GROUP = 5
WIDTH = GROUP * HEAD_DIM
ROWS = 32
HOPS = (0, 1, 7, 2, 6, 3, 5, 4)
PAIRS = ((0, 1), (2, 3), (4, 5), (9, 10), (6, 7), (8, 11))
X_ITEMS = 9
KEYS = 8 * ROWS
HIDDEN = -1e30


def device(y, z, x, core):
    return {"chain": (y * 2 + z // 4) * NX + x, "head": (z % 4) * 2 + core}


def place(i):
    if isinstance(i, int):
        return next((n, pair.index(i)) for n, pair in enumerate(PAIRS) if i in pair)
    return jnp.where(i < 6, i // 2, jnp.where(i < 8, 4, 5)), i % 2


def group_columns(z):
    group = (z % 4) * 2 + z // 4
    return pl.ds(pl.multiple_of(group * WIDTH, 128), WIDTH)


def kernel(
    levels, timesteps, cache_mask, latent, query_in, key_in, value_in, cache_keys, cache_values, time_weight,
    out,
    query, turned, kv, attended, returned, shifted, weight, gate, scored, weighed, factor, peak, total, summed,
    other_query, partial, other_partial, other_peak, other_total, bias,
    send_z, send_x, send_y, send_o, send_c, recv_q, recv_k, recv_v, recv_x, recv_y, recv_o, recv_c, local,
):
    chain, head = lax.axis_index("chain"), lax.axis_index("head")
    y, x = chain // 8, chain % 4
    zh, zl, core = (chain // 4) % 2, head // 2, head % 2
    z = zh * 4 + zl
    up, down = (y + 1) % 4, (y + 3) % 4
    right, left = (x + 1) % 4, (x + 3) % 4
    sibling = device(y, z, x, 1 - core)
    across = device(y, (z + 4) % 8, x, 1 - core)

    def remote(src, dst, send, recv, to):
        return pltpu.make_async_remote_copy(
            src_ref=src, dst_ref=dst, send_sem=send, recv_sem=recv, device_id=to, device_id_type=MESH
        )

    def item(i):
        pair, member = place(i)
        return kv.at[pair, :, member]

    mine = group_columns(z)
    own = [
        pltpu.make_async_copy(key_in.at[:, mine], item(0).at[0, 0], recv_k.at[0]),
        pltpu.make_async_copy(value_in.at[:, mine], item(0).at[1, 0], recv_v.at[0]),
        pltpu.make_async_copy(query_in.at[:, mine], query.at[0], recv_q.at[0]),
    ]
    for copy in own:
        copy.start()
    weight_copy = pltpu.make_async_copy(time_weight, weight, local.at[0])
    weight_copy.start()

    @pl.when(core == zh)
    def _():
        pltpu.make_async_copy(cache_keys, item(1).at[0, 0], recv_k.at[1]).start()
        pltpu.make_async_copy(cache_values, item(1).at[1, 0], recv_v.at[1]).start()

    barrier = pltpu.get_barrier_semaphore()
    partners = [sibling, across, device(y, z, right, core), device(y, z, left, core)]
    partners += [device(up, z, x, core), device(down, z, x, core)]
    for hop in HOPS[1:]:
        partners += [device(row, (z + hop) % 8, x, core) for row in (y, up, down)]
    for partner in partners:
        pl.semaphore_signal(barrier, inc=1, device_id=partner, device_id_type=MESH)
    pl.semaphore_wait(barrier, len(partners))

    def cache_across(which, source, recv):
        return remote(source, item(1).at[which, 0], send_z.at[0, which], recv.at[1], across)

    def query_over_z(j):
        to = (z + HOPS[j]) % 8
        return remote(
            query_in.at[:, group_columns(to)], query.at[j], send_z.at[j, 2], recv_q.at[j], device(y, to, x, core)
        )

    def kv_over_z(j, which, source, recv):
        to = (z + HOPS[j]) % 8
        return remote(
            source.at[:, group_columns(to)],
            item(j + 1).at[which, 0],
            send_z.at[j, which],
            recv.at[j + 1],
            device(y, to, x, core),
        )

    def over_x(i):
        here = item(i)
        return (
            remote(here.at[:, 0], here.at[:, 1], send_x.at[i, 0], recv_x.at[i, 0], device(y, z, right, core)),
            remote(here.at[:, 0], here.at[:, 3], send_x.at[i, 1], recv_x.at[i, 1], device(y, z, left, core)),
            remote(here.at[0, 1], here.at[0, 2], send_x.at[i, 2], recv_x.at[i, 2], device(y, z, right, core)),
            remote(here.at[1, 3], here.at[1, 2], send_x.at[i, 3], recv_x.at[i, 3], device(y, z, left, core)),
        )

    to_up, to_down = device(up, z, x, core), device(down, z, x, core)
    y_up = remote(item(1), item(9), send_y.at[0], recv_y.at[0], to_up)
    y_down = remote(item(1), item(10), send_y.at[1], recv_y.at[1], to_down)
    y_on_up = remote(item(9).at[0], item(11).at[0], send_y.at[2], recv_y.at[2], to_up)
    y_on_down = remote(item(10).at[1], item(11).at[1], send_y.at[3], recv_y.at[3], to_down)
    latent_down = remote(latent, shifted, send_y.at[4], recv_y.at[4], to_down)

    query_across = remote(query, other_query, send_c.at[0], recv_c.at[0], sibling)
    theirs = slice(KEYS, 2 * KEYS)
    partial_across = remote(partial, other_partial, send_c.at[1], recv_c.at[1], sibling)
    peak_across = remote(peak.at[:, :, theirs], other_peak, send_c.at[2], recv_c.at[2], sibling)
    total_across = remote(total.at[:, :, theirs], other_total, send_c.at[3], recv_c.at[3], sibling)

    def back(j):
        to = (z - HOPS[j] + 8) % 8
        return remote(attended.at[j], returned.at[:, mine], send_o.at[j], recv_o.at[j], device(down, to, x, core))

    @pl.when(core != zh)
    def _():
        cache_across(0, cache_keys, recv_k).start()
        cache_across(1, cache_values, recv_v).start()

    def start_kv(j):
        kv_over_z(j, 0, key_in, recv_k).start()
        kv_over_z(j, 1, value_in, recv_v).start()

    for j in range(1, 8):
        query_over_z(j).start()
    for j in range(1, 5):
        start_kv(j)
    latent_down.start()

    def prepare():
        for pair, items in enumerate(PAIRS):
            for slot in range(8):
                i = items[slot // 4]
                shown = jnp.float32(0.0)
                if i == 1 or i >= 9:
                    plane = {1: y, 9: down, 10: up, 11: (y + 2) % 4}[i]
                    block = plane * 8 + core * 4 + (x + (0, 3, 2, 1)[slot % 4]) % 4
                    shown = jnp.where(cache_mask[y, block] == 1, 0.0, HIDDEN).astype(jnp.float32)
                bias[pair * 8 + slot] = shown

        stamp = timesteps[levels[up]].astype(jnp.float32)
        count = 128
        index = lax.broadcasted_iota(jnp.int32, (8, count), 1).astype(jnp.float32)
        phase = stamp * jnp.exp(-math.log(10000.0) * index / count)
        embed = jnp.concatenate([jnp.cos(phase), jnp.sin(phase)], axis=1).astype(jnp.bfloat16)
        weight_copy.wait()

        def gate_columns(c, carry):
            columns = pl.ds(pl.multiple_of(c * WIDTH, 128), WIDTH)
            gate[:, columns] = jnp.dot(embed, weight[:, columns], preferred_element_type=jnp.float32)
            return carry

        lax.fori_loop(0, 8, gate_columns, 0)

        peak[...] = jnp.full_like(peak, HIDDEN)
        total[...] = jnp.zeros_like(total)
        summed[...] = jnp.zeros_like(summed)

    def attend(pair, half):
        def of_head(which, h):
            return kv[pair, which, :, :, :, h * HEAD_DIM : (h + 1) * HEAD_DIM].reshape(KEYS, HEAD_DIM)

        scale = 1.0 / math.sqrt(HEAD_DIM)
        for h in range(GROUP):
            scored[h] = jnp.dot(of_head(0, h), turned[half, h], preferred_element_type=jnp.float32)
        for h in range(GROUP):
            for side in (0, 128):
                scores = scored[h, :, side : side + 128]
                scores = jnp.concatenate(
                    [scores[slot * ROWS : (slot + 1) * ROWS] + bias[pair * 8 + slot] for slot in range(8)], axis=0
                )
                columns = pl.ds(pl.multiple_of(half * KEYS + side, 128), 128)
                old = peak[h, :, columns]
                new = jnp.maximum(old, jnp.max(scores, axis=0, keepdims=True) * scale)
                weights = jnp.exp(scores * scale - new)
                shrink = jnp.exp(old - new)
                peak[h, :, columns] = new
                factor[h, :, side : side + 128] = shrink
                total[h, :, columns] = shrink * total[h, :, columns] + jnp.sum(weights, axis=0, keepdims=True)
                weighed[h, :, side : side + 128] = weights.astype(jnp.bfloat16)
        for h in range(GROUP):
            added = lax.dot_general(
                of_head(1, h), weighed[h], (((0,), (0,)), ((), ())), preferred_element_type=jnp.float32
            )
            summed[half, h] = factor[h] * summed[half, h] + added

    def attend_both(pair):
        def half(n, carry):
            attend(pair, n)
            return carry

        lax.fori_loop(0, 2, half, 0)

    def turn_query(source, half):
        for h in range(GROUP):
            columns = slice(h * HEAD_DIM, (h + 1) * HEAD_DIM)
            turned[half, h] = source[:, :, columns].reshape(KEYS, HEAD_DIM).astype(jnp.float32).T.astype(jnp.bfloat16)

    def turn(t, carry):
        @pl.when((t >= 2) & (t < X_ITEMS + 2))
        def _():
            copies = over_x(t - 2)
            copies[0].wait_recv()
            copies[2].start()
            copies[1].wait_recv()
            copies[3].start()

        @pl.when(t >= 3)
        def _():
            copies = over_x(t - 3)
            copies[2].wait_recv()
            copies[3].wait_recv()

        @pl.when(t == 3)
        def _():
            own[2].wait()
            for j in range(1, 8):
                query_over_z(j).wait_recv()
            query_across.start()
            turn_query(query, 0)

        @pl.when(t == 4)
        def _():
            y_up.start()
            y_down.start()
            query_across.wait_recv()
            turn_query(other_query, 1)

        @pl.when(t == 7)
        def _():
            y_up.wait_recv()
            y_on_up.start()
            y_down.wait_recv()
            y_on_down.start()

        @pl.when((t == 4) | (t == 6) | ((t >= 8) & (t <= 10)))
        def _():
            attend_both(jnp.where(t < 8, (t - 4) // 2, t - 6))

        @pl.when(t < X_ITEMS)
        def _():
            here = item(t)
            pltpu.make_async_copy(here.at[0, 0], here.at[0, 0], recv_k.at[t]).wait()
            pltpu.make_async_copy(here.at[1, 0], here.at[1, 0], recv_v.at[t]).wait()
            over_x(t)[0].start()
            over_x(t)[1].start()

        for turn_of, hops in ((1, (5, 6)), (3, (7,))):

            @pl.when(t == turn_of)
            def _(hops=hops):
                for j in hops:
                    start_kv(j)

        pl.when(t == 1)(prepare)
        return carry

    lax.fori_loop(0, X_ITEMS + 3, turn, 0)
    y_on_up.wait_recv()
    y_on_down.wait_recv()
    attend(len(PAIRS) - 1, 1)
    for h in range(GROUP):
        partial[h] = (summed[1, h] * (1.0 / total[h, :, theirs])).astype(jnp.bfloat16)
    across_copies = (partial_across, peak_across, total_across)
    for copy in across_copies:
        copy.start()
    attend(len(PAIRS) - 1, 0)
    for copy in across_copies:
        copy.wait_recv()

    ours = slice(0, KEYS)
    for h in range(GROUP):
        new = jnp.maximum(peak[h, :, ours], other_peak[h])
        shrink = jnp.exp(peak[h, :, ours] - new)
        other_weight = other_total[h] * jnp.exp(other_peak[h] - new)
        whole = 1.0 / (shrink * total[h, :, ours] + other_weight)
        result = (shrink * whole) * summed[0, h] + (other_weight * whole) * other_partial[h].astype(jnp.float32)
        attended[:, :, h * HEAD_DIM : (h + 1) * HEAD_DIM] = result.T.astype(jnp.bfloat16).reshape(8, ROWS, HEAD_DIM)
    for j in range(8):
        back(j).start()

    @pl.when(core != zh)
    def _():
        cache_across(0, cache_keys, recv_k).wait_send()
        cache_across(1, cache_values, recv_v).wait_send()

    for j in range(1, 8):
        query_over_z(j).wait_send()
        kv_over_z(j, 0, key_in, recv_k).wait_send()
        kv_over_z(j, 1, value_in, recv_v).wait_send()

    def sent(i, carry):
        for copy in over_x(i):
            copy.wait_send()
        return carry

    lax.fori_loop(0, X_ITEMS, sent, 0)
    for copy in (y_up, y_down, y_on_up, y_on_down, latent_down, query_across) + across_copies:
        copy.wait_send()

    latent_down.wait_recv()
    for j in range(8):
        back(j).wait_recv()
        columns = group_columns((z + HOPS[j]) % 8)
        out[:, columns] = (
            shifted[:, columns].astype(jnp.float32) + gate[0:1, columns] * returned[:, columns].astype(jnp.float32)
        ).astype(jnp.bfloat16)
    for j in range(8):
        back(j).wait_send()


def shards(
    latent, query_in, key_in, value_in, cache_keys, cache_values, levels, timesteps, cache_mask, time_weight
):
    anywhere = pl.BlockSpec(memory_space=pl.ANY)
    scalars = pl.BlockSpec(memory_space=pltpu.SMEM)
    bf16, f32 = jnp.bfloat16, jnp.float32
    dma = pltpu.SemaphoreType.DMA
    return pl.pallas_call(
        kernel,
        out_shape=jax.ShapeDtypeStruct(latent.shape, latent.dtype),
        in_specs=[scalars] * 3 + [anywhere] * 7,
        out_specs=pl.BlockSpec(memory_space=pltpu.VMEM),
        scratch_shapes=[
            pltpu.VMEM((8, ROWS, WIDTH), bf16),
            pltpu.VMEM((2, GROUP, HEAD_DIM, KEYS), bf16),
            pltpu.VMEM((len(PAIRS), 2, 2, 4, ROWS, WIDTH), bf16),
            pltpu.VMEM((8, ROWS, WIDTH), bf16),
            pltpu.VMEM(latent.shape, bf16),
            pltpu.VMEM(latent.shape, bf16),
            pltpu.VMEM(time_weight.shape, bf16),
            pltpu.VMEM((8, latent.shape[1]), f32),
            pltpu.VMEM((GROUP, KEYS, KEYS), f32),
            pltpu.VMEM((GROUP, KEYS, KEYS), bf16),
            pltpu.VMEM((GROUP, 1, KEYS), f32),
            pltpu.VMEM((GROUP, 1, 2 * KEYS), f32),
            pltpu.VMEM((GROUP, 1, 2 * KEYS), f32),
            pltpu.VMEM((2, GROUP, HEAD_DIM, KEYS), f32),
            pltpu.VMEM((8, ROWS, WIDTH), bf16),
            pltpu.VMEM((GROUP, HEAD_DIM, KEYS), bf16),
            pltpu.VMEM((GROUP, HEAD_DIM, KEYS), bf16),
            pltpu.VMEM((GROUP, 1, KEYS), f32),
            pltpu.VMEM((GROUP, 1, KEYS), f32),
            pltpu.SMEM((len(PAIRS) * 8,), f32),
            dma((8, 3)),
            dma((X_ITEMS, 4)),
            dma((5,)),
            dma((8,)),
            dma((4,)),
            dma((8,)),
            dma((X_ITEMS,)),
            dma((X_ITEMS,)),
            dma((X_ITEMS, 4)),
            dma((5,)),
            dma((8,)),
            dma((4,)),
            dma((1,)),
        ],
        compiler_params=pltpu.CompilerParams(
            collective_id=0, has_side_effects=True, vmem_limit_bytes=64 * 1024 * 1024
        ),
        cost_estimate=pl.CostEstimate(flops=2 * 10**9, bytes_accessed=5 * 10**6, transcendentals=4 * 10**6),
    )(
        levels, timesteps, cache_mask, latent, query_in, key_in, value_in, cache_keys, cache_values, time_weight
    )


def solution(mesh):
    return jax.shard_map(
        shards,
        mesh=mesh,
        in_specs=(
            P(("chain", "head"), None),
            P(("chain", "head"), None),
            P(("chain", "head"), None),
            P(("chain", "head"), None),
            P("chain", "head"),
            P("chain", "head"),
            P(),
            P(),
            P(),
            P(),
        ),
        out_specs=P(("chain", "head"), None),
        check_vma=False,
    )
```

time: 67.2 us -> 69.8 us (1.039)
  Pallas kernels: 65.1 us -> 67.9 us
    pallas_call x1, Pallas kernels: 65.1 us -> 67.9 us  [shards(): pl.pallas_call(kernel, out_shape=jax.ShapeDtypeStruct(latent.shape, laten...]
where the time goes in v11:
time: 69.8 us; the launch traced here: 69.6 us
  Pallas kernels  67.9 us (97%)
  local copies, waits for them, and re-layouts  1.72 us (2%)
    pallas_call x1, Pallas kernels, shards(): pl.pallas_call(kernel, out_shape=jax.ShapeDtypeStruct(latent.shape, laten...  67.9 us
    unnamed x1, local copies, waits for them, and re-layouts  1.72 us

profile of v11, /device:TPU:1, one launch (start us, length us, event | category | flops | bytes accessed | tf_op | source)
XLA Modules:
  0.0 69.6 jit_solution(17462483321056143062)
XLA Ops:
  0.0 67.9 %shard_map.100 = bf16[32,5120]{1,0:T(8,128)(2,1)} custom-call(s32[4]{0:T(128)} %levels.1, s32[50]{0:T(128)} %timesteps.1, s32[4,32]{1,0:T(4,128)} %cache_mask.1, bf16[32,5120]{1,0:T(8,128)(2,1)} %latent.1, bf16[32,5120]{1,0:T(8,128)(2,1)} %query_in.1, bf16[32,5120]{1,0:T(8,128)(2,1)} %key_in.1, bf16[32,5120]{1,0:T(8,128)(2,1)} %value_in.1, ...), custom_call_target="tpu_custom_call" | custom-call | flops 2000000000 | bytes 5000000 | tf_op jit(solution)/shard_map/pallas_call | solution.py:339
  67.9 1.7 %copy.12 = bf16[32,5120]{1,0:T(8,128)(2,1)} copy(bf16[32,5120]{1,0:T(8,128)(2,1)} %shard_map.100) | data formatting | bytes 655360

commit v12 on v8

--- a/solution.py
+++ b/solution.py
@@ -359,7 +359,10 @@
             dma((1,)),
         ],
         compiler_params=pltpu.CompilerParams(
-            collective_id=0, has_side_effects=True, vmem_limit_bytes=64 * 1024 * 1024
+            collective_id=0,
+            has_side_effects=True,
+            vmem_limit_bytes=64 * 1024 * 1024,
+            fuse_transposed_lhs_in_matmul=True,
         ),
         cost_estimate=pl.CostEstimate(flops=2 * 10**9, bytes_accessed=5 * 10**6, transcendentals=4 * 10**6),
     )(

time: 66.7 us -> 67 us (level)
  no operation moved by 1% of the time
where the time goes in v12:
time: 67 us; the launch traced here: 65.9 us
  Pallas kernels  64.1 us (96%)
  local copies, waits for them, and re-layouts  1.72 us (3%)
    pallas_call x1, Pallas kernels, shards(): pl.pallas_call(kernel, out_shape=jax.ShapeDtypeStruct(latent.shape, laten...  64.1 us
    unnamed x1, local copies, waits for them, and re-layouts  1.72 us

profile of v12, /device:TPU:1, one launch (start us, length us, event | category | flops | bytes accessed | tf_op | source)
XLA Modules:
  0.0 65.9 jit_solution(6030136185391944404)
XLA Ops:
  0.0 64.1 %shard_map.100 = bf16[32,5120]{1,0:T(8,128)(2,1)} custom-call(s32[4]{0:T(128)} %levels.1, s32[50]{0:T(128)} %timesteps.1, s32[4,32]{1,0:T(4,128)} %cache_mask.1, bf16[32,5120]{1,0:T(8,128)(2,1)} %latent.1, bf16[32,5120]{1,0:T(8,128)(2,1)} %query_in.1, bf16[32,5120]{1,0:T(8,128)(2,1)} %key_in.1, bf16[32,5120]{1,0:T(8,128)(2,1)} %value_in.1, ...), custom_call_target="tpu_custom_call" | custom-call | flops 2000000000 | bytes 5000000 | tf_op jit(solution)/shard_map/pallas_call | solution.py:328
  64.2 1.7 %copy.12 = bf16[32,5120]{1,0:T(8,128)(2,1)} copy(bf16[32,5120]{1,0:T(8,128)(2,1)} %shard_map.100) | data formatting | bytes 655360

commit v13 on v9

--- a/solution.py
+++ b/solution.py
@@ -27,15 +27,18 @@
     return {"chain": (y * 2 + z // 4) * NX + x, "head": (z % 4) * 2 + core}
 
 
+def group_of(z):
+    return (z % 4) * 2 + z // 4
+
+
 def group_columns(z):
-    group = (z % 4) * 2 + z // 4
-    return pl.ds(pl.multiple_of(group * WIDTH, 128), WIDTH)
+    return pl.ds(pl.multiple_of(group_of(z) * WIDTH, 128), WIDTH)
 
 
 def kernel(
     levels, timesteps, cache_mask, latent, query_in, key_in, value_in, cache_keys, cache_values, time_weight,
     out,
-    query, turned, kv, attended, returned, shifted, weight, gate, scored, weighed, factor, peak, total, summed, bias,
+    staged, query, turned, kv, attended, returned, shifted, weight, gate, scored, weighed, factor, peak, total, summed, bias,
     send_z, send_x, send_y, send_o, recv_q, recv_k, recv_v, recv_x, recv_y, recv_o, local,
 ):
     chain, head = lax.axis_index("chain"), lax.axis_index("head")
@@ -52,6 +55,10 @@
             src_ref=src, dst_ref=dst, send_sem=send, recv_sem=recv, device_id=to, device_id_type=MESH
         )
 
+    for n, source in enumerate((query_in, key_in, value_in)):
+        for group in range(8):
+            columns = slice(group * WIDTH, (group + 1) * WIDTH)
+            pltpu.make_async_copy(source.at[:, columns], staged.at[n, group], local.at[n + 1]).start()
     mine = group_columns(z)
     own = [
         pltpu.make_async_copy(key_in.at[:, mine], kv.at[0, 0, 0], recv_k.at[0]),
@@ -77,19 +84,22 @@
         pl.semaphore_signal(barrier, inc=1, device_id=partner, device_id_type=MESH)
     pl.semaphore_wait(barrier, len(partners))
 
+    for n in range(3):
+        pltpu.make_async_copy(staged.at[n], staged.at[n], local.at[n + 1]).wait()
+
     def cache_across(which, source, recv):
         return remote(source, kv.at[1, which, 0], send_z.at[0, which], recv.at[1], across)
 
     def query_over_z(j):
         to = (z + HOPS[j]) % 8
         return remote(
-            query_in.at[:, group_columns(to)], query.at[j], send_z.at[j, 2], recv_q.at[j], device(y, to, x, core)
+            staged.at[0, group_of(to)], query.at[j], send_z.at[j, 2], recv_q.at[j], device(y, to, x, core)
         )
 
     def kv_over_z(j, which, source, recv):
         to = (z + HOPS[j]) % 8
         return remote(
-            source.at[:, group_columns(to)],
+            staged.at[1 + which, group_of(to)],
             kv.at[j + 1, which, 0],
             send_z.at[j, which],
             recv.at[j + 1],
@@ -124,7 +134,7 @@
 
     def back(j):
         to = (z - HOPS[j] + 8) % 8
-        return remote(attended.at[j], returned.at[:, mine], send_o.at[j], recv_o.at[j], device(down, to, x, core))
+        return remote(attended.at[j], returned.at[j], send_o.at[j], recv_o.at[j], device(down, to, x, core))
 
     @pl.when(core != zh)
     def _():
@@ -308,7 +318,7 @@
         back(j).wait_recv()
         columns = group_columns((z + HOPS[j]) % 8)
         out[:, columns] = (
-            shifted[:, columns].astype(jnp.float32) + gate[0:1, columns] * returned[:, columns].astype(jnp.float32)
+            shifted[:, columns].astype(jnp.float32) + gate[0:1, columns] * returned[j].astype(jnp.float32)
         ).astype(jnp.bfloat16)
     for j in range(8):
         back(j).wait_send()
@@ -327,11 +337,12 @@
         in_specs=[scalars] * 3 + [anywhere] * 7,
         out_specs=pl.BlockSpec(memory_space=pltpu.VMEM),
         scratch_shapes=[
+            pltpu.VMEM((3, 8, ROWS, WIDTH), bf16),
             pltpu.VMEM((8, ROWS, WIDTH), bf16),
             pltpu.VMEM((GROUP, HEAD_DIM, KEYS), bf16),
             pltpu.VMEM((CHUNKS, 2, 8, ROWS, WIDTH), bf16),
             pltpu.VMEM((8, ROWS, WIDTH), bf16),
-            pltpu.VMEM(latent.shape, bf16),
+            pltpu.VMEM((8, ROWS, WIDTH), bf16),
             pltpu.VMEM(latent.shape, bf16),
             pltpu.VMEM(time_weight.shape, bf16),
             pltpu.VMEM((8, latent.shape[1]), f32),
@@ -352,7 +363,7 @@
             dma((X_CHUNKS, 5)),
             dma((8,)),
             dma((8,)),
-            dma((1,)),
+            dma((4,)),
         ],
         compiler_params=pltpu.CompilerParams(
             collective_id=0, has_side_effects=True, vmem_limit_bytes=64 * 1024 * 1024

time: 67.2 us -> 67.8 us (level)
  Pallas kernels: 65.1 us -> 65.9 us
    pallas_call x1, Pallas kernels: 65.1 us -> 65.9 us  [shards(): pl.pallas_call(kernel, out_shape=jax.ShapeDtypeStruct(latent.shape, laten...]
where the time goes in v13:
time: 67.8 us; the launch traced here: 67.6 us
  Pallas kernels  65.9 us (97%)
  local copies, waits for them, and re-layouts  1.72 us (3%)
    pallas_call x1, Pallas kernels, shards(): pl.pallas_call(kernel, out_shape=jax.ShapeDtypeStruct(latent.shape, laten...  65.9 us
    unnamed x1, local copies, waits for them, and re-layouts  1.72 us

profile of v13, /device:TPU:1, one launch (start us, length us, event | category | flops | bytes accessed | tf_op | source)
XLA Modules:
  0.0 67.6 jit_solution(11075855069121604218)
XLA Ops:
  0.0 65.9 %shard_map.100 = bf16[32,5120]{1,0:T(8,128)(2,1)} custom-call(s32[4]{0:T(128)} %levels.1, s32[50]{0:T(128)} %timesteps.1, s32[4,32]{1,0:T(4,128)} %cache_mask.1, bf16[32,5120]{1,0:T(8,128)(2,1)} %latent.1, bf16[32,5120]{1,0:T(8,128)(2,1)} %query_in.1, bf16[32,5120]{1,0:T(8,128)(2,1)} %key_in.1, bf16[32,5120]{1,0:T(8,128)(2,1)} %value_in.1, ...), custom_call_target="tpu_custom_call" | custom-call | flops 2000000000 | bytes 5000000 | tf_op jit(solution)/shard_map/pallas_call | solution.py:334
  65.9 1.7 %copy.12 = bf16[32,5120]{1,0:T(8,128)(2,1)} copy(bf16[32,5120]{1,0:T(8,128)(2,1)} %shard_map.100) | data formatting | bytes 655360

commit v14 on v9

v14 whole, which is shorter than its diff:
```python
import functools
import math

import jax
import jax.numpy as jnp
from jax import lax
from jax.experimental import pallas as pl
from jax.experimental.pallas import tpu as pltpu
from jax.sharding import PartitionSpec as P

MESH = pl.DeviceIdType.MESH
HEAD_DIM = 128
SPANS = 4
NY, NX, NZ = 4, 4, 8
GROUP = 5
WIDTH = GROUP * HEAD_DIM
ROWS = 32
HOPS = (0, 1, 7, 2, 6, 3, 5, 4)
CHUNKS = 12
FIRST_Z = 2
X_CHUNKS = 9
KEYS = 8 * ROWS
HIDDEN = -1e30


def device(y, z, x, core):
    return {"chain": (y * 2 + z // 4) * NX + x, "head": (z % 4) * 2 + core}


def group_of(z):
    return (z % 4) * 2 + z // 4


def group_columns(z):
    return pl.ds(pl.multiple_of(group_of(z) * WIDTH, 128), WIDTH)


def kernel(
    levels, timesteps, cache_mask, latent, query_in, key_in, value_in, cache_keys, cache_values, time_weight,
    out,
    query, row_query, turned, landed, kv, attended, returned, shifted, weight, gate,
    scored, weighed, factor, peak, total, summed, bias,
    send_z, send_x, send_y, send_q, send_o, recv_q, recv_kv, recv_x, recv_y, recv_rq, recv_o, local, own_x,
):
    chain, head = lax.axis_index("chain"), lax.axis_index("head")
    y, x = chain // 8, chain % 4
    zh, zl, core = (chain // 4) % 2, head // 2, head % 2
    z = zh * 4 + zl
    up, down = (y + 1) % 4, (y + 3) % 4
    x_right, x_left, x_far = (x + 1) % 4, (x + 3) % 4, (x + 2) % 4
    right, left, far = (device(y, z, to, core) for to in (x_right, x_left, x_far))
    sibling = device(y, z, x, 1 - core)
    across = device(y, (z + 4) % 8, x, 1 - core)
    to_up, to_down = device(up, z, x, core), device(down, z, x, core)
    mine = group_columns(z)

    def remote(src, dst, send, recv, to):
        return pltpu.make_async_remote_copy(
            src_ref=src, dst_ref=dst, send_sem=send, recv_sem=recv, device_id=to, device_id_type=MESH
        )

    def of_head(h):
        return pl.ds(pl.multiple_of(h * HEAD_DIM, 128), HEAD_DIM)

    own_query = pltpu.make_async_copy(query_in.at[:, mine], query.at[0], recv_q.at[0])
    own_query.start()
    pltpu.make_async_copy(key_in.at[:, mine], landed.at[0, 0], recv_kv.at[0, 0]).start()
    pltpu.make_async_copy(value_in.at[:, mine], landed.at[0, 1], recv_kv.at[0, 1]).start()
    weight_copy = pltpu.make_async_copy(time_weight, weight, local.at[0])
    weight_copy.start()

    @pl.when(core == zh)
    def _():
        pltpu.make_async_copy(cache_keys, landed.at[1, 0], recv_kv.at[1, 0]).start()
        pltpu.make_async_copy(cache_values, landed.at[1, 1], recv_kv.at[1, 1]).start()

    barrier = pltpu.get_barrier_semaphore()
    partners = [sibling, across, right, left, far, to_up, to_down]
    partners += [device(y, (z + hop) % 8, x, core) for hop in HOPS[1:]]
    for partner in partners:
        pl.semaphore_signal(barrier, inc=1, device_id=partner, device_id_type=MESH)
    pl.semaphore_wait(barrier, len(partners))

    def cache_across(which):
        source = (cache_keys, cache_values)[which]
        return remote(source, landed.at[1, which], send_z.at[0, which], recv_kv.at[1, which], across)

    def query_over_z(j):
        to = (z + HOPS[j]) % 8
        return remote(
            query_in.at[:, group_columns(to)], query.at[j], send_z.at[j, 2], recv_q.at[j], device(y, to, x, core)
        )

    def kv_over_z(j, which):
        to = (z + HOPS[j]) % 8
        source = (key_in, value_in)[which].at[:, group_columns(to)]
        return remote(
            source, landed.at[j + 1, which], send_z.at[j, which], recv_kv.at[j + 1, which], device(y, to, x, core)
        )

    shared = slice((GROUP - 1) * HEAD_DIM, GROUP * HEAD_DIM)

    def own_copies(i):
        return (
            pltpu.make_async_copy(landed.at[i, :, :, of_head(x)], kv.at[i, :, 0, 0], own_x.at[i, 0]),
            pltpu.make_async_copy(landed.at[i, :, :, shared], kv.at[i, :, 1, 0], own_x.at[i, 1]),
        )

    def x_copy(i, n):
        src, dst, to = (
            lambda: (landed.at[i, :, :, of_head(x_right)], kv.at[i, :, 0, 1], right),
            lambda: (landed.at[i, :, :, shared], kv.at[i, :, 1, 1], right),
            lambda: (landed.at[i, :, :, of_head(x_left)], kv.at[i, :, 0, 3], left),
            lambda: (landed.at[i, :, :, shared], kv.at[i, :, 1, 3], left),
            lambda: (landed.at[i, :, :, of_head(x_far)], kv.at[i, :, 0, 2], far),
            lambda: (kv.at[i, 0, 1, 1], kv.at[i, 0, 1, 2], right),
            lambda: (kv.at[i, 1, 1, 3], kv.at[i, 1, 1, 2], left),
            lambda: (kv.at[i, :, :, 0:4], kv.at[i, :, :, 4:8], sibling),
        )[n]()
        return remote(src, dst, send_x.at[i, n], recv_x.at[i, n], to)

    def y_copy(n):
        src, dst, to = (
            lambda: (kv.at[1, :, :, 0:4], kv.at[9, :, :, 0:4], to_up),
            lambda: (kv.at[1, :, :, 0:4], kv.at[10, :, :, 0:4], to_down),
            lambda: (kv.at[9, 0, :, 0:4], kv.at[11, 0, :, 0:4], to_up),
            lambda: (kv.at[10, 1, :, 0:4], kv.at[11, 1, :, 0:4], to_down),
            lambda: (kv.at[9, :, :, 0:4], kv.at[9, :, :, 4:8], sibling),
            lambda: (kv.at[10, :, :, 0:4], kv.at[10, :, :, 4:8], sibling),
            lambda: (kv.at[11, :, :, 0:4], kv.at[11, :, :, 4:8], sibling),
            lambda: (latent, shifted, to_down),
        )[n]()
        return remote(src, dst, send_y.at[n], recv_y.at[n], to)

    def query_over_x(n):
        to, slot = ((x_right, 0), (x_far, 1), (x_left, 2))[n]
        return remote(
            query.at[:, :, of_head(to)], row_query.at[slot], send_q.at[n], recv_rq.at[n], device(y, z, to, core)
        )

    def back(tile, j):
        to_x = x if tile == GROUP - 1 else (x + (0, 3, 2, 1)[tile]) % 4
        to = device(down, (z - HOPS[j] + 8) % 8, to_x, core)
        return remote(attended.at[tile, j], returned.at[tile, j], send_o.at[tile, j], recv_o.at[tile, j], to)

    def start_kv(j):
        kv_over_z(j, 0).start()
        kv_over_z(j, 1).start()

    @pl.when(core != zh)
    def _():
        cache_across(0).start()
        cache_across(1).start()

    for j in range(1, 8):
        query_over_z(j).start()
    for j in range(1, 5):
        start_kv(j)
    y_copy(7).start()

    def prepare():
        for i in range(CHUNKS):
            for slot in range(8):
                if i == 1 or i >= 9:
                    plane = {1: y, 9: down, 10: up, 11: (y + 2) % 4}[i]
                    side = core if slot < 4 else 1 - core
                    block = plane * 8 + side * 4 + (x + (0, 3, 2, 1)[slot % 4]) % 4
                    bias[i * 8 + slot] = jnp.where(cache_mask[y, block] == 1, 0.0, HIDDEN).astype(jnp.float32)
                else:
                    bias[i * 8 + slot] = jnp.float32(0.0)

        stamp = timesteps[levels[up]].astype(jnp.float32)
        count = 128
        index = lax.broadcasted_iota(jnp.int32, (8, count), 1).astype(jnp.float32)
        phase = stamp * jnp.exp(-math.log(10000.0) * index / count)
        embed = jnp.concatenate([jnp.cos(phase), jnp.sin(phase)], axis=1).astype(jnp.bfloat16)
        weight_copy.wait()

        def gate_columns(c, carry):
            columns = pl.ds(pl.multiple_of(c * WIDTH, 128), WIDTH)
            gate[:, columns] = jnp.dot(embed, weight[:, columns], preferred_element_type=jnp.float32)
            return carry

        lax.fori_loop(0, 8, gate_columns, 0)

        peak[...] = jnp.full_like(peak, HIDDEN)
        total[...] = jnp.zeros_like(total)
        summed[...] = jnp.zeros_like(summed)

    def attend(i, cached, finish=None):
        def rows(which, tile):
            return kv[i, which, tile // (GROUP - 1)].reshape(KEYS, HEAD_DIM)

        scale = 1.0 / math.sqrt(HEAD_DIM)
        for h in range(GROUP):
            scored[h] = jnp.dot(rows(0, h), turned[h], preferred_element_type=jnp.float32)
        for h in range(GROUP):
            for side in (slice(0, 128), slice(128, 256)):
                scores = scored[h, :, side]
                if cached:
                    scores = jnp.concatenate(
                        [scores[slot * ROWS : (slot + 1) * ROWS] + bias[i * 8 + slot] for slot in range(8)], axis=0
                    )
                old = peak[h, :, side]
                new = jnp.maximum(old, jnp.max(scores, axis=0, keepdims=True) * scale)
                weights = jnp.exp(scores * scale - new)
                shrink = jnp.exp(old - new)
                peak[h, :, side] = new
                factor[h, :, side] = shrink
                total[h, :, side] = shrink * total[h, :, side] + jnp.sum(weights, axis=0, keepdims=True)
                weighed[h, :, side] = weights.astype(jnp.bfloat16)
        for h in range(GROUP):
            added = lax.dot_general(
                rows(1, h), weighed[h], (((0,), (0,)), ((), ())), preferred_element_type=jnp.float32
            )
            value_sum = factor[h] * summed[h] + added
            if finish is None:
                summed[h] = value_sum
            else:
                finish(h, value_sum)

    def finish(h, value_sum):
        result = value_sum * (1.0 / total[h])
        attended[h] = result.T.astype(jnp.bfloat16).reshape(8, ROWS, HEAD_DIM)
        for j in range(8):
            back(h, j).start()

    def turn_query(h, rows):
        turned[h] = rows.reshape(KEYS, HEAD_DIM).astype(jnp.float32).T.astype(jnp.bfloat16)

    def turn(t, carry):
        @pl.when((t >= 2) & (t < X_CHUNKS + 2))
        def _():
            i = t - 2
            x_copy(i, 0).wait_recv()
            x_copy(i, 1).wait_recv()
            x_copy(i, 5).start()
            x_copy(i, 2).wait_recv()
            x_copy(i, 3).wait_recv()
            x_copy(i, 6).start()

        @pl.when(t >= 3)
        def _():
            i = t - 3
            for copy in own_copies(i):
                copy.wait()
            for n in (4, 5, 6):
                x_copy(i, n).wait_recv()
            x_copy(i, 7).start()

        @pl.when(t == 3)
        def _():
            own_query.wait()
            for j in range(1, 8):
                query_over_z(j).wait_recv()
            for n in range(3):
                query_over_x(n).start()

        @pl.when(t == 4)
        def _():
            y_copy(0).start()
            y_copy(1).start()
            turn_query(0, query[:, :, of_head(x)])
            turn_query(4, query[:, :, shared])
            for n in range(3):
                query_over_x(n).wait_recv()
            turn_query(1, row_query[0])
            turn_query(2, row_query[1])
            turn_query(3, row_query[2])

        @pl.when(t == 7)
        def _():
            for n in (0, 1):
                y_copy(n).wait_recv()
                y_copy(n + 2).start()
                y_copy(n + 4).start()

        @pl.when(t == 9)
        def _():
            y_copy(2).wait_recv()
            y_copy(3).wait_recv()
            y_copy(6).start()

        @pl.when(t >= 4)
        def _():
            x_copy(t - 4, 7).wait_recv()

        @pl.when((t >= 4) & (t != 5))
        def _():
            attend(t - 4, False)

        for i in (9, 10, 11):

            @pl.when(t == i)
            def _(i=i):
                y_copy(i - 5).wait_recv()

        @pl.when((t == 5) | (t >= 9))
        def _():
            attend(jnp.where(t == 5, 1, t), True)

        @pl.when(t < X_CHUNKS)
        def _():
            for which in (0, 1):
                place = landed.at[t, which]
                pltpu.make_async_copy(place, place, recv_kv.at[t, which]).wait()
            for n in range(5):
                x_copy(t, n).start()
            for copy in own_copies(t):
                copy.start()

        for turn_of, hops in ((1, (5, 6)), (3, (7,))):

            @pl.when(t == turn_of)
            def _(hops=hops):
                for j in hops:
                    start_kv(j)

        pl.when(t == 1)(prepare)
        return carry

    lax.fori_loop(0, X_CHUNKS + 3, turn, 0)
    x_copy(X_CHUNKS - 1, 7).wait_recv()
    attend(X_CHUNKS - 1, False, finish)

    @pl.when(core != zh)
    def _():
        cache_across(0).wait_send()
        cache_across(1).wait_send()

    for j in range(1, 8):
        query_over_z(j).wait_send()
        kv_over_z(j, 0).wait_send()
        kv_over_z(j, 1).wait_send()

    def sent(i, carry):
        for n in range(8):
            x_copy(i, n).wait_send()
        return carry

    lax.fori_loop(0, X_CHUNKS, sent, 0)
    for n in range(8):
        y_copy(n).wait_send()
    for n in range(3):
        query_over_x(n).wait_send()

    y_copy(7).wait_recv()
    for tile in range(GROUP):
        for j in range(8):
            back(tile, j).wait_recv()
            of = GROUP - 1 if tile == GROUP - 1 else (x + tile) % 4
            first = group_of((z + HOPS[j]) % 8) * WIDTH + of * HEAD_DIM
            columns = pl.ds(pl.multiple_of(first, 128), HEAD_DIM)
            out[:, columns] = (
                shifted[:, columns].astype(jnp.float32)
                + gate[0:1, columns] * returned[tile, j].astype(jnp.float32)
            ).astype(jnp.bfloat16)
    for tile in range(GROUP):
        for j in range(8):
            back(tile, j).wait_send()


def shards(
    latent, query_in, key_in, value_in, cache_keys, cache_values, levels, timesteps, cache_mask, time_weight
):
    anywhere = pl.BlockSpec(memory_space=pl.ANY)
    scalars = pl.BlockSpec(memory_space=pltpu.SMEM)
    bf16, f32 = jnp.bfloat16, jnp.float32
    dma = pltpu.SemaphoreType.DMA
    return pl.pallas_call(
        kernel,
        out_shape=jax.ShapeDtypeStruct(latent.shape, latent.dtype),
        in_specs=[scalars] * 3 + [anywhere] * 7,
        out_specs=pl.BlockSpec(memory_space=pltpu.VMEM),
        scratch_shapes=[
            pltpu.VMEM((8, ROWS, WIDTH), bf16),
            pltpu.VMEM((3, 8, ROWS, HEAD_DIM), bf16),
            pltpu.VMEM((GROUP, HEAD_DIM, KEYS), bf16),
            pltpu.VMEM((X_CHUNKS, 2, ROWS, WIDTH), bf16),
            pltpu.VMEM((CHUNKS, 2, 2, 8, ROWS, HEAD_DIM), bf16),
            pltpu.VMEM((GROUP, 8, ROWS, HEAD_DIM), bf16),
            pltpu.VMEM((GROUP, 8, ROWS, HEAD_DIM), bf16),
            pltpu.VMEM(latent.shape, bf16),
            pltpu.VMEM(time_weight.shape, bf16),
            pltpu.VMEM((8, latent.shape[1]), f32),
            pltpu.VMEM((GROUP, KEYS, KEYS), f32),
            pltpu.VMEM((GROUP, KEYS, KEYS), bf16),
            pltpu.VMEM((GROUP, 1, KEYS), f32),
            pltpu.VMEM((GROUP, 1, KEYS), f32),
            pltpu.VMEM((GROUP, 1, KEYS), f32),
            pltpu.VMEM((GROUP, HEAD_DIM, KEYS), f32),
            pltpu.SMEM((CHUNKS * 8,), f32),
            dma((8, 3)),
            dma((X_CHUNKS, 8)),
            dma((8,)),
            dma((3,)),
            dma((GROUP, 8)),
            dma((8,)),
            dma((X_CHUNKS, 2)),
            dma((X_CHUNKS, 8)),
            dma((8,)),
            dma((3,)),
            dma((GROUP, 8)),
            dma((1,)),
            dma((X_CHUNKS, 2)),
        ],
        compiler_params=pltpu.CompilerParams(
            collective_id=0, has_side_effects=True, vmem_limit_bytes=64 * 1024 * 1024
        ),
        cost_estimate=pl.CostEstimate(flops=2 * 10**9, bytes_accessed=5 * 10**6, transcendentals=4 * 10**6),
    )(
        levels, timesteps, cache_mask, latent, query_in, key_in, value_in, cache_keys, cache_values, time_weight
    )


def solution(mesh):
    return jax.shard_map(
        shards,
        mesh=mesh,
        in_specs=(
            P(("chain", "head"), None),
            P(("chain", "head"), None),
            P(("chain", "head"), None),
            P(("chain", "head"), None),
            P("chain", "head"),
            P("chain", "head"),
            P(),
            P(),
            P(),
            P(),
        ),
        out_specs=P(("chain", "head"), None),
        check_vma=False,
    )
```

time: 67.2 us -> 65.3 us (0.972)
  Pallas kernels: 65.1 us -> 62.7 us
    pallas_call x1, Pallas kernels: 65.1 us -> 62.7 us  [shards(): pl.pallas_call(kernel, out_shape=jax.ShapeDtypeStruct(latent.shape, laten...]
where the time goes in v14:
time: 65.3 us; the launch traced here: 64.4 us
  Pallas kernels  62.7 us (96%)
  local copies, waits for them, and re-layouts  1.72 us (3%)
    pallas_call x1, Pallas kernels, shards(): pl.pallas_call(kernel, out_shape=jax.ShapeDtypeStruct(latent.shape, laten...  62.7 us
    unnamed x1, local copies, waits for them, and re-layouts  1.72 us

profile of v14, /device:TPU:1, one launch (start us, length us, event | category | flops | bytes accessed | tf_op | source)
XLA Modules:
  0.0 64.4 jit_solution(6136288882667630396)
XLA Ops:
  0.0 62.7 %shard_map.100 = bf16[32,5120]{1,0:T(8,128)(2,1)} custom-call(s32[4]{0:T(128)} %levels.1, s32[50]{0:T(128)} %timesteps.1, s32[4,32]{1,0:T(4,128)} %cache_mask.1, bf16[32,5120]{1,0:T(8,128)(2,1)} %latent.1, bf16[32,5120]{1,0:T(8,128)(2,1)} %query_in.1, bf16[32,5120]{1,0:T(8,128)(2,1)} %key_in.1, bf16[32,5120]{1,0:T(8,128)(2,1)} %value_in.1, ...), custom_call_target="tpu_custom_call" | custom-call | flops 2000000000 | bytes 5000000 | tf_op jit(solution)/shard_map/pallas_call | solution.py:370
  62.7 1.7 %copy.12 = bf16[32,5120]{1,0:T(8,128)(2,1)} copy(bf16[32,5120]{1,0:T(8,128)(2,1)} %shard_map.100) | data formatting | bytes 655360

commit v15 on v14

--- a/solution.py
+++ b/solution.py
@@ -187,46 +187,48 @@
         total[...] = jnp.zeros_like(total)
         summed[...] = jnp.zeros_like(summed)
 
-    def attend(i, cached, finish=None):
-        def rows(which, tile):
-            return kv[i, which, tile // (GROUP - 1)].reshape(KEYS, HEAD_DIM)
-
+    def attend(i, cached):
         scale = 1.0 / math.sqrt(HEAD_DIM)
-        for h in range(GROUP):
-            scored[h] = jnp.dot(rows(0, h), turned[h], preferred_element_type=jnp.float32)
-        for h in range(GROUP):
-            for side in (slice(0, 128), slice(128, 256)):
-                scores = scored[h, :, side]
-                if cached:
-                    scores = jnp.concatenate(
-                        [scores[slot * ROWS : (slot + 1) * ROWS] + bias[i * 8 + slot] for slot in range(8)], axis=0
-                    )
-                old = peak[h, :, side]
-                new = jnp.maximum(old, jnp.max(scores, axis=0, keepdims=True) * scale)
-                weights = jnp.exp(scores * scale - new)
-                shrink = jnp.exp(old - new)
-                peak[h, :, side] = new
-                factor[h, :, side] = shrink
-                total[h, :, side] = shrink * total[h, :, side] + jnp.sum(weights, axis=0, keepdims=True)
-                weighed[h, :, side] = weights.astype(jnp.bfloat16)
-        for h in range(GROUP):
-            added = lax.dot_general(
-                rows(1, h), weighed[h], (((0,), (0,)), ((), ())), preferred_element_type=jnp.float32
+        spans = (slice(0, 4 * KEYS), slice(4 * KEYS, 5 * KEYS))
+        keys = [kv[i, 0, n].reshape(KEYS, HEAD_DIM) for n in (0, 1)]
+        scores = [jnp.dot(keys[n], turned[:, spans[n]], preferred_element_type=jnp.float32) for n in (0, 1)]
+        for n in (0, 1):
+            scored[:, spans[n]] = scores[n]
+        for first in range(0, GROUP * KEYS, 128):
+            side = slice(first, first + 128)
+            scores = scored[:, side]
+            if cached:
+                scores = jnp.concatenate(
+                    [scores[slot * ROWS : (slot + 1) * ROWS] + bias[i * 8 + slot] for slot in range(8)], axis=0
+                )
+            old = peak[:, side]
+            new = jnp.maximum(old, jnp.max(scores, axis=0, keepdims=True) * scale)
+            weights = jnp.exp(scores * scale - new)
+            shrink = jnp.exp(old - new)
+            peak[:, side] = new
+            factor[:, side] = shrink
+            total[:, side] = shrink * total[:, side] + jnp.sum(weights, axis=0, keepdims=True)
+            weighed[:, side] = weights.astype(jnp.bfloat16)
+        values = [kv[i, 1, n].reshape(KEYS, HEAD_DIM) for n in (0, 1)]
+        added = [
+            lax.dot_general(
+                values[n], weighed[:, spans[n]], (((0,), (0,)), ((), ())), preferred_element_type=jnp.float32
             )
-            value_sum = factor[h] * summed[h] + added
-            if finish is None:
-                summed[h] = value_sum
-            else:
-                finish(h, value_sum)
-
-    def finish(h, value_sum):
-        result = value_sum * (1.0 / total[h])
+            for n in (0, 1)
+        ]
+        for n in (0, 1):
+            summed[:, spans[n]] = factor[:, spans[n]] * summed[:, spans[n]] + added[n]
+
+    def finish(h):
+        tile = slice(h * KEYS, (h + 1) * KEYS)
+        result = summed[:, tile] * (1.0 / total[:, tile])
         attended[h] = result.T.astype(jnp.bfloat16).reshape(8, ROWS, HEAD_DIM)
         for j in range(8):
             back(h, j).start()
 
     def turn_query(h, rows):
-        turned[h] = rows.reshape(KEYS, HEAD_DIM).astype(jnp.float32).T.astype(jnp.bfloat16)
+        tile = slice(h * KEYS, (h + 1) * KEYS)
+        turned[:, tile] = rows.reshape(KEYS, HEAD_DIM).astype(jnp.float32).T.astype(jnp.bfloat16)
 
     def turn(t, carry):
         @pl.when((t >= 2) & (t < X_CHUNKS + 2))
@@ -321,7 +323,9 @@
 
     lax.fori_loop(0, X_CHUNKS + 3, turn, 0)
     x_copy(X_CHUNKS - 1, 7).wait_recv()
-    attend(X_CHUNKS - 1, False, finish)
+    attend(X_CHUNKS - 1, False)
+    for h in range(GROUP):
+        finish(h)
 
     @pl.when(core != zh)
     def _():
@@ -375,7 +379,7 @@
         scratch_shapes=[
             pltpu.VMEM((8, ROWS, WIDTH), bf16),
             pltpu.VMEM((3, 8, ROWS, HEAD_DIM), bf16),
-            pltpu.VMEM((GROUP, HEAD_DIM, KEYS), bf16),
+            pltpu.VMEM((HEAD_DIM, GROUP * KEYS), bf16),
             pltpu.VMEM((X_CHUNKS, 2, ROWS, WIDTH), bf16),
             pltpu.VMEM((CHUNKS, 2, 2, 8, ROWS, HEAD_DIM), bf16),
             pltpu.VMEM((GROUP, 8, ROWS, HEAD_DIM), bf16),
@@ -383,12 +387,12 @@
             pltpu.VMEM(latent.shape, bf16),
             pltpu.VMEM(time_weight.shape, bf16),
             pltpu.VMEM((8, latent.shape[1]), f32),
-            pltpu.VMEM((GROUP, KEYS, KEYS), f32),
-            pltpu.VMEM((GROUP, KEYS, KEYS), bf16),
-            pltpu.VMEM((GROUP, 1, KEYS), f32),
-            pltpu.VMEM((GROUP, 1, KEYS), f32),
-            pltpu.VMEM((GROUP, 1, KEYS), f32),
-            pltpu.VMEM((GROUP, HEAD_DIM, KEYS), f32),
+            pltpu.VMEM((KEYS, GROUP * KEYS), f32),
+            pltpu.VMEM((KEYS, GROUP * KEYS), bf16),
+            pltpu.VMEM((1, GROUP * KEYS), f32),
+            pltpu.VMEM((1, GROUP * KEYS), f32),
+            pltpu.VMEM((1, GROUP * KEYS), f32),
+            pltpu.VMEM((HEAD_DIM, GROUP * KEYS), f32),
             pltpu.SMEM((CHUNKS * 8,), f32),
             dma((8, 3)),
             dma((X_CHUNKS, 8)),

time: 65.3 us -> 65.4 us (level)
  no operation moved by 1% of the time
where the time goes in v15:
time: 65.4 us; the launch traced here: 64.5 us
  Pallas kernels  62.8 us (96%)
  local copies, waits for them, and re-layouts  1.72 us (3%)
    pallas_call x1, Pallas kernels, shards(): pl.pallas_call(kernel, out_shape=jax.ShapeDtypeStruct(latent.shape, laten...  62.8 us
    unnamed x1, local copies, waits for them, and re-layouts  1.72 us

profile of v15, /device:TPU:1, one launch (start us, length us, event | category | flops | bytes accessed | tf_op | source)
XLA Modules:
  0.0 64.5 jit_solution(8565446150431282769)
XLA Ops:
  0.0 62.8 %shard_map.100 = bf16[32,5120]{1,0:T(8,128)(2,1)} custom-call(s32[4]{0:T(128)} %levels.1, s32[50]{0:T(128)} %timesteps.1, s32[4,32]{1,0:T(4,128)} %cache_mask.1, bf16[32,5120]{1,0:T(8,128)(2,1)} %latent.1, bf16[32,5120]{1,0:T(8,128)(2,1)} %query_in.1, bf16[32,5120]{1,0:T(8,128)(2,1)} %key_in.1, bf16[32,5120]{1,0:T(8,128)(2,1)} %value_in.1, ...), custom_call_target="tpu_custom_call" | custom-call | flops 2000000000 | bytes 5000000 | tf_op jit(solution)/shard_map/pallas_call | solution.py:374
  62.8 1.7 %copy.12 = bf16[32,5120]{1,0:T(8,128)(2,1)} copy(bf16[32,5120]{1,0:T(8,128)(2,1)} %shard_map.100) | data formatting | bytes 655360

commit v16 on v15

--- a/solution.py
+++ b/solution.py
@@ -36,9 +36,9 @@
 
 
 def kernel(
-    levels, timesteps, cache_mask, latent, query_in, key_in, value_in, cache_keys, cache_values, time_weight,
-    out,
-    query, row_query, turned, landed, kv, attended, returned, shifted, weight, gate,
+    levels_in, timesteps_in, mask_in, latent, query_in, key_in, value_in, cache_keys, cache_values, time_weight,
+    returned, shifted, gate,
+    levels, timesteps, cache_mask, query, row_query, turned, landed, kv, attended, weight,
     scored, weighed, factor, peak, total, summed, bias,
     send_z, send_x, send_y, send_q, send_o, recv_q, recv_kv, recv_x, recv_y, recv_rq, recv_o, local, own_x,
 ):
@@ -68,6 +68,14 @@
     pltpu.make_async_copy(value_in.at[:, mine], landed.at[0, 1], recv_kv.at[0, 1]).start()
     weight_copy = pltpu.make_async_copy(time_weight, weight, local.at[0])
     weight_copy.start()
+    scalar_copies = [
+        pltpu.make_async_copy(source, place, local.at[n])
+        for n, (source, place) in enumerate(
+            ((levels_in, levels), (timesteps_in, timesteps), (mask_in, cache_mask)), start=1
+        )
+    ]
+    for copy in scalar_copies:
+        copy.start()
 
     @pl.when(core == zh)
     def _():
@@ -113,8 +121,7 @@
             lambda: (landed.at[i, :, :, of_head(x_left)], kv.at[i, :, 0, 3], left),
             lambda: (landed.at[i, :, :, shared], kv.at[i, :, 1, 3], left),
             lambda: (landed.at[i, :, :, of_head(x_far)], kv.at[i, :, 0, 2], far),
-            lambda: (kv.at[i, 0, 1, 1], kv.at[i, 0, 1, 2], right),
-            lambda: (kv.at[i, 1, 1, 3], kv.at[i, 1, 1, 2], left),
+            lambda: (landed.at[i, :, :, shared], kv.at[i, :, 1, 2], far),
             lambda: (kv.at[i, :, :, 0:4], kv.at[i, :, :, 4:8], sibling),
         )[n]()
         return remote(src, dst, send_x.at[i, n], recv_x.at[i, n], to)
@@ -139,9 +146,10 @@
         )
 
     def back(tile, j):
-        to_x = x if tile == GROUP - 1 else (x + (0, 3, 2, 1)[tile]) % 4
+        to_x, of = (x, GROUP - 1) if tile == GROUP - 1 else ((x + (0, 3, 2, 1)[tile]) % 4, x)
         to = device(down, (z - HOPS[j] + 8) % 8, to_x, core)
-        return remote(attended.at[tile, j], returned.at[tile, j], send_o.at[tile, j], recv_o.at[tile, j], to)
+        columns = pl.ds(pl.multiple_of(group_of(z) * WIDTH + of * HEAD_DIM, 128), HEAD_DIM)
+        return remote(attended.at[tile, j], returned.at[:, columns], send_o.at[tile, j], recv_o.at[tile, j], to)
 
     def start_kv(j):
         kv_over_z(j, 0).start()
@@ -152,13 +160,15 @@
         cache_across(0).start()
         cache_across(1).start()
 
+    start_kv(1)
+    start_kv(2)
     for j in range(1, 8):
         query_over_z(j).start()
-    for j in range(1, 5):
-        start_kv(j)
     y_copy(7).start()
 
     def prepare():
+        for copy in scalar_copies:
+            copy.wait()
         for i in range(CHUNKS):
             for slot in range(8):
                 if i == 1 or i >= 9:
@@ -178,7 +188,7 @@
 
         def gate_columns(c, carry):
             columns = pl.ds(pl.multiple_of(c * WIDTH, 128), WIDTH)
-            gate[:, columns] = jnp.dot(embed, weight[:, columns], preferred_element_type=jnp.float32)
+            gate[:, columns] = jnp.dot(embed, weight[:, columns], preferred_element_type=jnp.float32)[0:1]
             return carry
 
         lax.fori_loop(0, 8, gate_columns, 0)
@@ -231,98 +241,83 @@
         turned[:, tile] = rows.reshape(KEYS, HEAD_DIM).astype(jnp.float32).T.astype(jnp.bfloat16)
 
     def turn(t, carry):
-        @pl.when((t >= 2) & (t < X_CHUNKS + 2))
+        @pl.when(t >= 2)
         def _():
             i = t - 2
-            x_copy(i, 0).wait_recv()
-            x_copy(i, 1).wait_recv()
-            x_copy(i, 5).start()
-            x_copy(i, 2).wait_recv()
-            x_copy(i, 3).wait_recv()
-            x_copy(i, 6).start()
-
-        @pl.when(t >= 3)
-        def _():
-            i = t - 3
             for copy in own_copies(i):
                 copy.wait()
-            for n in (4, 5, 6):
+            for n in range(6):
                 x_copy(i, n).wait_recv()
-            x_copy(i, 7).start()
+            x_copy(i, 6).start()
 
         @pl.when(t == 3)
+        def _():
+            y_copy(0).start()
+            y_copy(1).start()
+
+        @pl.when(t == 4)
         def _():
             own_query.wait()
             for j in range(1, 8):
                 query_over_z(j).wait_recv()
             for n in range(3):
                 query_over_x(n).start()
-
-        @pl.when(t == 4)
-        def _():
-            y_copy(0).start()
-            y_copy(1).start()
+            for n in (0, 1):
+                y_copy(n).wait_recv()
+                y_copy(n + 2).start()
+                y_copy(n + 4).start()
             turn_query(0, query[:, :, of_head(x)])
             turn_query(4, query[:, :, shared])
             for n in range(3):
                 query_over_x(n).wait_recv()
-            turn_query(1, row_query[0])
-            turn_query(2, row_query[1])
-            turn_query(3, row_query[2])
-
-        @pl.when(t == 7)
-        def _():
-            for n in (0, 1):
-                y_copy(n).wait_recv()
-                y_copy(n + 2).start()
-                y_copy(n + 4).start()
-
-        @pl.when(t == 9)
-        def _():
-            y_copy(2).wait_recv()
-            y_copy(3).wait_recv()
-            y_copy(6).start()
+            for n in range(3):
+                turn_query(n + 1, row_query[n])
+            x_copy(0, 6).wait_recv()
 
         @pl.when(t >= 4)
         def _():
-            x_copy(t - 4, 7).wait_recv()
-
-        @pl.when((t >= 4) & (t != 5))
-        def _():
-            attend(t - 4, False)
+            x_copy(t - 3, 6).wait_recv()
 
         for i in (9, 10, 11):
 
-            @pl.when(t == i)
+            @pl.when(t == i - 4)
             def _(i=i):
+                if i == 9:
+                    y_copy(2).wait_recv()
+                    y_copy(3).wait_recv()
+                    y_copy(6).start()
                 y_copy(i - 5).wait_recv()
 
-        @pl.when((t == 5) | (t >= 9))
-        def _():
-            attend(jnp.where(t == 5, 1, t), True)
+        @pl.when(t >= 4)
+        def _():
+            attend(jnp.where(t == 4, 0, t - 3), False)
+
+        @pl.when((t >= 4) & (t <= 7))
+        def _():
+            attend(jnp.where(t == 4, 1, t + 4), True)
 
         @pl.when(t < X_CHUNKS)
         def _():
             for which in (0, 1):
                 place = landed.at[t, which]
                 pltpu.make_async_copy(place, place, recv_kv.at[t, which]).wait()
-            for n in range(5):
+            for n in range(6):
                 x_copy(t, n).start()
             for copy in own_copies(t):
                 copy.start()
 
-        for turn_of, hops in ((1, (5, 6)), (3, (7,))):
+        for turn_of, hops in ((1, (3, 4)), (2, (5, 6)), (3, (7,))):
 
             @pl.when(t == turn_of)
             def _(hops=hops):
                 for j in hops:
                     start_kv(j)
 
-        pl.when(t == 1)(prepare)
+        pl.when(t == 3)(prepare)
         return carry
 
-    lax.fori_loop(0, X_CHUNKS + 3, turn, 0)
-    x_copy(X_CHUNKS - 1, 7).wait_recv()
+    lax.fori_loop(0, X_CHUNKS + 2, turn, 0)
+    x_copy(X_CHUNKS - 1, 6).wait_recv()
     attend(X_CHUNKS - 1, False)
     for h in range(GROUP):
         finish(h)
@@ -338,7 +333,7 @@
         kv_over_z(j, 1).wait_send()
 
     def sent(i, carry):
-        for n in range(8):
+        for n in range(7):
             x_copy(i, n).wait_send()
         return carry
 
@@ -352,13 +347,6 @@
     for tile in range(GROUP):
         for j in range(8):
             back(tile, j).wait_recv()
-            of = GROUP - 1 if tile == GROUP - 1 else (x + tile) % 4
-            first = group_of((z + HOPS[j]) % 8) * WIDTH + of * HEAD_DIM
-            columns = pl.ds(pl.multiple_of(first, 128), HEAD_DIM)
-            out[:, columns] = (
-                shifted[:, columns].astype(jnp.float32)
-                + gate[0:1, columns] * returned[tile, j].astype(jnp.float32)
-            ).astype(jnp.bfloat16)
     for tile in range(GROUP):
         for j in range(8):
             back(tile, j).wait_send()
@@ -368,25 +356,28 @@
     latent, query_in, key_in, value_in, cache_keys, cache_values, levels, timesteps, cache_mask, time_weight
 ):
     anywhere = pl.BlockSpec(memory_space=pl.ANY)
-    scalars = pl.BlockSpec(memory_space=pltpu.SMEM)
-    bf16, f32 = jnp.bfloat16, jnp.float32
+    bf16, f32, i32 = jnp.bfloat16, jnp.float32, jnp.int32
     dma = pltpu.SemaphoreType.DMA
-    return pl.pallas_call(
+    returned, shifted, gate = pl.pallas_call(
         kernel,
-        out_shape=jax.ShapeDtypeStruct(latent.shape, latent.dtype),
-        in_specs=[scalars] * 3 + [anywhere] * 7,
-        out_specs=pl.BlockSpec(memory_space=pltpu.VMEM),
+        out_shape=(
+            jax.ShapeDtypeStruct(latent.shape, bf16),
+            jax.ShapeDtypeStruct(latent.shape, bf16),
+            jax.ShapeDtypeStruct((1, latent.shape[1]), f32),
+        ),
+        in_specs=[anywhere] * 10,
+        out_specs=(anywhere, anywhere, pl.BlockSpec(memory_space=pltpu.VMEM)),
         scratch_shapes=[
+            pltpu.SMEM(levels.shape, i32),
+            pltpu.SMEM(timesteps.shape, i32),
+            pltpu.SMEM(cache_mask.shape, i32),
             pltpu.VMEM((8, ROWS, WIDTH), bf16),
             pltpu.VMEM((3, 8, ROWS, HEAD_DIM), bf16),
             pltpu.VMEM((HEAD_DIM, GROUP * KEYS), bf16),
             pltpu.VMEM((X_CHUNKS, 2, ROWS, WIDTH), bf16),
             pltpu.VMEM((CHUNKS, 2, 2, 8, ROWS, HEAD_DIM), bf16),
             pltpu.VMEM((GROUP, 8, ROWS, HEAD_DIM), bf16),
-            pltpu.VMEM((GROUP, 8, ROWS, HEAD_DIM), bf16),
-            pltpu.VMEM(latent.shape, bf16),
             pltpu.VMEM(time_weight.shape, bf16),
-            pltpu.VMEM((8, latent.shape[1]), f32),
             pltpu.VMEM((KEYS, GROUP * KEYS), f32),
             pltpu.VMEM((KEYS, GROUP * KEYS), bf16),
             pltpu.VMEM((1, GROUP * KEYS), f32),
@@ -395,17 +386,17 @@
             pltpu.VMEM((HEAD_DIM, GROUP * KEYS), f32),
             pltpu.SMEM((CHUNKS * 8,), f32),
             dma((8, 3)),
-            dma((X_CHUNKS, 8)),
+            dma((X_CHUNKS, 7)),
             dma((8,)),
             dma((3,)),
             dma((GROUP, 8)),
             dma((8,)),
             dma((X_CHUNKS, 2)),
-            dma((X_CHUNKS, 8)),
+            dma((X_CHUNKS, 7)),
             dma((8,)),
             dma((3,)),
             dma((GROUP, 8)),
-            dma((1,)),
+            dma((4,)),
             dma((X_CHUNKS, 2)),
         ],
         compiler_params=pltpu.CompilerParams(
@@ -415,6 +406,7 @@
     )(
         levels, timesteps, cache_mask, latent, query_in, key_in, value_in, cache_keys, cache_values, time_weight
     )
+    return (shifted.astype(f32) + gate * returned.astype(f32)).astype(bf16)
 
 
 def solution(mesh):

time: 65.4 us -> 66.5 us (1.017); the launches traced: 64.5 us -> 66.3 us
  other arithmetic: 0 us -> 1.9 us
  local copies, waits for them, and re-layouts: 1.72 us -> 0 us
  Pallas kernels: 62.8 us -> 64.4 us
    convert_element_type x0 -> x1, other arithmetic: none -> 1.9 us  [shards(): return (shifted.astype(f32) + gate * returned.astype(f32)).astype(bf16)]
    unnamed x1 -> x0, local copies, waits for them, and re-layouts: 1.72 us -> none
    pallas_call x1, Pallas kernels: 62.8 us -> 64.4 us  [shards(): pl.pallas_call(kernel, out_shape=(jax.ShapeDtypeStruct(latent.shape, bf16...]
where the time goes in v16:
time: 66.5 us; the launch traced here: 66.3 us
  Pallas kernels  64.4 us (97%)
  other arithmetic  1.9 us (3%)
    pallas_call x1, Pallas kernels, shards(): pl.pallas_call(kernel, out_shape=(jax.ShapeDtypeStruct(latent.shape, bf16...  64.4 us
    convert_element_type x1, other arithmetic, shards(): return (shifted.astype(f32) + gate * returned.astype(f32)).astype(bf16)  1.9 us

profile of v16, /device:TPU:1, one launch (start us, length us, event | category | flops | bytes accessed | tf_op | source)
XLA Modules:
  0.0 66.3 jit_solution(8403641033562213196)
XLA Ops:
  0.0 64.4 %shard_map.100 = (bf16[32,5120]{1,0:T(8,128)(2,1)}, bf16[32,5120]{1,0:T(8,128)(2,1)}, f32[1,5120]{1,0:T(1,128)}) custom-call(s32[4]{0:T(128)} %levels_in.1, s32[50]{0:T(128)} %timesteps_in.1, s32[4,32]{1,0:T(4,128)} %mask_in.1, bf16[32,5120]{1,0:T(8,128)(2,1)} %latent.1, bf16[32,5120]{1,0:T(8,128)(2,1)} %query_in.1, bf16[32,5120]{1,0:T(8,128)(2,1)} %key_in.1, ...), custom_call_target="tpu_custom_call" | custom-call | flops 2000000000 | bytes 5000000 | tf_op jit(solution)/shard_map/pallas_call | solution.py:361
  64.4 1.9 %add_convert_fusion = bf16[32,5120]{1,0:T(8,128)(2,1)} fusion(bf16[32,5120]{1,0:T(8,128)(2,1)} %get-tuple-element.10, bf16[32,5120]{1,0:T(8,128)(2,1)} %get-tuple-element.8, f32[5120]{0:T(1024)} %bitcast.1), kind=kLoop, calls=%fused_computation | loop fusion | flops 819200 | bytes 1003520 | tf_op jit(solution)/shard_map/convert_element_type | solution.py:409

commit v17 on v15

--- a/solution.py
+++ b/solution.py
@@ -15,7 +15,6 @@
 GROUP = 5
 WIDTH = GROUP * HEAD_DIM
 ROWS = 32
-HOPS = (0, 1, 7, 2, 6, 3, 5, 4)
 CHUNKS = 12
 FIRST_Z = 2
 X_CHUNKS = 9
@@ -25,6 +24,10 @@
 
 def device(y, z, x, core):
     return {"chain": (y * 2 + z // 4) * NX + x, "head": (z % 4) * 2 + core}
+
+
+def hop_of(j):
+    return jnp.where(j % 2 == 1, (j + 1) // 2, (8 - j // 2) % 8)
 
 
 def group_of(z):
@@ -54,6 +57,13 @@
     to_up, to_down = device(up, z, x, core), device(down, z, x, core)
     mine = group_columns(z)
 
+    def loop(lower, upper, body):
+        def step(n, carry):
+            body(n)
+            return carry
+
+        lax.fori_loop(lower, upper, step, 0)
+
     def remote(src, dst, send, recv, to):
         return pltpu.make_async_remote_copy(
             src_ref=src, dst_ref=dst, send_sem=send, recv_sem=recv, device_id=to, device_id_type=MESH
@@ -76,23 +86,27 @@
 
     barrier = pltpu.get_barrier_semaphore()
     partners = [sibling, across, right, left, far, to_up, to_down]
-    partners += [device(y, (z + hop) % 8, x, core) for hop in HOPS[1:]]
+
+    def greet(partner):
+        pl.semaphore_signal(barrier, inc=1, device_id=partner, device_id_type=MESH)
+
+    loop(1, 8, lambda hop: greet(device(y, (z + hop) % 8, x, core)))
     for partner in partners:
-        pl.semaphore_signal(barrier, inc=1, device_id=partner, device_id_type=MESH)
-    pl.semaphore_wait(barrier, len(partners))
+        greet(partner)
+    pl.semaphore_wait(barrier, 7 + len(partners))
 
     def cache_across(which):
         source = (cache_keys, cache_values)[which]
         return remote(source, landed.at[1, which], send_z.at[0, which], recv_kv.at[1, which], across)
 
     def query_over_z(j):
-        to = (z + HOPS[j]) % 8
+        to = (z + hop_of(j)) % 8
         return remote(
             query_in.at[:, group_columns(to)], query.at[j], send_z.at[j, 2], recv_q.at[j], device(y, to, x, core)
         )
 
     def kv_over_z(j, which):
-        to = (z + HOPS[j]) % 8
+        to = (z + hop_of(j)) % 8
         source = (key_in, value_in)[which].at[:, group_columns(to)]
         return remote(
             source, landed.at[j + 1, which], send_z.at[j, which], recv_kv.at[j + 1, which], device(y, to, x, core)
@@ -133,14 +147,19 @@
         return remote(src, dst, send_y.at[n], recv_y.at[n], to)
 
     def query_over_x(n):
-        to, slot = ((x_right, 0), (x_far, 1), (x_left, 2))[n]
+        to = (x + n) % 4
         return remote(
-            query.at[:, :, of_head(to)], row_query.at[slot], send_q.at[n], recv_rq.at[n], device(y, z, to, core)
+            query.at[:, :, of_head(to)], row_query.at[n], send_q.at[n], recv_rq.at[n], device(y, z, to, core)
+        )
+
+    def own_query_copies():
+        return (
+            pltpu.make_async_copy(query.at[:, :, of_head(x)], row_query.at[0], recv_rq.at[0]),
+            pltpu.make_async_copy(query.at[:, :, shared], row_query.at[4], recv_rq.at[4]),
         )
 
     def back(tile, j):
-        to_x = x if tile == GROUP - 1 else (x + (0, 3, 2, 1)[tile]) % 4
-        to = device(down, (z - HOPS[j] + 8) % 8, to_x, core)
+        to = device(down, (z - hop_of(j) + 8) % 8, (x + 4 - tile) % 4, core)
         return remote(attended.at[tile, j], returned.at[tile, j], send_o.at[tile, j], recv_o.at[tile, j], to)
 
     def start_kv(j):
@@ -152,22 +171,20 @@
         cache_across(0).start()
         cache_across(1).start()
 
-    for j in range(1, 8):
-        query_over_z(j).start()
-    for j in range(1, 5):
-        start_kv(j)
+    loop(1, 8, lambda j: query_over_z(j).start())
+    loop(1, 5, start_kv)
     y_copy(7).start()
 
     def prepare():
-        for i in range(CHUNKS):
-            for slot in range(8):
-                if i == 1 or i >= 9:
-                    plane = {1: y, 9: down, 10: up, 11: (y + 2) % 4}[i]
-                    side = core if slot < 4 else 1 - core
-                    block = plane * 8 + side * 4 + (x + (0, 3, 2, 1)[slot % 4]) % 4
-                    bias[i * 8 + slot] = jnp.where(cache_mask[y, block] == 1, 0.0, HIDDEN).astype(jnp.float32)
-                else:
-                    bias[i * 8 + slot] = jnp.float32(0.0)
+        def show(n):
+            i, slot = n // 8, n % 8
+            plane = jnp.where(i == 1, y, jnp.where(i == 9, down, jnp.where(i == 10, up, (y + 2) % 4)))
+            side = jnp.where(slot < 4, core, 1 - core)
+            block = plane * 8 + side * 4 + (x + 4 - slot % 4) % 4
+            hidden = ((i == 1) | (i >= 9)) & (cache_mask[y, block] == 0)
+            bias[n] = jnp.where(hidden, HIDDEN, 0.0).astype(jnp.float32)
+
+        loop(0, CHUNKS * 8, show)
 
         stamp = timesteps[levels[up]].astype(jnp.float32)
         count = 128
@@ -187,28 +204,32 @@
         total[...] = jnp.zeros_like(total)
         summed[...] = jnp.zeros_like(summed)
 
-    def attend(i, cached):
+    def attend(i):
         scale = 1.0 / math.sqrt(HEAD_DIM)
         spans = (slice(0, 4 * KEYS), slice(4 * KEYS, 5 * KEYS))
         keys = [kv[i, 0, n].reshape(KEYS, HEAD_DIM) for n in (0, 1)]
         scores = [jnp.dot(keys[n], turned[:, spans[n]], preferred_element_type=jnp.float32) for n in (0, 1)]
         for n in (0, 1):
             scored[:, spans[n]] = scores[n]
-        for first in range(0, GROUP * KEYS, 128):
-            side = slice(first, first + 128)
-            scores = scored[:, side]
-            if cached:
+        shown = [bias[i * 8 + slot] for slot in range(8)]
+
+        def softmax(tile):
+            for half in (0, 128):
+                side = pl.ds(pl.multiple_of(tile * KEYS + half, 128), 128)
+                scores = scored[:, side]
                 scores = jnp.concatenate(
-                    [scores[slot * ROWS : (slot + 1) * ROWS] + bias[i * 8 + slot] for slot in range(8)], axis=0
+                    [scores[slot * ROWS : (slot + 1) * ROWS] + shown[slot] for slot in range(8)], axis=0
                 )
-            old = peak[:, side]
-            new = jnp.maximum(old, jnp.max(scores, axis=0, keepdims=True) * scale)
-            weights = jnp.exp(scores * scale - new)
-            shrink = jnp.exp(old - new)
-            peak[:, side] = new
-            factor[:, side] = shrink
-            total[:, side] = shrink * total[:, side] + jnp.sum(weights, axis=0, keepdims=True)
-            weighed[:, side] = weights.astype(jnp.bfloat16)
+                old = peak[:, side]
+                new = jnp.maximum(old, jnp.max(scores, axis=0, keepdims=True) * scale)
+                weights = jnp.exp(scores * scale - new)
+                shrink = jnp.exp(old - new)
+                peak[:, side] = new
+                factor[:, side] = shrink
+                total[:, side] = shrink * total[:, side] + jnp.sum(weights, axis=0, keepdims=True)
+                weighed[:, side] = weights.astype(jnp.bfloat16)
+
+        loop(0, GROUP, softmax)
         values = [kv[i, 1, n].reshape(KEYS, HEAD_DIM) for n in (0, 1)]
         added = [
             lax.dot_general(
@@ -219,18 +240,19 @@
         for n in (0, 1):
             summed[:, spans[n]] = factor[:, spans[n]] * summed[:, spans[n]] + added[n]
 
+    def tile_columns(h):
+        return pl.ds(pl.multiple_of(h * KEYS, 128), KEYS)
+
     def finish(h):
-        tile = slice(h * KEYS, (h + 1) * KEYS)
-        result = summed[:, tile] * (1.0 / total[:, tile])
+        result = summed[:, tile_columns(h)] * (1.0 / total[:, tile_columns(h)])
         attended[h] = result.T.astype(jnp.bfloat16).reshape(8, ROWS, HEAD_DIM)
-        for j in range(8):
-            back(h, j).start()
-
-    def turn_query(h, rows):
-        tile = slice(h * KEYS, (h + 1) * KEYS)
-        turned[:, tile] = rows.reshape(KEYS, HEAD_DIM).astype(jnp.float32).T.astype(jnp.bfloat16)
-
-    def turn(t, carry):
+        loop(0, 8, lambda j: back(h, j).start())
+
+    def turn_query(h):
+        rows = row_query[h].reshape(KEYS, HEAD_DIM)
+        turned[:, tile_columns(h)] = rows.astype(jnp.float32).T.astype(jnp.bfloat16)
+
+    def turn(t):
         @pl.when((t >= 2) & (t < X_CHUNKS + 2))
         def _():
             i = t - 2
@@ -241,7 +263,7 @@
             x_copy(i, 3).wait_recv()
             x_copy(i, 6).start()
 
-        @pl.when(t >= 3)
+        @pl.when((t >= 3) & (t < X_CHUNKS + 3))
         def _():
             i = t - 3
             for copy in own_copies(i):
@@ -253,22 +275,19 @@
         @pl.when(t == 3)
         def _():
             own_query.wait()
-            for j in range(1, 8):
-                query_over_z(j).wait_recv()
-            for n in range(3):
-                query_over_x(n).start()
+            loop(1, 8, lambda j: query_over_z(j).wait_recv())
+            loop(1, 4, lambda n: query_over_x(n).start())
+            for copy in own_query_copies():
+                copy.start()
 
         @pl.when(t == 4)
         def _():
             y_copy(0).start()
             y_copy(1).start()
-            turn_query(0, query[:, :, of_head(x)])
-            turn_query(4, query[:, :, shared])
-            for n in range(3):
-                query_over_x(n).wait_recv()
-            turn_query(1, row_query[0])
-            turn_query(2, row_query[1])
-            turn_query(3, row_query[2])
+            for copy in own_query_copies():
+                copy.wait()
+            loop(1, 4, lambda n: query_over_x(n).wait_recv())
+            loop(0, GROUP, turn_query)
 
         @pl.when(t == 7)
         def _():
@@ -287,19 +306,14 @@
         def _():
             x_copy(t - 4, 7).wait_recv()
 
-        @pl.when((t >= 4) & (t != 5))
-        def _():
-            attend(t - 4, False)
-
         for i in (9, 10, 11):
 
             @pl.when(t == i)
             def _(i=i):
                 y_copy(i - 5).wait_recv()
 
-        @pl.when((t == 5) | (t >= 9))
-        def _():
-            attend(jnp.where(t == 5, 1, t), True)
+        ready = jnp.where(t < 4, 0, jnp.where((t >= 9) & (t <= 11), 2, 1))
+        loop(0, ready, lambda n: attend(jnp.where(n == 0, t - 4, t)))
 
         @pl.when(t < X_CHUNKS)
         def _():
@@ -311,57 +325,47 @@
             for copy in own_copies(t):
                 copy.start()
 
-        for turn_of, hops in ((1, (5, 6)), (3, (7,))):
-
-            @pl.when(t == turn_of)
-            def _(hops=hops):
-                for j in hops:
-                    start_kv(j)
-
+        pl.when(t == 1)(lambda: loop(5, 7, start_kv))
+        pl.when(t == 3)(lambda: start_kv(7))
         pl.when(t == 1)(prepare)
-        return carry
-
-    lax.fori_loop(0, X_CHUNKS + 3, turn, 0)
-    x_copy(X_CHUNKS - 1, 7).wait_recv()
-    attend(X_CHUNKS - 1, False)
-    for h in range(GROUP):
-        finish(h)
+
+    loop(0, X_CHUNKS + 4, turn)
+    loop(0, GROUP, finish)
 
     @pl.when(core != zh)
     def _():
         cache_across(0).wait_send()
         cache_across(1).wait_send()
 
-    for j in range(1, 8):
+    @functools.partial(loop, 1, 8)
+    def _(j):
         query_over_z(j).wait_send()
         kv_over_z(j, 0).wait_send()
         kv_over_z(j, 1).wait_send()
 
-    def sent(i, carry):
+    @functools.partial(loop, 0, X_CHUNKS)
+    def _(i):
         for n in range(8):
             x_copy(i, n).wait_send()
-        return carry
-
-    lax.fori_loop(0, X_CHUNKS, sent, 0)
+
     for n in range(8):
         y_copy(n).wait_send()
-    for n in range(3):
-        query_over_x(n).wait_send()
+    loop(1, 4, lambda n: query_over_x(n).wait_send())
 
     y_copy(7).wait_recv()
-    for tile in range(GROUP):
-        for j in range(8):
-            back(tile, j).wait_recv()
-            of = GROUP - 1 if tile == GROUP - 1 else (x + tile) % 4
-            first = group_of((z + HOPS[j]) % 8) * WIDTH + of * HEAD_DIM
-            columns = pl.ds(pl.multiple_of(first, 128), HEAD_DIM)
-            out[:, columns] = (
-                shifted[:, columns].astype(jnp.float32)
-                + gate[0:1, columns] * returned[tile, j].astype(jnp.float32)
-            ).astype(jnp.bfloat16)
-    for tile in range(GROUP):
-        for j in range(8):
-            back(tile, j).wait_send()
+
+    @functools.partial(loop, 0, GROUP * 8)
+    def _(n):
+        tile, j = n // 8, n % 8
+        back(tile, j).wait_recv()
+        of = jnp.where(tile == GROUP - 1, GROUP - 1, (x + tile) % 4)
+        first = group_of((z + hop_of(j)) % 8) * WIDTH + of * HEAD_DIM
+        columns = pl.ds(pl.multiple_of(first, 128), HEAD_DIM)
+        out[:, columns] = (
+            shifted[:, columns].astype(jnp.float32) + gate[0:1, columns] * returned[tile, j].astype(jnp.float32)
+        ).astype(jnp.bfloat16)
+
+    loop(0, GROUP * 8, lambda n: back(n // 8, n % 8).wait_send())
 
 
 def shards(
@@ -378,7 +382,7 @@
         out_specs=pl.BlockSpec(memory_space=pltpu.VMEM),
         scratch_shapes=[
             pltpu.VMEM((8, ROWS, WIDTH), bf16),
-            pltpu.VMEM((3, 8, ROWS, HEAD_DIM), bf16),
+            pltpu.VMEM((5, 8, ROWS, HEAD_DIM), bf16),
             pltpu.VMEM((HEAD_DIM, GROUP * KEYS), bf16),
             pltpu.VMEM((X_CHUNKS, 2, ROWS, WIDTH), bf16),
             pltpu.VMEM((CHUNKS, 2, 2, 8, ROWS, HEAD_DIM), bf16),
@@ -397,13 +401,13 @@
             dma((8, 3)),
             dma((X_CHUNKS, 8)),
             dma((8,)),
-            dma((3,)),
+            dma((5,)),
             dma((GROUP, 8)),
             dma((8,)),
             dma((X_CHUNKS, 2)),
             dma((X_CHUNKS, 8)),
             dma((8,)),
-            dma((3,)),
+            dma((5,)),
             dma((GROUP, 8)),
             dma((1,)),
             dma((X_CHUNKS, 2)),

time: 65.4 us -> 69 us (1.055)
  the two profiles are of different devices: /device:TPU:1 before, /device:TPU:8 now
where the time goes in v17:
time: 69 us; the launch traced here: 68.9 us
  Pallas kernels  67.1 us (97%)
  local copies, waits for them, and re-layouts  1.72 us (2%)
    pallas_call x1, Pallas kernels, shards(): pl.pallas_call(kernel, out_shape=jax.ShapeDtypeStruct(latent.shape, laten...  67.1 us
    unnamed x1, local copies, waits for them, and re-layouts  1.72 us

profile of v17, /device:TPU:8, one launch (start us, length us, event | category | flops | bytes accessed | tf_op | source)
XLA Modules:
  0.0 68.9 jit_solution(12412391786185916654)
XLA Ops:
  0.0 67.1 %shard_map.100 = bf16[32,5120]{1,0:T(8,128)(2,1)} custom-call(s32[4]{0:T(128)} %levels.1, s32[50]{0:T(128)} %timesteps.1, s32[4,32]{1,0:T(4,128)} %cache_mask.1, bf16[32,5120]{1,0:T(8,128)(2,1)} %latent.1, bf16[32,5120]{1,0:T(8,128)(2,1)} %query_in.1, bf16[32,5120]{1,0:T(8,128)(2,1)} %key_in.1, bf16[32,5120]{1,0:T(8,128)(2,1)} %value_in.1, ...), custom_call_target="tpu_custom_call" | custom-call | flops 2000000000 | bytes 5000000 | tf_op jit(solution)/shard_map/pallas_call | solution.py:378
  67.1 1.7 %copy.12 = bf16[32,5120]{1,0:T(8,128)(2,1)} copy(bf16[32,5120]{1,0:T(8,128)(2,1)} %shard_map.100) | data formatting | bytes 655360

commit v18 on v16

--- a/solution.py
+++ b/solution.py
@@ -20,6 +20,9 @@
 FIRST_Z = 2
 X_CHUNKS = 9
 KEYS = 8 * ROWS
+LOG2E = 1.4426950408889634
+ATTEND = (0, 1, 9, 10, 2, 3, 11, 4, 5, 6, 7, 8)
+PLACE = tuple(ATTEND.index(i) for i in range(CHUNKS))
 HIDDEN = -1e30
 
 
@@ -108,33 +111,36 @@
 
     shared = slice((GROUP - 1) * HEAD_DIM, GROUP * HEAD_DIM)
 
+    def chunk(i):
+        return kv.at[PLACE[i]]
+
     def own_copies(i):
         return (
-            pltpu.make_async_copy(landed.at[i, :, :, of_head(x)], kv.at[i, :, 0, 0], own_x.at[i, 0]),
-            pltpu.make_async_copy(landed.at[i, :, :, shared], kv.at[i, :, 1, 0], own_x.at[i, 1]),
+            pltpu.make_async_copy(landed.at[i, :, :, of_head(x)], chunk(i).at[:, 0, 0], own_x.at[i, 0]),
+            pltpu.make_async_copy(landed.at[i, :, :, shared], chunk(i).at[:, 1, 0], own_x.at[i, 1]),
         )
 
     def x_copy(i, n):
         src, dst, to = (
-            lambda: (landed.at[i, :, :, of_head(x_right)], kv.at[i, :, 0, 1], right),
-            lambda: (landed.at[i, :, :, shared], kv.at[i, :, 1, 1], right),
-            lambda: (landed.at[i, :, :, of_head(x_left)], kv.at[i, :, 0, 3], left),
-            lambda: (landed.at[i, :, :, shared], kv.at[i, :, 1, 3], left),
-            lambda: (landed.at[i, :, :, of_head(x_far)], kv.at[i, :, 0, 2], far),
-            lambda: (landed.at[i, :, :, shared], kv.at[i, :, 1, 2], far),
-            lambda: (kv.at[i, :, :, 0:4], kv.at[i, :, :, 4:8], sibling),
+            lambda: (landed.at[i, :, :, of_head(x_right)], chunk(i).at[:, 0, 1], right),
+            lambda: (landed.at[i, :, :, shared], chunk(i).at[:, 1, 1], right),
+            lambda: (landed.at[i, :, :, of_head(x_left)], chunk(i).at[:, 0, 3], left),
+            lambda: (landed.at[i, :, :, shared], chunk(i).at[:, 1, 3], left),
+            lambda: (landed.at[i, :, :, of_head(x_far)], chunk(i).at[:, 0, 2], far),
+            lambda: (landed.at[i, :, :, shared], chunk(i).at[:, 1, 2], far),
+            lambda: (chunk(i).at[:, :, 0:4], chunk(i).at[:, :, 4:8], sibling),
         )[n]()
         return remote(src, dst, send_x.at[i, n], recv_x.at[i, n], to)
 
     def y_copy(n):
         src, dst, to = (
-            lambda: (kv.at[1, :, :, 0:4], kv.at[9, :, :, 0:4], to_up),
-            lambda: (kv.at[1, :, :, 0:4], kv.at[10, :, :, 0:4], to_down),
-            lambda: (kv.at[9, 0, :, 0:4], kv.at[11, 0, :, 0:4], to_up),
-            lambda: (kv.at[10, 1, :, 0:4], kv.at[11, 1, :, 0:4], to_down),
-            lambda: (kv.at[9, :, :, 0:4], kv.at[9, :, :, 4:8], sibling),
-            lambda: (kv.at[10, :, :, 0:4], kv.at[10, :, :, 4:8], sibling),
-            lambda: (kv.at[11, :, :, 0:4], kv.at[11, :, :, 4:8], sibling),
+            lambda: (chunk(1).at[:, :, 0:4], chunk(9).at[:, :, 0:4], to_up),
+            lambda: (chunk(1).at[:, :, 0:4], chunk(10).at[:, :, 0:4], to_down),
+            lambda: (chunk(9).at[0, :, 0:4], chunk(11).at[0, :, 0:4], to_up),
+            lambda: (chunk(10).at[1, :, 0:4], chunk(11).at[1, :, 0:4], to_down),
+            lambda: (chunk(9).at[:, :, 0:4], chunk(9).at[:, :, 4:8], sibling),
+            lambda: (chunk(10).at[:, :, 0:4], chunk(10).at[:, :, 4:8], sibling),
+            lambda: (chunk(11).at[:, :, 0:4], chunk(11).at[:, :, 4:8], sibling),
             lambda: (latent, shifted, to_down),
         )[n]()
         return remote(src, dst, send_y.at[n], recv_y.at[n], to)
@@ -160,9 +166,7 @@
         cache_across(0).start()
         cache_across(1).start()
 
-    start_kv(1)
-    start_kv(2)
-    for j in range(1, 8):
+    for j in reversed(range(1, 8)):
         query_over_z(j).start()
     y_copy(7).start()
 
@@ -175,9 +179,9 @@
                     plane = {1: y, 9: down, 10: up, 11: (y + 2) % 4}[i]
                     side = core if slot < 4 else 1 - core
                     block = plane * 8 + side * 4 + (x + (0, 3, 2, 1)[slot % 4]) % 4
-                    bias[i * 8 + slot] = jnp.where(cache_mask[y, block] == 1, 0.0, HIDDEN).astype(jnp.float32)
+                    bias[PLACE[i] * 8 + slot] = jnp.where(cache_mask[y, block] == 1, 0.0, HIDDEN).astype(jnp.float32)
                 else:
-                    bias[i * 8 + slot] = jnp.float32(0.0)
+                    bias[PLACE[i] * 8 + slot] = jnp.float32(0.0)
 
         stamp = timesteps[levels[up]].astype(jnp.float32)
         count = 128
@@ -197,130 +201,152 @@
         total[...] = jnp.zeros_like(total)
         summed[...] = jnp.zeros_like(summed)
 
-    def attend(i, cached):
-        scale = 1.0 / math.sqrt(HEAD_DIM)
-        spans = (slice(0, 4 * KEYS), slice(4 * KEYS, 5 * KEYS))
-        keys = [kv[i, 0, n].reshape(KEYS, HEAD_DIM) for n in (0, 1)]
+    scale = LOG2E / math.sqrt(HEAD_DIM)
+    spans = (slice(0, 4 * KEYS), slice(4 * KEYS, 5 * KEYS))
+
+    def score(c):
+        keys = [kv[c, 0, n].reshape(KEYS, HEAD_DIM) for n in (0, 1)]
         scores = [jnp.dot(keys[n], turned[:, spans[n]], preferred_element_type=jnp.float32) for n in (0, 1)]
         for n in (0, 1):
             scored[:, spans[n]] = scores[n]
-        for first in range(0, GROUP * KEYS, 128):
+
+    def softmax(c, lower, upper, cached):
+        for first in range(lower, upper, 128):
             side = slice(first, first + 128)
             scores = scored[:, side]
             if cached:
                 scores = jnp.concatenate(
-                    [scores[slot * ROWS : (slot + 1) * ROWS] + bias[i * 8 + slot] for slot in range(8)], axis=0
+                    [scores[slot * ROWS : (slot + 1) * ROWS] + bias[c * 8 + slot] for slot in range(8)], axis=0
                 )
             old = peak[:, side]
             new = jnp.maximum(old, jnp.max(scores, axis=0, keepdims=True) * scale)
-            weights = jnp.exp(scores * scale - new)
-            shrink = jnp.exp(old - new)
+            weights = jnp.exp2(scores * scale - new)
+            shrink = jnp.exp2(old - new)
             peak[:, side] = new
             factor[:, side] = shrink
             total[:, side] = shrink * total[:, side] + jnp.sum(weights, axis=0, keepdims=True)
             weighed[:, side] = weights.astype(jnp.bfloat16)
-        values = [kv[i, 1, n].reshape(KEYS, HEAD_DIM) for n in (0, 1)]
-        added = [
-            lax.dot_general(
-                values[n], weighed[:, spans[n]], (((0,), (0,)), ((), ())), preferred_element_type=jnp.float32
-            )
-            for n in (0, 1)
-        ]
+
+    def add_values(values, columns):
+        added = lax.dot_general(
+            values, weighed[:, columns], (((0,), (0,)), ((), ())), preferred_element_type=jnp.float32
+        )
+        return factor[:, columns] * summed[:, columns] + added
+
+    def attend(c, cached):
+        score(c)
+        softmax(c, 0, GROUP * KEYS, cached)
+        values = [kv[c, 1, n].reshape(KEYS, HEAD_DIM) for n in (0, 1)]
+        sums = [add_values(values[n], spans[n]) for n in (0, 1)]
         for n in (0, 1):
-            summed[:, spans[n]] = factor[:, spans[n]] * summed[:, spans[n]] + added[n]
-
-    def finish(h):
-        tile = slice(h * KEYS, (h + 1) * KEYS)
-        result = summed[:, tile] * (1.0 / total[:, tile])
-        attended[h] = result.T.astype(jnp.bfloat16).reshape(8, ROWS, HEAD_DIM)
-        for j in range(8):
-            back(h, j).start()
+            summed[:, spans[n]] = sums[n]
+
+    def attend_last(c):
+        score(c)
+        values = [kv[c, 1, n].reshape(KEYS, HEAD_DIM) for n in (0, 1)]
+        for h in range(GROUP):
+            tile = slice(h * KEYS, (h + 1) * KEYS)
+            softmax(c, h * KEYS, (h + 1) * KEYS, False)
+            result = add_values(values[h // (GROUP - 1)], tile) * (1.0 / total[:, tile])
+            attended[h] = result.T.astype(jnp.bfloat16).reshape(8, ROWS, HEAD_DIM)
+            for j in reversed(range(8)):
+                back(h, j).start()
 
     def turn_query(h, rows):
         tile = slice(h * KEYS, (h + 1) * KEYS)
         turned[:, tile] = rows.reshape(KEYS, HEAD_DIM).astype(jnp.float32).T.astype(jnp.bfloat16)
 
-    def turn(t, carry):
-        @pl.when(t >= 2)
-        def _():
-            i = t - 2
+    def arrived(*items):
+        for i in items:
+            for which in (0, 1):
+                place = landed.at[i, which]
+                pltpu.make_async_copy(place, place, recv_kv.at[i, which]).wait()
+            for n in range(6):
+                x_copy(i, n).start()
+            for copy in own_copies(i):
+                copy.start()
+
+    def gathered(*items):
+        for i in items:
             for copy in own_copies(i):
                 copy.wait()
             for n in range(6):
                 x_copy(i, n).wait_recv()
             x_copy(i, 6).start()
 
-        @pl.when(t == 3)
-        def _():
+    def complete(i):
+        if i >= X_CHUNKS:
+            y_copy(i - 5).wait_recv()
+        else:
+            x_copy(i, 6).wait_recv()
+
+    def before(c):
+        if c == 0:
+            arrived(0)
+            prepare()
+            arrived(1)
+            gathered(0, 1)
             y_copy(0).start()
             y_copy(1).start()
-
-        @pl.when(t == 4)
-        def _():
+            for j in (1, 2, 3, 4):
+                query_over_z(j).wait_recv()
+            start_kv(1)
+            start_kv(2)
             own_query.wait()
-            for j in range(1, 8):
+            for j in (5, 6, 7):
                 query_over_z(j).wait_recv()
             for n in range(3):
                 query_over_x(n).start()
+            for j in (3, 4, 5, 6):
+                start_kv(j)
+            turn_query(0, query[:, :, of_head(x)])
+            turn_query(4, query[:, :, shared])
             for n in (0, 1):
                 y_copy(n).wait_recv()
                 y_copy(n + 2).start()
                 y_copy(n + 4).start()
-            turn_query(0, query[:, :, of_head(x)])
-            turn_query(4, query[:, :, shared])
             for n in range(3):
                 query_over_x(n).wait_recv()
             for n in range(3):
                 turn_query(n + 1, row_query[n])
-            x_copy(0, 6).wait_recv()
-
-        @pl.when(t >= 4)
-        def _():
-            x_copy(t - 3, 6).wait_recv()
-
-        for i in (9, 10, 11):
-
-            @pl.when(t == i - 4)
-            def _(i=i):
-                if i == 9:
-                    y_copy(2).wait_recv()
-                    y_copy(3).wait_recv()
-                    y_copy(6).start()
-                y_copy(i - 5).wait_recv()
-
-        @pl.when(t >= 4)
-        def _():
-            attend(jnp.where(t == 4, 0, t - 3), False)
-
-        @pl.when((t >= 4) & (t <= 7))
-        def _():
-            attend(jnp.where(t == 4, 1, t + 4), True)
-
-        @pl.when(t < X_CHUNKS)
-        def _():
-            for which in (0, 1):
-                place = landed.at[t, which]
-                pltpu.make_async_copy(place, place, recv_kv.at[t, which]).wait()
-            for n in range(6):
-                x_copy(t, n).start()
-            for copy in own_copies(t):
-                copy.start()
-
-        for turn_of, hops in ((1, (3, 4)), (2, (5, 6)), (3, (7,))):
-
-            @pl.when(t == turn_of)
-            def _(hops=hops):
-                for j in hops:
-                    start_kv(j)
-
-        pl.when(t == 3)(prepare)
+        if c == 1:
+            arrived(2, 3)
+        if c == 2:
+            start_kv(7)
+            y_copy(2).wait_recv()
+            y_copy(3).wait_recv()
+            y_copy(6).start()
+        if c == 3:
+            gathered(2, 3)
+        if c == 5:
+            arrived(4, 5)
+        if c == 6:
+            gathered(4)
+        if c == 7:
+            gathered(5)
+            arrived(6)
+        if c == 8:
+            arrived(7)
+        if c == 9:
+            gathered(6, 7)
+            arrived(8)
+        if c == 11:
+            gathered(8)
+        complete(ATTEND[c])
+
+    def turn(c, carry):
+        cached = False
+        for now in range(CHUNKS - 1):
+            pl.when(c == now)(functools.partial(before, now))
+            if ATTEND[now] == 1 or ATTEND[now] >= X_CHUNKS:
+                cached = cached | (c == now)
+        pl.when(cached)(functools.partial(attend, c, True))
+        pl.when(jnp.logical_not(cached))(functools.partial(attend, c, False))
         return carry
 
-    lax.fori_loop(0, X_CHUNKS + 2, turn, 0)
-    x_copy(X_CHUNKS - 1, 6).wait_recv()
-    attend(X_CHUNKS - 1, False)
-    for h in range(GROUP):
-        finish(h)
+    lax.fori_loop(0, CHUNKS - 1, turn, 0)
+    before(CHUNKS - 1)
+    attend_last(CHUNKS - 1)
 
     @pl.when(core != zh)
     def _():
@@ -332,12 +358,9 @@
         kv_over_z(j, 0).wait_send()
         kv_over_z(j, 1).wait_send()
 
-    def sent(i, carry):
+    for i in range(X_CHUNKS):
         for n in range(7):
             x_copy(i, n).wait_send()
-        return carry
-
-    lax.fori_loop(0, X_CHUNKS, sent, 0)
     for n in range(8):
         y_copy(n).wait_send()
     for n in range(3):

time: 66.5 us -> 65.9 us (level)
  no operation moved by 1% of the time
where the time goes in v18:
time: 65.9 us; the launch traced here: 65.8 us
  Pallas kernels  63.9 us (97%)
  other arithmetic  1.9 us (3%)
    pallas_call x1, Pallas kernels, shards(): pl.pallas_call(kernel, out_shape=(jax.ShapeDtypeStruct(latent.shape, bf16...  63.9 us
    convert_element_type x1, other arithmetic, shards(): return (shifted.astype(f32) + gate * returned.astype(f32)).astype(bf16)  1.9 us

profile of v18, /device:TPU:1, one launch (start us, length us, event | category | flops | bytes accessed | tf_op | source)
XLA Modules:
  0.0 65.8 jit_solution(16066407162438337558)
XLA Ops:
  0.0 63.9 %shard_map.100 = (bf16[32,5120]{1,0:T(8,128)(2,1)}, bf16[32,5120]{1,0:T(8,128)(2,1)}, f32[1,5120]{1,0:T(1,128)}) custom-call(s32[4]{0:T(128)} %levels_in.1, s32[50]{0:T(128)} %timesteps_in.1, s32[4,32]{1,0:T(4,128)} %mask_in.1, bf16[32,5120]{1,0:T(8,128)(2,1)} %latent.1, bf16[32,5120]{1,0:T(8,128)(2,1)} %query_in.1, bf16[32,5120]{1,0:T(8,128)(2,1)} %key_in.1, ...), custom_call_target="tpu_custom_call" | custom-call | flops 2000000000 | bytes 5000000 | tf_op jit(solution)/shard_map/pallas_call | solution.py:384
  63.9 1.9 %add_convert_fusion = bf16[32,5120]{1,0:T(8,128)(2,1)} fusion(bf16[32,5120]{1,0:T(8,128)(2,1)} %get-tuple-element.10, bf16[32,5120]{1,0:T(8,128)(2,1)} %get-tuple-element.8, f32[5120]{0:T(1024)} %bitcast.1), kind=kLoop, calls=%fused_computation | loop fusion | flops 819200 | bytes 1003520 | tf_op jit(solution)/shard_map/convert_element_type | solution.py:432

commit v19 on v18

--- a/solution.py
+++ b/solution.py
@@ -202,55 +202,62 @@
         summed[...] = jnp.zeros_like(summed)
 
     scale = LOG2E / math.sqrt(HEAD_DIM)
-    spans = (slice(0, 4 * KEYS), slice(4 * KEYS, 5 * KEYS))
-
-    def score(c):
+
+    def attend(c, cached, last=False):
+        def tile_of(h):
+            return slice(h * KEYS, (h + 1) * KEYS)
+
         keys = [kv[c, 0, n].reshape(KEYS, HEAD_DIM) for n in (0, 1)]
-        scores = [jnp.dot(keys[n], turned[:, spans[n]], preferred_element_type=jnp.float32) for n in (0, 1)]
-        for n in (0, 1):
-            scored[:, spans[n]] = scores[n]
-
-    def softmax(c, lower, upper, cached):
-        for first in range(lower, upper, 128):
-            side = slice(first, first + 128)
-            scores = scored[:, side]
-            if cached:
-                scores = jnp.concatenate(
-                    [scores[slot * ROWS : (slot + 1) * ROWS] + bias[c * 8 + slot] for slot in range(8)], axis=0
+        values = [kv[c, 1, n].reshape(KEYS, HEAD_DIM) for n in (0, 1)]
+
+        def score(h):
+            if h < GROUP:
+                scored[:, tile_of(h)] = jnp.dot(
+                    keys[h // (GROUP - 1)], turned[:, tile_of(h)], preferred_element_type=jnp.float32
                 )
-            old = peak[:, side]
-            new = jnp.maximum(old, jnp.max(scores, axis=0, keepdims=True) * scale)
-            weights = jnp.exp2(scores * scale - new)
-            shrink = jnp.exp2(old - new)
-            peak[:, side] = new
-            factor[:, side] = shrink
-            total[:, side] = shrink * total[:, side] + jnp.sum(weights, axis=0, keepdims=True)
-            weighed[:, side] = weights.astype(jnp.bfloat16)
-
-    def add_values(values, columns):
-        added = lax.dot_general(
-            values, weighed[:, columns], (((0,), (0,)), ((), ())), preferred_element_type=jnp.float32
-        )
-        return factor[:, columns] * summed[:, columns] + added
-
-    def attend(c, cached):
-        score(c)
-        softmax(c, 0, GROUP * KEYS, cached)
-        values = [kv[c, 1, n].reshape(KEYS, HEAD_DIM) for n in (0, 1)]
-        sums = [add_values(values[n], spans[n]) for n in (0, 1)]
-        for n in (0, 1):
-            summed[:, spans[n]] = sums[n]
-
-    def attend_last(c):
-        score(c)
-        values = [kv[c, 1, n].reshape(KEYS, HEAD_DIM) for n in (0, 1)]
-        for h in range(GROUP):
-            tile = slice(h * KEYS, (h + 1) * KEYS)
-            softmax(c, h * KEYS, (h + 1) * KEYS, False)
-            result = add_values(values[h // (GROUP - 1)], tile) * (1.0 / total[:, tile])
+
+        def softmax(h):
+            for first in (h * KEYS, h * KEYS + 128):
+                side = slice(first, first + 128)
+                scores = scored[:, side]
+                if cached:
+                    scores = jnp.concatenate(
+                        [scores[slot * ROWS : (slot + 1) * ROWS] + bias[c * 8 + slot] for slot in range(8)], axis=0
+                    )
+                old = peak[:, side]
+                new = jnp.maximum(old, jnp.max(scores, axis=0, keepdims=True) * scale)
+                weights = jnp.exp2(scores * scale - new)
+                shrink = jnp.exp2(old - new)
+                peak[:, side] = new
+                factor[:, side] = shrink
+                total[:, side] = shrink * total[:, side] + jnp.sum(weights, axis=0, keepdims=True)
+                weighed[:, side] = weights.astype(jnp.bfloat16)
+
+        def add_values(h):
+            tile = tile_of(h)
+            added = lax.dot_general(
+                values[h // (GROUP - 1)],
+                weighed[:, tile],
+                (((0,), (0,)), ((), ())),
+                preferred_element_type=jnp.float32,
+            )
+            sums = factor[:, tile] * summed[:, tile] + added
+            if not last:
+                summed[:, tile] = sums
+                return
+            result = sums * (1.0 / total[:, tile])
             attended[h] = result.T.astype(jnp.bfloat16).reshape(8, ROWS, HEAD_DIM)
             for j in reversed(range(8)):
                 back(h, j).start()
+
+        score(0)
+        score(1)
+        for h in range(GROUP):
+            softmax(h)
+            score(h + 2)
+            if h:
+                add_values(h - 1)
+        add_values(GROUP - 1)
 
     def turn_query(h, rows):
         tile = slice(h * KEYS, (h + 1) * KEYS)
@@ -297,22 +304,21 @@
                 query_over_z(j).wait_recv()
             for n in range(3):
                 query_over_x(n).start()
-            for j in (3, 4, 5, 6):
+            for j in (3, 4, 5, 6, 7):
                 start_kv(j)
             turn_query(0, query[:, :, of_head(x)])
             turn_query(4, query[:, :, shared])
-            for n in (0, 1):
-                y_copy(n).wait_recv()
-                y_copy(n + 2).start()
-                y_copy(n + 4).start()
             for n in range(3):
                 query_over_x(n).wait_recv()
             for n in range(3):
                 turn_query(n + 1, row_query[n])
         if c == 1:
+            for n in (0, 1):
+                y_copy(n).wait_recv()
+                y_copy(n + 2).start()
+                y_copy(n + 4).start()
             arrived(2, 3)
-        if c == 2:
-            start_kv(7)
+        if c == 3:
             y_copy(2).wait_recv()
             y_copy(3).wait_recv()
             y_copy(6).start()
@@ -346,7 +352,7 @@
 
     lax.fori_loop(0, CHUNKS - 1, turn, 0)
     before(CHUNKS - 1)
-    attend_last(CHUNKS - 1)
+    attend(CHUNKS - 1, False, True)
 
     @pl.when(core != zh)
     def _():

time: 65.9 us -> 66 us (level)
  no operation moved by 1% of the time
where the time goes in v19:
time: 66 us; the launch traced here: 65.9 us
  Pallas kernels  64 us (97%)
  other arithmetic  1.9 us (3%)
    pallas_call x1, Pallas kernels, shards(): pl.pallas_call(kernel, out_shape=(jax.ShapeDtypeStruct(latent.shape, bf16...  64 us
    convert_element_type x1, other arithmetic, shards(): return (shifted.astype(f32) + gate * returned.astype(f32)).astype(bf16)  1.9 us

profile of v19, /device:TPU:1, one launch (start us, length us, event | category | flops | bytes accessed | tf_op | source)
XLA Modules:
  0.0 65.9 jit_solution(4314484796334329486)
XLA Ops:
  0.0 64.0 %shard_map.100 = (bf16[32,5120]{1,0:T(8,128)(2,1)}, bf16[32,5120]{1,0:T(8,128)(2,1)}, f32[1,5120]{1,0:T(1,128)}) custom-call(s32[4]{0:T(128)} %levels_in.1, s32[50]{0:T(128)} %timesteps_in.1, s32[4,32]{1,0:T(4,128)} %mask_in.1, bf16[32,5120]{1,0:T(8,128)(2,1)} %latent.1, bf16[32,5120]{1,0:T(8,128)(2,1)} %query_in.1, bf16[32,5120]{1,0:T(8,128)(2,1)} %key_in.1, ...), custom_call_target="tpu_custom_call" | custom-call | flops 2000000000 | bytes 5000000 | tf_op jit(solution)/shard_map/pallas_call | solution.py:390
  64.0 1.9 %add_convert_fusion = bf16[32,5120]{1,0:T(8,128)(2,1)} fusion(bf16[32,5120]{1,0:T(8,128)(2,1)} %get-tuple-element.10, bf16[32,5120]{1,0:T(8,128)(2,1)} %get-tuple-element.8, f32[5120]{0:T(1024)} %bitcast.1), kind=kLoop, calls=%fused_computation | loop fusion | flops 819200 | bytes 1003520 | tf_op jit(solution)/shard_map/convert_element_type | solution.py:438

commit v20 on v19

--- a/solution.py
+++ b/solution.py
@@ -20,6 +20,7 @@
 FIRST_Z = 2
 X_CHUNKS = 9
 KEYS = 8 * ROWS
+RELAYED = 2
 LOG2E = 1.4426950408889634
 ATTEND = (0, 1, 9, 10, 2, 3, 11, 4, 5, 6, 7, 8)
 PLACE = tuple(ATTEND.index(i) for i in range(CHUNKS))
@@ -41,9 +42,9 @@
 def kernel(
     levels_in, timesteps_in, mask_in, latent, query_in, key_in, value_in, cache_keys, cache_values, time_weight,
     returned, shifted, gate,
-    levels, timesteps, cache_mask, query, row_query, turned, landed, kv, attended, weight,
+    levels, timesteps, cache_mask, query, row_query, turned, landed, relay, relay_o, kv, attended, weight,
     scored, weighed, factor, peak, total, summed, bias,
-    send_z, send_x, send_y, send_q, send_o, recv_q, recv_kv, recv_x, recv_y, recv_rq, recv_o, local, own_x,
+    send_z, send_x, send_y, send_q, send_o, recv_q, recv_kv, recv_relay, recv_x, recv_y, recv_rq, recv_o, local, own_x,
 ):
     chain, head = lax.axis_index("chain"), lax.axis_index("head")
     y, x = chain // 8, chain % 4
@@ -55,6 +56,7 @@
     sibling = device(y, z, x, 1 - core)
     across = device(y, (z + 4) % 8, x, 1 - core)
     to_up, to_down = device(up, z, x, core), device(down, z, x, core)
+    on_two = device(y, (z + 2) % 8, x, core)
     mine = group_columns(z)
 
     def remote(src, dst, send, recv, to):
@@ -105,9 +107,14 @@
     def kv_over_z(j, which):
         to = (z + HOPS[j]) % 8
         source = (key_in, value_in)[which].at[:, group_columns(to)]
+        if HOPS[j] == 4:
+            return remote(source, relay.at[which], send_z.at[j, which], recv_relay.at[which], on_two)
         return remote(
             source, landed.at[j + 1, which], send_z.at[j, which], recv_kv.at[j + 1, which], device(y, to, x, core)
         )
+
+    def relay_on(which):
+        return remote(relay.at[which], landed.at[8, which], send_z.at[8, which], recv_kv.at[8, which], on_two)
 
     shared = slice((GROUP - 1) * HEAD_DIM, GROUP * HEAD_DIM)
 
@@ -153,9 +160,17 @@
 
     def back(tile, j):
         to_x, of = (x, GROUP - 1) if tile == GROUP - 1 else ((x + (0, 3, 2, 1)[tile]) % 4, x)
+        if HOPS[j] == 4 and tile < RELAYED:
+            to = device(down, (z + 2) % 8, to_x, core)
+            return remote(attended.at[tile, j], relay_o.at[tile], send_o.at[tile, j], recv_relay.at[2 + tile], to)
         to = device(down, (z - HOPS[j] + 8) % 8, to_x, core)
         columns = pl.ds(pl.multiple_of(group_of(z) * WIDTH + of * HEAD_DIM, 128), HEAD_DIM)
         return remote(attended.at[tile, j], returned.at[:, columns], send_o.at[tile, j], recv_o.at[tile, j], to)
+
+    def back_on(tile):
+        first = group_of((z + 6) % 8) * WIDTH + (x + tile) % 4 * HEAD_DIM
+        columns = pl.ds(pl.multiple_of(first, 128), HEAD_DIM)
+        return remote(relay_o.at[tile], returned.at[:, columns], send_o.at[tile, 8], recv_o.at[tile, 7], on_two)
 
     def start_kv(j):
         kv_over_z(j, 0).start()
@@ -168,6 +183,7 @@
 
     for j in reversed(range(1, 8)):
         query_over_z(j).start()
+    start_kv(7)
     y_copy(7).start()
 
     def prepare():
@@ -304,8 +320,11 @@
                 query_over_z(j).wait_recv()
             for n in range(3):
                 query_over_x(n).start()
-            for j in (3, 4, 5, 6, 7):
+            for j in (3, 4, 5, 6):
                 start_kv(j)
+            for which in (0, 1):
+                kv_over_z(7, which).wait_recv()
+                relay_on(which).start()
             turn_query(0, query[:, :, of_head(x)])
             turn_query(4, query[:, :, shared])
             for n in range(3):
@@ -354,11 +373,17 @@
     before(CHUNKS - 1)
     attend(CHUNKS - 1, False, True)
 
+    for tile in range(RELAYED):
+        back(tile, 7).wait_recv()
+        back_on(tile).start()
+
     @pl.when(core != zh)
     def _():
         cache_across(0).wait_send()
         cache_across(1).wait_send()
 
+    relay_on(0).wait_send()
+    relay_on(1).wait_send()
     for j in range(1, 8):
         query_over_z(j).wait_send()
         kv_over_z(j, 0).wait_send()
@@ -375,7 +400,12 @@
     y_copy(7).wait_recv()
     for tile in range(GROUP):
         for j in range(8):
-            back(tile, j).wait_recv()
+            if j == 7 and tile < RELAYED:
+                back_on(tile).wait_recv()
+            else:
+                back(tile, j).wait_recv()
+    for tile in range(RELAYED):
+        back_on(tile).wait_send()
     for tile in range(GROUP):
         for j in range(8):
             back(tile, j).wait_send()
@@ -404,6 +434,8 @@
             pltpu.VMEM((3, 8, ROWS, HEAD_DIM), bf16),
             pltpu.VMEM((HEAD_DIM, GROUP * KEYS), bf16),
             pltpu.VMEM((X_CHUNKS, 2, ROWS, WIDTH), bf16),
+            pltpu.VMEM((2, ROWS, WIDTH), bf16),
+            pltpu.VMEM((RELAYED, ROWS, HEAD_DIM), bf16),
             pltpu.VMEM((CHUNKS, 2, 2, 8, ROWS, HEAD_DIM), bf16),
             pltpu.VMEM((GROUP, 8, ROWS, HEAD_DIM), bf16),
             pltpu.VMEM(time_weight.shape, bf16),
@@ -414,13 +446,14 @@
             pltpu.VMEM((1, GROUP * KEYS), f32),
             pltpu.VMEM((HEAD_DIM, GROUP * KEYS), f32),
             pltpu.SMEM((CHUNKS * 8,), f32),
-            dma((8, 3)),
+            dma((9, 3)),
             dma((X_CHUNKS, 7)),
             dma((8,)),
             dma((3,)),
-            dma((GROUP, 8)),
+            dma((GROUP, 9)),
             dma((8,)),
             dma((X_CHUNKS, 2)),
+            dma((2 + RELAYED,)),
             dma((X_CHUNKS, 7)),
             dma((8,)),
             dma((3,)),

time: 66 us -> 67.3 us (1.020)
  Pallas kernels: 64 us -> 65.3 us
    pallas_call x1, Pallas kernels: 64 us -> 65.3 us  [shards(): pl.pallas_call(kernel, out_shape=(jax.ShapeDtypeStruct(latent.shape, bf16...]
where the time goes in v20:
time: 67.3 us; the launch traced here: 67.2 us
  Pallas kernels  65.3 us (97%)
  other arithmetic  1.9 us (3%)
    pallas_call x1, Pallas kernels, shards(): pl.pallas_call(kernel, out_shape=(jax.ShapeDtypeStruct(latent.shape, bf16...  65.3 us
    convert_element_type x1, other arithmetic, shards(): return (shifted.astype(f32) + gate * returned.astype(f32)).astype(bf16)  1.9 us

profile of v20, /device:TPU:1, one launch (start us, length us, event | category | flops | bytes accessed | tf_op | source)
XLA Modules:
  0.0 67.2 jit_solution(2654602615931943471)
XLA Ops:
  0.0 65.3 %shard_map.100 = (bf16[32,5120]{1,0:T(8,128)(2,1)}, bf16[32,5120]{1,0:T(8,128)(2,1)}, f32[1,5120]{1,0:T(1,128)}) custom-call(s32[4]{0:T(128)} %levels_in.1, s32[50]{0:T(128)} %timesteps_in.1, s32[4,32]{1,0:T(4,128)} %mask_in.1, bf16[32,5120]{1,0:T(8,128)(2,1)} %latent.1, bf16[32,5120]{1,0:T(8,128)(2,1)} %query_in.1, bf16[32,5120]{1,0:T(8,128)(2,1)} %key_in.1, ...), custom_call_target="tpu_custom_call" | custom-call | flops 2000000000 | bytes 5000000 | tf_op jit(solution)/shard_map/pallas_call | solution.py:420
  65.3 1.9 %add_convert_fusion = bf16[32,5120]{1,0:T(8,128)(2,1)} fusion(bf16[32,5120]{1,0:T(8,128)(2,1)} %get-tuple-element.10, bf16[32,5120]{1,0:T(8,128)(2,1)} %get-tuple-element.8, f32[5120]{0:T(1024)} %bitcast.1), kind=kLoop, calls=%fused_computation | loop fusion | flops 819200 | bytes 1003520 | tf_op jit(solution)/shard_map/convert_element_type | solution.py:471

commit v21 on v19

--- a/solution.py
+++ b/solution.py
@@ -182,20 +182,6 @@
                     bias[PLACE[i] * 8 + slot] = jnp.where(cache_mask[y, block] == 1, 0.0, HIDDEN).astype(jnp.float32)
                 else:
                     bias[PLACE[i] * 8 + slot] = jnp.float32(0.0)
-
-        stamp = timesteps[levels[up]].astype(jnp.float32)
-        count = 128
-        index = lax.broadcasted_iota(jnp.int32, (8, count), 1).astype(jnp.float32)
-        phase = stamp * jnp.exp(-math.log(10000.0) * index / count)
-        embed = jnp.concatenate([jnp.cos(phase), jnp.sin(phase)], axis=1).astype(jnp.bfloat16)
-        weight_copy.wait()
-
-        def gate_columns(c, carry):
-            columns = pl.ds(pl.multiple_of(c * WIDTH, 128), WIDTH)
-            gate[:, columns] = jnp.dot(embed, weight[:, columns], preferred_element_type=jnp.float32)[0:1]
-            return carry
-
-        lax.fori_loop(0, 8, gate_columns, 0)
 
         peak[...] = jnp.full_like(peak, HIDDEN)
         total[...] = jnp.zeros_like(total)
@@ -353,6 +339,20 @@
     lax.fori_loop(0, CHUNKS - 1, turn, 0)
     before(CHUNKS - 1)
     attend(CHUNKS - 1, False, True)
+
+    stamp = timesteps[levels[up]].astype(jnp.float32)
+    count = 128
+    index = lax.broadcasted_iota(jnp.int32, (8, count), 1).astype(jnp.float32)
+    phase = stamp * jnp.exp(-math.log(10000.0) * index / count)
+    embed = jnp.concatenate([jnp.cos(phase), jnp.sin(phase)], axis=1).astype(jnp.bfloat16)
+    weight_copy.wait()
+
+    def gate_columns(c, carry):
+        columns = pl.ds(pl.multiple_of(c * WIDTH, 128), WIDTH)
+        gate[:, columns] = jnp.dot(embed, weight[:, columns], preferred_element_type=jnp.float32)[0:1]
+        return carry
+
+    lax.fori_loop(0, 8, gate_columns, 0)
 
     @pl.when(core != zh)
     def _():

time: 66 us -> 66 us (level)
  no operation moved by 1% of the time
where the time goes in v21:
time: 66 us; the launch traced here: 65.9 us
  Pallas kernels  64 us (97%)
  other arithmetic  1.9 us (3%)
    pallas_call x1, Pallas kernels, shards(): pl.pallas_call(kernel, out_shape=(jax.ShapeDtypeStruct(latent.shape, bf16...  64 us
    convert_element_type x1, other arithmetic, shards(): return (shifted.astype(f32) + gate * returned.astype(f32)).astype(bf16)  1.9 us

profile of v21, /device:TPU:1, one launch (start us, length us, event | category | flops | bytes accessed | tf_op | source)
XLA Modules:
  0.0 65.9 jit_solution(2228396450016878086)
XLA Ops:
  0.0 64.0 %shard_map.100 = (bf16[32,5120]{1,0:T(8,128)(2,1)}, bf16[32,5120]{1,0:T(8,128)(2,1)}, f32[1,5120]{1,0:T(1,128)}) custom-call(s32[4]{0:T(128)} %levels_in.1, s32[50]{0:T(128)} %timesteps_in.1, s32[4,32]{1,0:T(4,128)} %mask_in.1, bf16[32,5120]{1,0:T(8,128)(2,1)} %latent.1, bf16[32,5120]{1,0:T(8,128)(2,1)} %query_in.1, bf16[32,5120]{1,0:T(8,128)(2,1)} %key_in.1, ...), custom_call_target="tpu_custom_call" | custom-call | flops 2000000000 | bytes 5000000 | tf_op jit(solution)/shard_map/pallas_call | solution.py:390
  64.0 1.9 %add_convert_fusion = bf16[32,5120]{1,0:T(8,128)(2,1)} fusion(bf16[32,5120]{1,0:T(8,128)(2,1)} %get-tuple-element.10, bf16[32,5120]{1,0:T(8,128)(2,1)} %get-tuple-element.8, f32[5120]{0:T(1024)} %bitcast.1), kind=kLoop, calls=%fused_computation | loop fusion | flops 819200 | bytes 1003520 | tf_op jit(solution)/shard_map/convert_element_type | solution.py:438

commit v22 on v21

--- a/solution.py
+++ b/solution.py
@@ -41,7 +41,7 @@
 def kernel(
     levels_in, timesteps_in, mask_in, latent, query_in, key_in, value_in, cache_keys, cache_values, time_weight,
     returned, shifted, gate,
-    levels, timesteps, cache_mask, query, row_query, turned, landed, kv, attended, weight,
+    levels, timesteps, cache_mask, query, row_query, landed, kv, attended, weight,
     scored, weighed, factor, peak, total, summed, bias,
     send_z, send_x, send_y, send_q, send_o, recv_q, recv_kv, recv_x, recv_y, recv_rq, recv_o, local, own_x,
 ):
@@ -146,7 +146,7 @@
         return remote(src, dst, send_y.at[n], recv_y.at[n], to)
 
     def query_over_x(n):
-        to, slot = ((x_right, 0), (x_far, 1), (x_left, 2))[n]
+        to, slot = ((x_right, 1), (x_far, 2), (x_left, 3))[n]
         return remote(
             query.at[:, :, of_head(to)], row_query.at[slot], send_q.at[n], recv_rq.at[n], device(y, z, to, core)
         )
@@ -173,15 +173,16 @@
     def prepare():
         for copy in scalar_copies:
             copy.wait()
-        for i in range(CHUNKS):
+        slots = lax.broadcasted_iota(jnp.int32, (1, KEYS), 1) // ROWS
+        for i in (1, 9, 10, 11):
+            plane = {1: y, 9: down, 10: up, 11: (y + 2) % 4}[i]
+            shown = jnp.zeros((1, KEYS), jnp.float32)
             for slot in range(8):
-                if i == 1 or i >= 9:
-                    plane = {1: y, 9: down, 10: up, 11: (y + 2) % 4}[i]
-                    side = core if slot < 4 else 1 - core
-                    block = plane * 8 + side * 4 + (x + (0, 3, 2, 1)[slot % 4]) % 4
-                    bias[PLACE[i] * 8 + slot] = jnp.where(cache_mask[y, block] == 1, 0.0, HIDDEN).astype(jnp.float32)
-                else:
-                    bias[PLACE[i] * 8 + slot] = jnp.float32(0.0)
+                side = core if slot < 4 else 1 - core
+                block = plane * 8 + side * 4 + (x + (0, 3, 2, 1)[slot % 4]) % 4
+                hidden = jnp.where(cache_mask[y, block] == 1, 0.0, HIDDEN).astype(jnp.float32)
+                shown = jnp.where(slots == slot, hidden, shown)
+            bias[PLACE[i]] = shown
 
         peak[...] = jnp.full_like(peak, HIDDEN)
         total[...] = jnp.zeros_like(total)
@@ -198,41 +199,38 @@
 
         def score(h):
             if h < GROUP:
-                scored[:, tile_of(h)] = jnp.dot(
-                    keys[h // (GROUP - 1)], turned[:, tile_of(h)], preferred_element_type=jnp.float32
+                scored[tile_of(h)] = lax.dot_general(
+                    row_query[h].reshape(KEYS, HEAD_DIM),
+                    keys[h // (GROUP - 1)],
+                    (((1,), (1,)), ((), ())),
+                    preferred_element_type=jnp.float32,
                 )
 
         def softmax(h):
             for first in (h * KEYS, h * KEYS + 128):
-                side = slice(first, first + 128)
-                scores = scored[:, side]
+                rows = slice(first, first + 128)
+                sides = [scored[rows, 0:128], scored[rows, 128:256]]
                 if cached:
-                    scores = jnp.concatenate(
-                        [scores[slot * ROWS : (slot + 1) * ROWS] + bias[c * 8 + slot] for slot in range(8)], axis=0
-                    )
-                old = peak[:, side]
-                new = jnp.maximum(old, jnp.max(scores, axis=0, keepdims=True) * scale)
-                weights = jnp.exp2(scores * scale - new)
+                    sides = [sides[n] + bias[c, :, n * 128 : (n + 1) * 128] for n in (0, 1)]
+                old = peak[rows]
+                new = jnp.maximum(old, jnp.max(jnp.maximum(*sides), axis=1, keepdims=True) * scale)
+                weights = [jnp.exp2(side * scale - new) for side in sides]
                 shrink = jnp.exp2(old - new)
-                peak[:, side] = new
-                factor[:, side] = shrink
-                total[:, side] = shrink * total[:, side] + jnp.sum(weights, axis=0, keepdims=True)
-                weighed[:, side] = weights.astype(jnp.bfloat16)
+                peak[rows] = new
+                factor[rows] = shrink
+                total[rows] = shrink * total[rows] + (weights[0] + weights[1])
+                weighed[rows, 0:128] = weights[0].astype(jnp.bfloat16)
+                weighed[rows, 128:256] = weights[1].astype(jnp.bfloat16)
 
         def add_values(h):
             tile = tile_of(h)
-            added = lax.dot_general(
-                values[h // (GROUP - 1)],
-                weighed[:, tile],
-                (((0,), (0,)), ((), ())),
-                preferred_element_type=jnp.float32,
-            )
-            sums = factor[:, tile] * summed[:, tile] + added
+            added = jnp.dot(weighed[tile], values[h // (GROUP - 1)], preferred_element_type=jnp.float32)
+            sums = factor[tile] * summed[tile] + added
             if not last:
-                summed[:, tile] = sums
+                summed[tile] = sums
                 return
-            result = sums * (1.0 / total[:, tile])
-            attended[h] = result.T.astype(jnp.bfloat16).reshape(8, ROWS, HEAD_DIM)
+            result = sums * (1.0 / jnp.sum(total[tile], axis=1, keepdims=True))
+            attended[h] = result.astype(jnp.bfloat16).reshape(8, ROWS, HEAD_DIM)
             for j in reversed(range(8)):
                 back(h, j).start()
 
@@ -244,10 +242,6 @@
             if h:
                 add_values(h - 1)
         add_values(GROUP - 1)
-
-    def turn_query(h, rows):
-        tile = slice(h * KEYS, (h + 1) * KEYS)
-        turned[:, tile] = rows.reshape(KEYS, HEAD_DIM).astype(jnp.float32).T.astype(jnp.bfloat16)
 
     def arrived(*items):
         for i in items:
@@ -292,12 +286,10 @@
                 query_over_x(n).start()
             for j in (3, 4, 5, 6, 7):
                 start_kv(j)
-            turn_query(0, query[:, :, of_head(x)])
-            turn_query(4, query[:, :, shared])
+            row_query[0] = query[:, :, of_head(x)]
+            row_query[4] = query[:, :, shared]
             for n in range(3):
                 query_over_x(n).wait_recv()
-            for n in range(3):
-                turn_query(n + 1, row_query[n])
         if c == 1:
             for n in (0, 1):
                 y_copy(n).wait_recv()
@@ -401,19 +393,18 @@
             pltpu.SMEM(timesteps.shape, i32),
             pltpu.SMEM(cache_mask.shape, i32),
             pltpu.VMEM((8, ROWS, WIDTH), bf16),
-            pltpu.VMEM((3, 8, ROWS, HEAD_DIM), bf16),
-            pltpu.VMEM((HEAD_DIM, GROUP * KEYS), bf16),
+            pltpu.VMEM((GROUP, 8, ROWS, HEAD_DIM), bf16),
             pltpu.VMEM((X_CHUNKS, 2, ROWS, WIDTH), bf16),
             pltpu.VMEM((CHUNKS, 2, 2, 8, ROWS, HEAD_DIM), bf16),
             pltpu.VMEM((GROUP, 8, ROWS, HEAD_DIM), bf16),
             pltpu.VMEM(time_weight.shape, bf16),
-            pltpu.VMEM((KEYS, GROUP * KEYS), f32),
-            pltpu.VMEM((KEYS, GROUP * KEYS), bf16),
-            pltpu.VMEM((1, GROUP * KEYS), f32),
-            pltpu.VMEM((1, GROUP * KEYS), f32),
-            pltpu.VMEM((1, GROUP * KEYS), f32),
-            pltpu.VMEM((HEAD_DIM, GROUP * KEYS), f32),
-            pltpu.SMEM((CHUNKS * 8,), f32),
+            pltpu.VMEM((GROUP * KEYS, KEYS), f32),
+            pltpu.VMEM((GROUP * KEYS, KEYS), bf16),
+            pltpu.VMEM((GROUP * KEYS, HEAD_DIM), f32),
+            pltpu.VMEM((GROUP * KEYS, HEAD_DIM), f32),
+            pltpu.VMEM((GROUP * KEYS, HEAD_DIM), f32),
+            pltpu.VMEM((GROUP * KEYS, HEAD_DIM), f32),
+            pltpu.VMEM((CHUNKS, 1, KEYS), f32),
             dma((8, 3)),
             dma((X_CHUNKS, 7)),
             dma((8,)),

time: 66 us -> 66.1 us (level)
  no operation moved by 1% of the time
where the time goes in v22:
time: 66.1 us; the launch traced here: 65.9 us
  Pallas kernels  64 us (97%)
  other arithmetic  1.9 us (3%)
    pallas_call x1, Pallas kernels, shards(): pl.pallas_call(kernel, out_shape=(jax.ShapeDtypeStruct(latent.shape, bf16...  64 us
    convert_element_type x1, other arithmetic, shards(): return (shifted.astype(f32) + gate * returned.astype(f32)).astype(bf16)  1.9 us

profile of v22, /device:TPU:1, one launch (start us, length us, event | category | flops | bytes accessed | tf_op | source)
XLA Modules:
  0.0 65.9 jit_solution(4797527398233124862)
XLA Ops:
  0.0 64.0 %shard_map.100 = (bf16[32,5120]{1,0:T(8,128)(2,1)}, bf16[32,5120]{1,0:T(8,128)(2,1)}, f32[1,5120]{1,0:T(1,128)}) custom-call(s32[4]{0:T(128)} %levels_in.1, s32[50]{0:T(128)} %timesteps_in.1, s32[4,32]{1,0:T(4,128)} %mask_in.1, bf16[32,5120]{1,0:T(8,128)(2,1)} %latent.1, bf16[32,5120]{1,0:T(8,128)(2,1)} %query_in.1, bf16[32,5120]{1,0:T(8,128)(2,1)} %key_in.1, ...), custom_call_target="tpu_custom_call" | custom-call | flops 2000000000 | bytes 5000000 | tf_op jit(solution)/shard_map/pallas_call | solution.py:382
  64.0 1.9 %add_convert_fusion = bf16[32,5120]{1,0:T(8,128)(2,1)} fusion(bf16[32,5120]{1,0:T(8,128)(2,1)} %get-tuple-element.10, bf16[32,5120]{1,0:T(8,128)(2,1)} %get-tuple-element.8, f32[5120]{0:T(1024)} %bitcast.1), kind=kLoop, calls=%fused_computation | loop fusion | flops 819200 | bytes 1003520 | tf_op jit(solution)/shard_map/convert_element_type | solution.py:429

commit v23 on v22

--- a/solution.py
+++ b/solution.py
@@ -284,30 +284,33 @@
                 query_over_z(j).wait_recv()
             for n in range(3):
                 query_over_x(n).start()
-            for j in (3, 4, 5, 6, 7):
-                start_kv(j)
+            start_kv(3)
+            start_kv(4)
             row_query[0] = query[:, :, of_head(x)]
             row_query[4] = query[:, :, shared]
             for n in range(3):
                 query_over_x(n).wait_recv()
         if c == 1:
+            arrived(2)
+            start_kv(5)
+            start_kv(6)
+            arrived(3)
             for n in (0, 1):
                 y_copy(n).wait_recv()
                 y_copy(n + 2).start()
                 y_copy(n + 4).start()
-            arrived(2, 3)
         if c == 3:
+            gathered(2, 3)
             y_copy(2).wait_recv()
             y_copy(3).wait_recv()
             y_copy(6).start()
-        if c == 3:
-            gathered(2, 3)
-        if c == 5:
-            arrived(4, 5)
+        if c == 4:
+            arrived(4)
+            start_kv(7)
+            arrived(5)
         if c == 6:
-            gathered(4)
+            gathered(4, 5)
         if c == 7:
-            gathered(5)
             arrived(6)
         if c == 8:
             arrived(7)

time: 66.1 us -> 65.2 us (0.986)
  Pallas kernels: 64 us -> 63.2 us
    pallas_call x1, Pallas kernels: 64 us -> 63.2 us  [shards(): pl.pallas_call(kernel, out_shape=(jax.ShapeDtypeStruct(latent.shape, bf16...]
where the time goes in v23:
time: 65.2 us; the launch traced here: 65.1 us
  Pallas kernels  63.2 us (97%)
  other arithmetic  1.9 us (3%)
    pallas_call x1, Pallas kernels, shards(): pl.pallas_call(kernel, out_shape=(jax.ShapeDtypeStruct(latent.shape, bf16...  63.2 us
    convert_element_type x1, other arithmetic, shards(): return (shifted.astype(f32) + gate * returned.astype(f32)).astype(bf16)  1.9 us

profile of v23, /device:TPU:1, one launch (start us, length us, event | category | flops | bytes accessed | tf_op | source)
XLA Modules:
  0.0 65.1 jit_solution(218516214787023916)
XLA Ops:
  0.0 63.2 %shard_map.100 = (bf16[32,5120]{1,0:T(8,128)(2,1)}, bf16[32,5120]{1,0:T(8,128)(2,1)}, f32[1,5120]{1,0:T(1,128)}) custom-call(s32[4]{0:T(128)} %levels_in.1, s32[50]{0:T(128)} %timesteps_in.1, s32[4,32]{1,0:T(4,128)} %mask_in.1, bf16[32,5120]{1,0:T(8,128)(2,1)} %latent.1, bf16[32,5120]{1,0:T(8,128)(2,1)} %query_in.1, bf16[32,5120]{1,0:T(8,128)(2,1)} %key_in.1, ...), custom_call_target="tpu_custom_call" | custom-call | flops 2000000000 | bytes 5000000 | tf_op jit(solution)/shard_map/pallas_call | solution.py:385
  63.2 1.9 %add_convert_fusion = bf16[32,5120]{1,0:T(8,128)(2,1)} fusion(bf16[32,5120]{1,0:T(8,128)(2,1)} %get-tuple-element.10, bf16[32,5120]{1,0:T(8,128)(2,1)} %get-tuple-element.8, f32[5120]{0:T(1024)} %bitcast.1), kind=kLoop, calls=%fused_computation | loop fusion | flops 819200 | bytes 1003520 | tf_op jit(solution)/shard_map/convert_element_type | solution.py:432

commit v24 on v23

--- a/solution.py
+++ b/solution.py
@@ -168,6 +168,8 @@
 
     for j in reversed(range(1, 8)):
         query_over_z(j).start()
+    start_kv(1)
+    start_kv(2)
     y_copy(7).start()
 
     def prepare():
@@ -277,37 +279,33 @@
             y_copy(1).start()
             for j in (1, 2, 3, 4):
                 query_over_z(j).wait_recv()
-            start_kv(1)
-            start_kv(2)
+            start_kv(3)
+            start_kv(4)
             own_query.wait()
             for j in (5, 6, 7):
                 query_over_z(j).wait_recv()
             for n in range(3):
                 query_over_x(n).start()
-            start_kv(3)
-            start_kv(4)
+            start_kv(5)
+            start_kv(6)
+            arrived(2, 3)
             row_query[0] = query[:, :, of_head(x)]
             row_query[4] = query[:, :, shared]
             for n in range(3):
                 query_over_x(n).wait_recv()
         if c == 1:
-            arrived(2)
-            start_kv(5)
-            start_kv(6)
-            arrived(3)
             for n in (0, 1):
                 y_copy(n).wait_recv()
                 y_copy(n + 2).start()
                 y_copy(n + 4).start()
         if c == 3:
             gathered(2, 3)
+            arrived(4)
+            start_kv(7)
+            arrived(5)
             y_copy(2).wait_recv()
             y_copy(3).wait_recv()
             y_copy(6).start()
-        if c == 4:
-            arrived(4)
-            start_kv(7)
-            arrived(5)
         if c == 6:
             gathered(4, 5)
         if c == 7:

time: 65.2 us -> 64 us (0.982)
  Pallas kernels: 63.2 us -> 61.9 us
    pallas_call x1, Pallas kernels: 63.2 us -> 61.9 us  [shards(): pl.pallas_call(kernel, out_shape=(jax.ShapeDtypeStruct(latent.shape, bf16...]
where the time goes in v24:
time: 64 us; the launch traced here: 63.8 us
  Pallas kernels  61.9 us (97%)
  other arithmetic  1.9 us (3%)
    pallas_call x1, Pallas kernels, shards(): pl.pallas_call(kernel, out_shape=(jax.ShapeDtypeStruct(latent.shape, bf16...  61.9 us
    convert_element_type x1, other arithmetic, shards(): return (shifted.astype(f32) + gate * returned.astype(f32)).astype(bf16)  1.9 us

profile of v24, /device:TPU:1, one launch (start us, length us, event | category | flops | bytes accessed | tf_op | source)
XLA Modules:
  0.0 63.8 jit_solution(31432402480277337)
XLA Ops:
  0.0 61.9 %shard_map.100 = (bf16[32,5120]{1,0:T(8,128)(2,1)}, bf16[32,5120]{1,0:T(8,128)(2,1)}, f32[1,5120]{1,0:T(1,128)}) custom-call(s32[4]{0:T(128)} %levels_in.1, s32[50]{0:T(128)} %timesteps_in.1, s32[4,32]{1,0:T(4,128)} %mask_in.1, bf16[32,5120]{1,0:T(8,128)(2,1)} %latent.1, bf16[32,5120]{1,0:T(8,128)(2,1)} %query_in.1, bf16[32,5120]{1,0:T(8,128)(2,1)} %key_in.1, ...), custom_call_target="tpu_custom_call" | custom-call | flops 2000000000 | bytes 5000000 | tf_op jit(solution)/shard_map/pallas_call | solution.py:383
  61.9 1.9 %add_convert_fusion = bf16[32,5120]{1,0:T(8,128)(2,1)} fusion(bf16[32,5120]{1,0:T(8,128)(2,1)} %get-tuple-element.10, bf16[32,5120]{1,0:T(8,128)(2,1)} %get-tuple-element.8, f32[5120]{0:T(1024)} %bitcast.1), kind=kLoop, calls=%fused_computation | loop fusion | flops 819200 | bytes 1003520 | tf_op jit(solution)/shard_map/convert_element_type | solution.py:430

commit v25 on v24

--- a/solution.py
+++ b/solution.py
@@ -274,20 +274,21 @@
             arrived(0)
             prepare()
             arrived(1)
+            start_kv(3)
+            start_kv(4)
             gathered(0, 1)
             y_copy(0).start()
             y_copy(1).start()
             for j in (1, 2, 3, 4):
                 query_over_z(j).wait_recv()
-            start_kv(3)
-            start_kv(4)
+            start_kv(5)
+            start_kv(6)
             own_query.wait()
             for j in (5, 6, 7):
                 query_over_z(j).wait_recv()
             for n in range(3):
                 query_over_x(n).start()
-            start_kv(5)
-            start_kv(6)
+            start_kv(7)
             arrived(2, 3)
             row_query[0] = query[:, :, of_head(x)]
             row_query[4] = query[:, :, shared]
@@ -301,7 +302,6 @@
         if c == 3:
             gathered(2, 3)
             arrived(4)
-            start_kv(7)
             arrived(5)
             y_copy(2).wait_recv()
             y_copy(3).wait_recv()

time: 64 us -> 63.9 us (level)
  no operation moved by 1% of the time
where the time goes in v25:
time: 63.9 us; the launch traced here: 63.8 us
  Pallas kernels  61.9 us (97%)
  other arithmetic  1.9 us (3%)
    pallas_call x1, Pallas kernels, shards(): pl.pallas_call(kernel, out_shape=(jax.ShapeDtypeStruct(latent.shape, bf16...  61.9 us
    convert_element_type x1, other arithmetic, shards(): return (shifted.astype(f32) + gate * returned.astype(f32)).astype(bf16)  1.9 us

profile of v25, /device:TPU:1, one launch (start us, length us, event | category | flops | bytes accessed | tf_op | source)
XLA Modules:
  0.0 63.8 jit_solution(4202424639306678231)
XLA Ops:
  0.0 61.9 %shard_map.100 = (bf16[32,5120]{1,0:T(8,128)(2,1)}, bf16[32,5120]{1,0:T(8,128)(2,1)}, f32[1,5120]{1,0:T(1,128)}) custom-call(s32[4]{0:T(128)} %levels_in.1, s32[50]{0:T(128)} %timesteps_in.1, s32[4,32]{1,0:T(4,128)} %mask_in.1, bf16[32,5120]{1,0:T(8,128)(2,1)} %latent.1, bf16[32,5120]{1,0:T(8,128)(2,1)} %query_in.1, bf16[32,5120]{1,0:T(8,128)(2,1)} %key_in.1, ...), custom_call_target="tpu_custom_call" | custom-call | flops 2000000000 | bytes 5000000 | tf_op jit(solution)/shard_map/pallas_call | solution.py:383
  61.9 1.9 %add_convert_fusion = bf16[32,5120]{1,0:T(8,128)(2,1)} fusion(bf16[32,5120]{1,0:T(8,128)(2,1)} %get-tuple-element.10, bf16[32,5120]{1,0:T(8,128)(2,1)} %get-tuple-element.8, f32[5120]{0:T(1024)} %bitcast.1), kind=kLoop, calls=%fused_computation | loop fusion | flops 819200 | bytes 1003520 | tf_op jit(solution)/shard_map/convert_element_type | solution.py:430
